TPU v7x, 32 devices: a whole 2x2x4 slice. The times are simulated.
32 devices in a mesh: groups: 2 (over y), seq: 16 (over z, x, core).
Axes of the slice: x: 2, y: 2, z: 4, core: 2. Of those that a mesh axis runs over, the one named last changes fastest.
Arguments:
- queries: bfloat16 [4096, 4096], P(('groups', 'seq')), parts along dimension 0, may hold values from -6 to 6
- suffix_kv: bfloat16 [4096, 1024], P(('groups', 'seq')), parts along dimension 0, may hold values from -6 to 6
- kv_store: bfloat16 [1024, 8, 1024], P(('groups', 'seq')), parts along dimension 0, may hold values from -6 to 6
- page_table: int32 [4, 16], P('groups'), parts along dimension 0, may hold values from 0 to 511, as said below
- hit_tokens: int32 [4], P('groups'), parts along dimension 0, may hold values from 0 to 128, as said below
- owner_offset: int32 [4, 4], P('groups'), parts along dimension 0, may hold values from 0 to 15
Outputs:
- attention_out: bfloat16 [4096, 4096], P(('groups', 'seq')), parts along dimension 0
- decode_cache: bfloat16 [32, 4, 128, 256], P(('groups', 'seq')), parts along dimension 0
There are 2 independent parts, one for each index of `groups`. A program takes and returns all parts, laid end to end along the dimension named above; each array names one. Nothing has to cross between parts.
Inputs may be any that keep to these rules, and one draw needn't show every extreme that they name: Slot page_table[r, j] is slot page_table[r, j] mod 32 of store device page_table[r, j] // 32; all entries of one group differ, and every store device holds exactly 1 pages of each request. `hit_tokens`: some request finds all 128 prefix tokens.
All inputs are finite; a program needn't handle non-finite values.
Results may differ from a plain program's by a relative error of at most 0.007.
Values may be sent and summed in bfloat16 or wider, within the bound.
No kernel may reach another device: no remote copies, remote signals or barrier semaphores. Data moves between devices by JAX's collectives and lax.ppermute only.
A program may use at most 128 MiB of HBM per device.

v0:
```python
import math

import jax
import jax.numpy as jnp
from jax import lax
from jax.sharding import PartitionSpec as P

HD = 128
QH = 32
KVH = 4
REQS = 2
PAGE = 8
CAP = 1
SLOTS = 32


NEG_FILL = -1e30


def passed_along(block, axis, distance):
    devices = range(lax.axis_size(axis))
    route = [(i - distance, i) for i in devices if i - distance in devices]
    return lax.ppermute(block, axis, route)


def fresh_state(kv_heads, tok_rows, per_group, head_size):
    return (
        jnp.full((kv_heads, tok_rows, per_group), NEG_FILL, jnp.float32),
        jnp.zeros((kv_heads, tok_rows, per_group), jnp.float32),
        jnp.zeros((kv_heads, tok_rows, per_group, head_size), jnp.float32),
    )


def absorb(running, query_heads, key_block, usable):
    head_size = query_heads.shape[-1]
    scores = jnp.einsum(
        "tgqd,kgd->gtqk",
        query_heads,
        key_block[:, :, :head_size],
        preferred_element_type=jnp.float32,
    ) * head_size ** (-0.5)
    scores = jnp.where(usable[None, :, None, :], scores, -jnp.inf)
    top_old, denom_old, weighted_old = running
    top_new = jnp.maximum(top_old, jnp.max(scores, axis=-1))
    probabilities = jnp.exp(scores - top_new[..., None])
    factor = jnp.exp(top_old - top_new)
    denom_new = denom_old * factor + jnp.sum(probabilities, axis=-1)
    weighted_new = weighted_old * factor[..., None] + jnp.einsum(
        "gtqk,kgd->gtqd",
        probabilities.astype(jnp.bfloat16),
        key_block[:, :, head_size:],
        preferred_element_type=jnp.float32,
    )
    return (top_new, denom_new, weighted_new)


def absorb_blocks(running, query_heads, key_blocks, block_ok):
    tok_rows = query_heads.shape[0]
    block_len = key_blocks.shape[1]

    def visit(carried, pieces):
        key_block, block_mask = pieces
        full_mask = jnp.broadcast_to(block_mask[None, :], (tok_rows, block_len))

        def take_block(current):
            return absorb(current, query_heads, key_block, full_mask)

        def keep_block(current):
            return current

        return (lax.cond(jnp.any(block_mask), take_block, keep_block, carried), None)

    return lax.scan(visit, running, (key_blocks, block_ok))[0]


def shards(queries, suffix_kv, kv_store, page_table, hit_tokens, owner_offset):
    devices = lax.axis_size("seq")
    my_index = lax.axis_index("seq")
    tok_rows = queries.shape[0]
    group_size = devices // REQS
    request = my_index // group_size
    rank_in_group = my_index % group_size
    per_group = QH // KVH
    query_heads = queries.reshape(tok_rows, KVH, per_group, HD)
    running = fresh_state(KVH, tok_rows, per_group, HD)
    store_of = page_table // SLOTS
    page_count = page_table.shape[1]
    page_ids = jnp.arange(page_count, dtype=jnp.int32)
    cap_ids = jnp.arange(CAP, dtype=jnp.int32)
    on_this_store = store_of == my_index
    page_rank = jnp.cumsum(on_this_store.astype(jnp.int32), axis=1) - 1
    selected = on_this_store[:, None, :] & (page_rank[:, None, :] == cap_ids[None, :, None])
    local_slot = jnp.sum(jnp.where(selected, (page_table % SLOTS)[:, None, :], 0), axis=2)
    outgoing = kv_store[local_slot]
    outgoing = jnp.broadcast_to(outgoing[:, None], (REQS, group_size) + outgoing.shape[1:])
    outgoing = outgoing.reshape((devices,) + outgoing.shape[2:])
    incoming = lax.all_to_all(outgoing, "seq", split_axis=0, concat_axis=0, tiled=True)
    store_ids = jnp.arange(devices, dtype=jnp.int32)
    table_row = store_of[request]
    holds = table_row[None, :] == store_ids[:, None]
    held_rank = jnp.cumsum(holds.astype(jnp.int32), axis=1) - 1
    chosen = holds[:, None, :] & (held_rank[:, None, :] == cap_ids[None, :, None])
    page_index = jnp.sum(jnp.where(chosen, page_ids[None, None, :], 0), axis=2)
    positions = page_index[:, :, None] * PAGE + jnp.arange(PAGE, dtype=jnp.int32)[None, None, :]
    prefix_usable = (positions < hit_tokens[request]).reshape(-1)
    prefix_keys = incoming.reshape(-1, KVH, 2 * HD)
    key_count = prefix_keys.shape[0]
    block_len = math.gcd(256, key_count)
    block_count = key_count // block_len
    running = absorb_blocks(
        running,
        query_heads,
        prefix_keys.reshape(block_count, block_len, KVH, 2 * HD),
        prefix_usable.reshape(block_count, block_len),
    )
    row_ids = jnp.arange(tok_rows, dtype=jnp.int32)
    causal = row_ids[:, None] >= row_ids[None, :]
    running = absorb(running, query_heads, suffix_kv.reshape(tok_rows, KVH, 2 * HD), causal)
    held_blocks = suffix_kv
    stride_len = 1
    while stride_len < group_size:
        arrived = passed_along(held_blocks, "seq", stride_len)
        arrived_count = arrived.shape[0] // tok_rows
        sources = my_index - 2 * stride_len + 1 + jnp.arange(arrived_count, dtype=jnp.int32)
        source_ok = sources >= my_index - rank_in_group
        block_ok = jnp.broadcast_to(source_ok[:, None], (arrived_count, tok_rows))
        running = absorb_blocks(
            running, query_heads, arrived.reshape(arrived_count, tok_rows, KVH, 2 * HD), block_ok
        )
        held_blocks = jnp.concatenate([arrived, held_blocks], axis=0)
        stride_len = stride_len * 2
    top_score, denominator, weighted = running
    attended = (weighted / denominator[..., None]).astype(jnp.bfloat16)
    attention_out = attended.transpose(1, 0, 2, 3).reshape(tok_rows, QH * HD)
    tokens_per_owner = tok_rows // devices
    offsets = owner_offset[request]
    arranged = suffix_kv.reshape(tokens_per_owner, devices, KVH, 2 * HD).transpose(2, 1, 0, 3)
    columns = (store_ids[None, :] - offsets[:, None]) % devices
    outgoing_new = jnp.take_along_axis(arranged, columns[:, :, None, None], axis=1)
    landed = lax.all_to_all(outgoing_new, "seq", split_axis=1, concat_axis=2, tiled=True)
    decode_cache = landed.reshape(1, KVH, tok_rows, 2 * HD)
    return (attention_out, decode_cache)


def solution(mesh):
    in_specs = (
        P(("groups", "seq"), None),
        P(("groups", "seq"), None),
        P(("groups", "seq"), None, None),
        P("groups", None),
        P("groups"),
        P("groups", None),
    )
    out_specs = (P(("groups", "seq"), None), P(("groups", "seq"), None, None, None))
    return jax.shard_map(shards, mesh=mesh, in_specs=in_specs, out_specs=out_specs, check_vma=False)
```

profile of v0, /device:TPU:11, one launch (start us, length us, event | category | flops | bytes accessed | tf_op | source)
XLA Modules:
  0.0 105.2 jit_solution(17695121810123089689)
XLA Ops:
  3.8 6.6 %all-to-all-start = ((bf16[16,1,8,1024]{3,2,1,0:T(8,128)(2,1)}), bf16[16,1,8,1024]{3,2,1,0:T(8,128)(2,1)S(1)}, u32[]{:S(2)}, u32[]{:S(2)}) async-start(bf16[16,1,8,1024]{3,2,1,0:T(8,128)(2,1)} %bitcast.28), calls=%async_computation | async-start | bytes 524288 | tf_op jit(solution)/shard_map/all_to_all | solution.py:97
  10.3 1.1 %copy.108 = bf16[128,1024]{0,1:T(8,128)(2,1)S(1)} copy(bf16[128,1024]{1,0:T(8,128)(2,1)} %param.19) | data formatting | bytes 524288 | tf_op args[1]
  11.4 3.3 %collective-permute-start = (bf16[128,1024]{0,1:T(8,128)(2,1)S(1)}, bf16[128,1024]{0,1:T(8,128)(2,1)S(1)}, u32[]{:S(2)}, u32[]{:S(2)}) collective-permute-start(bf16[128,1024]{0,1:T(8,128)(2,1)S(1)} %copy.108), channel_id=1, source_target_pairs={{0,1},{1,2},{2,3},{3,4},{4,5},{5,6},{6,7},{7,8},{8,9},{9,10},{10,1... | collective-permute-start | bytes 786440 | tf_op jit(solution)/shard_map/ppermute | solution.py:23
  15.2 1.3 %dynamic_slice.45 = s32[1]{0:T(128)} dynamic-slice(s32[2]{0:T(128)} %param.22, s32[]{:T(128)S(6)} %select_n.130), dynamic_slice_sizes={1} | dynamic-slice | bytes 12 | tf_op jit(solution)/shard_map/dynamic_slice | solution.py:105
  17.3 1.4 %fusion.60 = pred[]{:T(512)} fusion(s32[]{:T(128)} %bitcast.25, s32[16]{0:T(128)S(1)} %broadcast_multiply_fusion), kind=kLoop, calls=%fused_computation.115 | loop fusion | flops 383 | bytes 69 | tf_op jit(solution)/shard_map/while/body/eval_jaxpr/reduce_or | solution.py:71
  18.7 1.8 %reshape.368 = bf16[8,16,4,256]{3,2,1,0:T(4,128)(2,1)} reshape(bf16[128,1024]{1,0:T(8,128)(2,1)} %param.19) | data formatting | bytes 524288 | tf_op jit(solution)/shard_map/reshape | solution.py:137
  21.9 1.3 %copy.118 = bf16[128,4,8,128]{3,0,2,1:T(8,128)(2,1)} copy(bf16[128,4,8,128]{0,3,2,1:T(8,128)(2,1)S(1)} %bitcast.137) | data formatting | bytes 2097152 | tf_op jit(solution)/shard_map/while | solution.py:73
  24.2 1.5 %broadcast_in_dim.149 = f32[4,128,8,128]{3,1,2,0:T(8,128)} broadcast(f32[]{:T(128)} %constant.190.clone.1), dimensions={} | broadcast | bytes 2097156 | tf_op jit(solution)/shard_map/broadcast_in_dim | solution.py:30
  26.6 3.1 %collective-permute-start.1 = (bf16[256,1024]{0,1:T(8,128)(2,1)}, bf16[256,1024]{0,1:T(8,128)(2,1)}, u32[]{:S(2)}, u32[]{:S(2)}) collective-permute-start(bf16[256,1024]{0,1:T(8,128)(2,1)} %pad_maximum_fusion.1), channel_id=1, source_target_pairs={{0,2},{1,3},{2,4},{3,5},{4,6},{5,7},{6,8},{7,9},{8,10},{9,11},{10,... | collective-permute-start | bytes 1572872 | tf_op jit(solution)/shard_map/ppermute | solution.py:23
  30.6 1.8 %fusion.44 = (f32[4,128,8]{1,2,0:T(8,128)S(1)}, f32[4,128,8,128]{1,3,2,0:T(8,128)}) fusion(pred[128,128]{0,1:T(8,128)(4,1)S(1)} %iota_compare_fusion, bf16[128,4,8,128]{0,3,2,1:T(8,128)(2,1)S(1)} %bitcast.138, bf16[128,4,256]{0,2,1:T(8,128)(2,1)S(1)} %bitcast.142), kind=kOutput, calls=%fused_computation.81 | convolution fusion | flops 135786496 | bytes 3309568 | tf_op jit(solution)/shard_map/tgqd,kgd->gtqk/dot_general | solution.py:36
  32.4 4.9 %all-to-all-start.1 = ((bf16[4,16,8,256]{3,2,0,1:T(8,128)(2,1)}), bf16[4,16,8,256]{3,2,0,1:T(8,128)(2,1)}, u32[]{:S(2)}, u32[]{:S(2)}) async-start(bf16[4,16,8,256]{3,2,0,1:T(8,128)(2,1)} %copy_select_fusion), calls=%async_computation.1 | async-start | bytes 524288 | tf_op jit(solution)/shard_map/all_to_all | solution.py:140
  37.4 5.6 %conditional.4 = ((f32[4,128,8]{1,2,0:T(8,128)S(1)}, f32[4,128,8]{1,2,0:T(8,128)S(1)}, f32[4,128,8,128]{3,1,2,0:T(8,128)})) conditional(s32[]{:T(128)} %convert_element_type.47, (f32[4,128,8]{1,2,0:T(8,128)S(1)}, f32[4,128,8]{1,2,0:T(8,128)S(1)}, f32[4,128,8,128]{3,1,2,0:T(8,128)}) %tuple.52, (s32[16,1,1,8]{3,0,2,1:T(8,128)S(1)}, ...), branch_computations={%region_5.6_spmd, %region_6.9_spmd} | conditional | flops 275259648 | bytes 13109028 | solution.py:71
  39.5 3.5 %multiply_add_fusion = f32[4,128,8,128]{3,1,2,0:T(8,128)} fusion(f32[4,128,8,128]{3,1,2,0:T(8,128)} %get-tuple-element.227, f32[4,128,8,128]{1,3,2,0:T(8,128)S(1)} %get-tuple-element.453, f32[4,128,8]{1,2,0:T(8,128)S(1)} %get-tuple-element.435, f32[4,128,8]{1,2,0:T(8,128)S(1)} %max.12, pred[128]{0:T(512)(128)(4,1)S(1)} %lt.83, ...), kind=kOutput, calls=%fused_computation.2 | convolution fusion | flops 137363456 | bytes 6455424 | tf_op jit(solution)/shard_map/while/body/eval_jaxpr/cond/branch_1_fun/gtqk,kgd->gtqd/dot_general | solution.py:48
  43.0 1.2 %collective-permute-done.1 = bf16[256,1024]{0,1:T(8,128)(2,1)} collective-permute-done((bf16[256,1024]{0,1:T(8,128)(2,1)}, bf16[256,1024]{0,1:T(8,128)(2,1)}, u32[]{:S(2)}, u32[]{:S(2)}) %collective-permute-start.1) | collective-permute-done | bytes 524320 | tf_op jit(solution)/shard_map/ppermute | solution.py:23
  44.2 2.2 %pad_maximum_fusion = bf16[512,1024]{0,1:T(8,128)(2,1)} fusion(bf16[128,1024]{0,1:T(8,128)(2,1)S(1)} %copy.108, bf16[128,1024]{0,1:T(8,128)(2,1)S(1)} %collective-permute-done, bf16[256,1024]{0,1:T(8,128)(2,1)} %collective-permute-done.1), kind=kLoop, calls=%fused_computation.85 | loop fusion | flops 3145728 | bytes 2097152 | tf_op jit(solution)/shard_map/concatenate | solution.py:130
  46.4 3.6 %collective-permute-start.2 = (bf16[512,1024]{0,1:T(8,128)(2,1)}, bf16[512,1024]{0,1:T(8,128)(2,1)}, u32[]{:S(2)}, u32[]{:S(2)}) collective-permute-start(bf16[512,1024]{0,1:T(8,128)(2,1)} %pad_maximum_fusion), channel_id=1, source_target_pairs={{0,4},{1,5},{2,6},{3,7},{4,8},{5,9},{6,10},{7,11},{8,12},{9,13},{1... | collective-permute-start | bytes 3145736 | tf_op jit(solution)/shard_map/ppermute | solution.py:23
  50.5 2.4 %multiply_add_fusion.8 = f32[4,128,8,128]{3,1,2,0:T(8,128)S(1)} fusion(f32[4,128,8,128]{3,1,2,0:T(8,128)} %get-tuple-element.285, f32[4,128,8,128]{1,3,2,0:T(8,128)S(1)} %copy-done.3, f32[4,128,8]{1,2,0:T(8,128)S(1)} %get-tuple-element.447, f32[4,128,8]{1,2,0:T(8,128)S(1)} %max.17, pred[128,128]{0,1:T(8,128)(4,1)S(1)} %iota_compare_fusion, ...), kind=kOutput, calls=%fused_computation.78 | convolution fusion | flops 137363456 | bytes 6471680 | tf_op jit(solution)/shard_map/gtqk,kgd->gtqd/dot_general | solution.py:48
  52.9 3.9 %conditional.5 = ((f32[4,128,8]{1,2,0:T(8,128)S(1)}, f32[4,128,8]{1,2,0:T(8,128)S(1)}, f32[4,128,8,128]{3,1,2,0:T(8,128)S(1)})) conditional(s32[]{:T(128)} %convert_element_type.45, (f32[4,128,8]{1,2,0:T(8,128)S(1)}, f32[4,128,8]{1,2,0:T(8,128)S(1)}, f32[4,128,8,128]{3,1,2,0:T(8,128)S(1)}) %tuple.54, (pred[]{:T(512)}, ...), branch_computations={%region_11.12_spmd, %region_12.15_spmd} | conditional | flops 275259392 | bytes 12058659 | solution.py:71
  53.0 1.7 %fusion.11 = (f32[4,128,8]{1,2,0:T(8,128)S(1)}, f32[4,128,8,128]{1,3,2,0:T(8,128)S(1)}) fusion(pred[]{:T(512)} %get-tuple-element.229, bf16[128,4,8,128]{0,3,2,1:T(8,128)(2,1)} %get-tuple-element.388, bf16[128,4,256]{0,2,1:T(8,128)(2,1)S(1)} %bitcast.144), kind=kOutput, calls=%fused_computation.23 | convolution fusion | flops 135786496 | bytes 3293185 | tf_op jit(solution)/shard_map/while/body/eval_jaxpr/cond/branch_1_fun/tgqd,kgd->gtqk/dot_general | solution.py:36
  55.2 1.5 %multiply_add_fusion.2 = f32[4,128,8,128]{3,1,2,0:T(8,128)S(1)} fusion(f32[4,128,8,128]{3,1,2,0:T(8,128)S(1)} %get-tuple-element.233, f32[4,128,8,128]{1,3,2,0:T(8,128)S(1)} %get-tuple-element.455, f32[4,128,8]{1,2,0:T(8,128)S(1)} %get-tuple-element.437, f32[4,128,8]{1,2,0:T(8,128)S(1)} %max.13, pred[]{:T(512)} %get-tuple-element.229, ...), kind=kOutput, calls=%fused_computation.20 | convolution fusion | flops 137363456 | bytes 6455297 | tf_op jit(solution)/shard_map/while/body/eval_jaxpr/cond/branch_1_fun/gtqk,kgd->gtqd/dot_general | solution.py:48
  56.9 1.7 %copy.167 = bf16[4,16,8,256]{3,2,1,0:T(8,128)(2,1)} copy(bf16[4,16,8,256]{3,2,0,1:T(8,128)(2,1)} %all-to-all-done.1) | data formatting | bytes 524288 | tf_op jit(solution)/shard_map/all_to_all | solution.py:140
  58.5 2.0 %reshape.395 = bf16[2,128,4,256]{1,0,3,2:T(2,128)(2,1)} reshape(bf16[256,1024]{0,1:T(8,128)(2,1)} %collective-permute-done.1) | data formatting | bytes 1048576 | tf_op jit(solution)/shard_map/reshape | solution.py:128
  60.5 1.3 %copy.117 = bf16[2,128,4,256]{3,1,2,0:T(8,128)(2,1)S(1)} copy(bf16[2,128,4,256]{1,0,3,2:T(2,128)(2,1)} %reshape.395) | data formatting | bytes 1048576 | tf_op jit(solution)/shard_map/while | solution.py:73
  61.9 10.2 %while.4 = (s32[]{:T(128)}, f32[4,128,8]{1,2,0:T(8,128)S(1)}, f32[4,128,8]{1,2,0:T(8,128)S(1)}, f32[4,128,8,128]{3,1,2,0:T(8,128)S(1)}, pred[2,128]{1,0:T(4,128)...) while((s32[]{:T(128)}, f32[4,128,8]{1,2,0:T(8,128)S(1)}, ...), condition=%wide.region_21.22_spmd, body=%wide.region_15.21_spmd.sunk | while | flops 275259520 | bytes 12584531 | solution.py:73
  63.2 3.8 %conditional.8 = ((f32[4,128,8]{1,2,0:T(8,128)S(1)}, f32[4,128,8]{1,2,0:T(8,128)S(1)}, f32[4,128,8,128]{3,1,2,0:T(8,128)S(1)})) conditional(s32[]{:T(128)} %convert_element_type.68, (f32[4,128,8]{1,2,0:T(8,128)S(1)}, f32[4,128,8]{1,2,0:T(8,128)S(1)}, f32[4,128,8,128]{3,1,2,0:T(8,128)S(1)}) %tuple.111, (pred[1,128]{1,0:T(4,128)(4,1)S(1)}, ...), branch_computations={%region_17.17_spmd, %region_18.20_spmd} | conditional | flops 275259392 | bytes 12584100 | solution.py:71
  63.2 1.7 %bitcast_reduce_fusion = (f32[4,128,8]{1,2,0:T(8,128)S(1)}, f32[4,128,128,8]{2,1,3,0:T(8,128)S(1)}) fusion(pred[128]{0:T(512)(128)(4,1)S(1)} %bitcast.151, bf16[128,4,8,128]{3,0,2,1:T(8,128)(2,1)} %get-tuple-element.238, bf16[128,4,256]{2,0,1:T(8,128)(2,1)S(1)} %dynamic-slice_bitcast_fusion), kind=kOutput, calls=%fused_computation.38 | convolution fusion | flops 135786496 | bytes 3293696 | tf_op jit(solution)/shard_map/while/body/eval_jaxpr/cond/branch_1_fun/tgqd,kgd->gtqk/dot_general | solution.py:36
  65.5 1.4 %multiply_add_fusion.4 = f32[4,128,8,128]{3,1,2,0:T(8,128)S(1)} fusion(f32[4,128,8,128]{3,1,2,0:T(8,128)S(1)} %get-tuple-element.240, f32[4,128,128,8]{2,1,3,0:T(8,128)S(1)} %get-tuple-element.457, f32[4,128,8]{1,2,0:T(8,128)S(1)} %get-tuple-element.439, f32[4,128,8]{1,2,0:T(8,128)S(1)} %max.14, pred[128]{0:T(512)(128)(4,1)S(1)} %bitcast.153, ...), kind=kOutput, calls=%fused_computation.40 | convolution fusion | flops 137363456 | bytes 6455808 | tf_op jit(solution)/shard_map/while/body/eval_jaxpr/cond/branch_1_fun/gtqk,kgd->gtqd/dot_general | solution.py:48
  68.3 3.8 %conditional.8 = ((f32[4,128,8]{1,2,0:T(8,128)S(1)}, f32[4,128,8]{1,2,0:T(8,128)S(1)}, f32[4,128,8,128]{3,1,2,0:T(8,128)S(1)})) conditional(s32[]{:T(128)} %convert_element_type.68, (f32[4,128,8]{1,2,0:T(8,128)S(1)}, f32[4,128,8]{1,2,0:T(8,128)S(1)}, f32[4,128,8,128]{3,1,2,0:T(8,128)S(1)}) %tuple.111, (pred[1,128]{1,0:T(4,128)(4,1)S(1)}, ...), branch_computations={%region_17.17_spmd, %region_18.20_spmd} | conditional | flops 275259392 | bytes 12584100 | solution.py:71
  68.3 1.7 %bitcast_reduce_fusion = (f32[4,128,8]{1,2,0:T(8,128)S(1)}, f32[4,128,128,8]{2,1,3,0:T(8,128)S(1)}) fusion(pred[128]{0:T(512)(128)(4,1)S(1)} %bitcast.151, bf16[128,4,8,128]{3,0,2,1:T(8,128)(2,1)} %get-tuple-element.238, bf16[128,4,256]{2,0,1:T(8,128)(2,1)S(1)} %dynamic-slice_bitcast_fusion), kind=kOutput, calls=%fused_computation.38 | convolution fusion | flops 135786496 | bytes 3293696 | tf_op jit(solution)/shard_map/while/body/eval_jaxpr/cond/branch_1_fun/tgqd,kgd->gtqk/dot_general | solution.py:36
  70.6 1.4 %multiply_add_fusion.4 = f32[4,128,8,128]{3,1,2,0:T(8,128)S(1)} fusion(f32[4,128,8,128]{3,1,2,0:T(8,128)S(1)} %get-tuple-element.240, f32[4,128,128,8]{2,1,3,0:T(8,128)S(1)} %get-tuple-element.457, f32[4,128,8]{1,2,0:T(8,128)S(1)} %get-tuple-element.439, f32[4,128,8]{1,2,0:T(8,128)S(1)} %max.14, pred[128]{0:T(512)(128)(4,1)S(1)} %bitcast.153, ...), kind=kOutput, calls=%fused_computation.40 | convolution fusion | flops 137363456 | bytes 6455808 | tf_op jit(solution)/shard_map/while/body/eval_jaxpr/cond/branch_1_fun/gtqk,kgd->gtqd/dot_general | solution.py:48
  72.0 1.6 %collective-permute-done.2 = bf16[512,1024]{0,1:T(8,128)(2,1)} collective-permute-done((bf16[512,1024]{0,1:T(8,128)(2,1)}, bf16[512,1024]{0,1:T(8,128)(2,1)}, u32[]{:S(2)}, u32[]{:S(2)}) %collective-permute-start.2) | collective-permute-done | bytes 1048608 | tf_op jit(solution)/shard_map/ppermute | solution.py:23
  73.7 2.1 %reshape.396 = bf16[4,128,4,256]{1,0,3,2:T(4,128)(2,1)} reshape(bf16[512,1024]{0,1:T(8,128)(2,1)} %collective-permute-done.2) | data formatting | bytes 2097152 | tf_op jit(solution)/shard_map/reshape | solution.py:128
  75.8 2.4 %copy.121 = bf16[4,128,4,256]{3,1,2,0:T(8,128)(2,1)} copy(bf16[4,128,4,256]{1,0,3,2:T(4,128)(2,1)} %reshape.396) | data formatting | bytes 2097152 | tf_op jit(solution)/shard_map/while | solution.py:73
  78.3 24.1 %while.5 = (s32[]{:T(128)}, f32[4,128,8]{1,2,0:T(8,128)S(1)}, f32[4,128,8]{1,2,0:T(8,128)S(1)}, f32[4,128,8,128]{3,1,2,0:T(8,128)S(1)}, pred[4,128]{1,0:T(4,128)...) while((s32[]{:T(128)}, f32[4,128,8]{1,2,0:T(8,128)S(1)}, ...), condition=%wide.region_28.29_spmd, body=%wide.region_22.28_spmd.sunk | while | flops 275259520 | bytes 12584531 | solution.py:73
  79.6 4.7 %conditional.9 = ((f32[4,128,8]{1,2,0:T(8,128)S(1)}, f32[4,128,8]{1,2,0:T(8,128)S(1)}, f32[4,128,8,128]{3,1,2,0:T(8,128)S(1)})) conditional(s32[]{:T(128)} %convert_element_type.69, (f32[4,128,8]{1,2,0:T(8,128)S(1)}, f32[4,128,8]{1,2,0:T(8,128)S(1)}, f32[4,128,8,128]{3,1,2,0:T(8,128)S(1)}) %tuple.115, (pred[1,128]{1,0:T(4,128)(4,1)S(1)}, ...), branch_computations={%region_24.24_spmd, %region_25.27_spmd} | conditional | flops 275259392 | bytes 12584100 | solution.py:71
  79.6 1.0 dynamic-slice_bitcast_fusion.1
  80.6 1.7 %bitcast_reduce_fusion.1 = (f32[4,128,8]{1,2,0:T(8,128)S(1)}, f32[4,128,128,8]{2,1,3,0:T(8,128)S(1)}) fusion(pred[128]{0:T(512)(128)(4,1)S(1)} %bitcast.154, bf16[128,4,8,128]{3,0,2,1:T(8,128)(2,1)} %get-tuple-element.256, bf16[128,4,256]{2,0,1:T(8,128)(2,1)S(1)} %dynamic-slice_bitcast_fusion.1), kind=kOutput, calls=%fused_computation.58 | convolution fusion | flops 135786496 | bytes 3293696 | tf_op jit(solution)/shard_map/while/body/eval_jaxpr/cond/branch_1_fun/tgqd,kgd->gtqk/dot_general | solution.py:36
  82.8 1.4 %multiply_add_fusion.6 = f32[4,128,8,128]{3,1,2,0:T(8,128)S(1)} fusion(f32[4,128,8,128]{3,1,2,0:T(8,128)S(1)} %get-tuple-element.258, f32[4,128,128,8]{2,1,3,0:T(8,128)S(1)} %get-tuple-element.459, f32[4,128,8]{1,2,0:T(8,128)S(1)} %get-tuple-element.443, f32[4,128,8]{1,2,0:T(8,128)S(1)} %max.15, pred[128]{0:T(512)(128)(4,1)S(1)} %bitcast.156, ...), kind=kOutput, calls=%fused_computation.60 | convolution fusion | flops 137363456 | bytes 6455808 | tf_op jit(solution)/shard_map/while/body/eval_jaxpr/cond/branch_1_fun/gtqk,kgd->gtqd/dot_general | solution.py:48
  85.6 4.7 %conditional.9 = ((f32[4,128,8]{1,2,0:T(8,128)S(1)}, f32[4,128,8]{1,2,0:T(8,128)S(1)}, f32[4,128,8,128]{3,1,2,0:T(8,128)S(1)})) conditional(s32[]{:T(128)} %convert_element_type.69, (f32[4,128,8]{1,2,0:T(8,128)S(1)}, f32[4,128,8]{1,2,0:T(8,128)S(1)}, f32[4,128,8,128]{3,1,2,0:T(8,128)S(1)}) %tuple.115, (pred[1,128]{1,0:T(4,128)(4,1)S(1)}, ...), branch_computations={%region_24.24_spmd, %region_25.27_spmd} | conditional | flops 275259392 | bytes 12584100 | solution.py:71
  86.6 1.7 %bitcast_reduce_fusion.1 = (f32[4,128,8]{1,2,0:T(8,128)S(1)}, f32[4,128,128,8]{2,1,3,0:T(8,128)S(1)}) fusion(pred[128]{0:T(512)(128)(4,1)S(1)} %bitcast.154, bf16[128,4,8,128]{3,0,2,1:T(8,128)(2,1)} %get-tuple-element.256, bf16[128,4,256]{2,0,1:T(8,128)(2,1)S(1)} %dynamic-slice_bitcast_fusion.1), kind=kOutput, calls=%fused_computation.58 | convolution fusion | flops 135786496 | bytes 3293696 | tf_op jit(solution)/shard_map/while/body/eval_jaxpr/cond/branch_1_fun/tgqd,kgd->gtqk/dot_general | solution.py:36
  88.8 1.4 %multiply_add_fusion.6 = f32[4,128,8,128]{3,1,2,0:T(8,128)S(1)} fusion(f32[4,128,8,128]{3,1,2,0:T(8,128)S(1)} %get-tuple-element.258, f32[4,128,128,8]{2,1,3,0:T(8,128)S(1)} %get-tuple-element.459, f32[4,128,8]{1,2,0:T(8,128)S(1)} %get-tuple-element.443, f32[4,128,8]{1,2,0:T(8,128)S(1)} %max.15, pred[128]{0:T(512)(128)(4,1)S(1)} %bitcast.156, ...), kind=kOutput, calls=%fused_computation.60 | convolution fusion | flops 137363456 | bytes 6455808 | tf_op jit(solution)/shard_map/while/body/eval_jaxpr/cond/branch_1_fun/gtqk,kgd->gtqd/dot_general | solution.py:48
  91.6 4.7 %conditional.9 = ((f32[4,128,8]{1,2,0:T(8,128)S(1)}, f32[4,128,8]{1,2,0:T(8,128)S(1)}, f32[4,128,8,128]{3,1,2,0:T(8,128)S(1)})) conditional(s32[]{:T(128)} %convert_element_type.69, (f32[4,128,8]{1,2,0:T(8,128)S(1)}, f32[4,128,8]{1,2,0:T(8,128)S(1)}, f32[4,128,8,128]{3,1,2,0:T(8,128)S(1)}) %tuple.115, (pred[1,128]{1,0:T(4,128)(4,1)S(1)}, ...), branch_computations={%region_24.24_spmd, %region_25.27_spmd} | conditional | flops 275259392 | bytes 12584100 | solution.py:71
  92.6 1.7 %bitcast_reduce_fusion.1 = (f32[4,128,8]{1,2,0:T(8,128)S(1)}, f32[4,128,128,8]{2,1,3,0:T(8,128)S(1)}) fusion(pred[128]{0:T(512)(128)(4,1)S(1)} %bitcast.154, bf16[128,4,8,128]{3,0,2,1:T(8,128)(2,1)} %get-tuple-element.256, bf16[128,4,256]{2,0,1:T(8,128)(2,1)S(1)} %dynamic-slice_bitcast_fusion.1), kind=kOutput, calls=%fused_computation.58 | convolution fusion | flops 135786496 | bytes 3293696 | tf_op jit(solution)/shard_map/while/body/eval_jaxpr/cond/branch_1_fun/tgqd,kgd->gtqk/dot_general | solution.py:36
  94.9 1.4 %multiply_add_fusion.6 = f32[4,128,8,128]{3,1,2,0:T(8,128)S(1)} fusion(f32[4,128,8,128]{3,1,2,0:T(8,128)S(1)} %get-tuple-element.258, f32[4,128,128,8]{2,1,3,0:T(8,128)S(1)} %get-tuple-element.459, f32[4,128,8]{1,2,0:T(8,128)S(1)} %get-tuple-element.443, f32[4,128,8]{1,2,0:T(8,128)S(1)} %max.15, pred[128]{0:T(512)(128)(4,1)S(1)} %bitcast.156, ...), kind=kOutput, calls=%fused_computation.60 | convolution fusion | flops 137363456 | bytes 6455808 | tf_op jit(solution)/shard_map/while/body/eval_jaxpr/cond/branch_1_fun/gtqk,kgd->gtqd/dot_general | solution.py:48
  97.6 4.7 %conditional.9 = ((f32[4,128,8]{1,2,0:T(8,128)S(1)}, f32[4,128,8]{1,2,0:T(8,128)S(1)}, f32[4,128,8,128]{3,1,2,0:T(8,128)S(1)})) conditional(s32[]{:T(128)} %convert_element_type.69, (f32[4,128,8]{1,2,0:T(8,128)S(1)}, f32[4,128,8]{1,2,0:T(8,128)S(1)}, f32[4,128,8,128]{3,1,2,0:T(8,128)S(1)}) %tuple.115, (pred[1,128]{1,0:T(4,128)(4,1)S(1)}, ...), branch_computations={%region_24.24_spmd, %region_25.27_spmd} | conditional | flops 275259392 | bytes 12584100 | solution.py:71
  98.6 1.7 %bitcast_reduce_fusion.1 = (f32[4,128,8]{1,2,0:T(8,128)S(1)}, f32[4,128,128,8]{2,1,3,0:T(8,128)S(1)}) fusion(pred[128]{0:T(512)(128)(4,1)S(1)} %bitcast.154, bf16[128,4,8,128]{3,0,2,1:T(8,128)(2,1)} %get-tuple-element.256, bf16[128,4,256]{2,0,1:T(8,128)(2,1)S(1)} %dynamic-slice_bitcast_fusion.1), kind=kOutput, calls=%fused_computation.58 | convolution fusion | flops 135786496 | bytes 3293696 | tf_op jit(solution)/shard_map/while/body/eval_jaxpr/cond/branch_1_fun/tgqd,kgd->gtqk/dot_general | solution.py:36
  100.9 1.4 %multiply_add_fusion.6 = f32[4,128,8,128]{3,1,2,0:T(8,128)S(1)} fusion(f32[4,128,8,128]{3,1,2,0:T(8,128)S(1)} %get-tuple-element.258, f32[4,128,128,8]{2,1,3,0:T(8,128)S(1)} %get-tuple-element.459, f32[4,128,8]{1,2,0:T(8,128)S(1)} %get-tuple-element.443, f32[4,128,8]{1,2,0:T(8,128)S(1)} %max.15, pred[128]{0:T(512)(128)(4,1)S(1)} %bitcast.156, ...), kind=kOutput, calls=%fused_computation.60 | convolution fusion | flops 137363456 | bytes 6455808 | tf_op jit(solution)/shard_map/while/body/eval_jaxpr/cond/branch_1_fun/gtqk,kgd->gtqd/dot_general | solution.py:48
  103.8 1.4 %copy.166 = bf16[16,8,32,128]{3,1,2,0:T(8,128)(2,1)} copy(bf16[16,8,32,128]{3,2,1,0:T(8,128)(2,1)S(1)} %bitcast.141) | data formatting | bytes 2097152
  (98 shorter events, 22.3 us)
Async XLA Ops:
  0.6 1.8 %copy-start = (bf16[32,8,1024]{2,1,0:T(8,128)(2,1)S(1)}, bf16[32,8,1024]{2,1,0:T(8,128)(2,1)}, u32[]{:S(2)}) copy-start(bf16[32,8,1024]{2,1,0:T(8,128)(2,1)} %param.20) | copy-start | bytes 1572868
  0.6 19.9 %copy-start.4 = (bf16[128,4096]{1,0:T(8,128)(2,1)S(1)}, bf16[128,4096]{1,0:T(8,128)(2,1)}, u32[]{:S(2)}) copy-start(bf16[128,4096]{1,0:T(8,128)(2,1)} %param.18) | copy-start | bytes 3145732
  3.8 28.6 %all-to-all-start = ((bf16[16,1,8,1024]{3,2,1,0:T(8,128)(2,1)}), bf16[16,1,8,1024]{3,2,1,0:T(8,128)(2,1)S(1)}, u32[]{:S(2)}, u32[]{:S(2)}) async-start(bf16[16,1,8,1024]{3,2,1,0:T(8,128)(2,1)} %bitcast.28), calls=%async_computation | async-start | bytes 524288 | tf_op jit(solution)/shard_map/all_to_all | solution.py:97
  11.4 14.3 %collective-permute-start = (bf16[128,1024]{0,1:T(8,128)(2,1)S(1)}, bf16[128,1024]{0,1:T(8,128)(2,1)S(1)}, u32[]{:S(2)}, u32[]{:S(2)}) collective-permute-start(bf16[128,1024]{0,1:T(8,128)(2,1)S(1)} %copy.108), channel_id=1, source_target_pairs={{0,1},{1,2},{2,3},{3,4},{4,5},{5,6},{6,7},{7,8},{8,9},{9,10},{10,1... | collective-permute-start | bytes 786440 | tf_op jit(solution)/shard_map/ppermute | solution.py:23
  21.2 16.2 %copy-start.1 = (bf16[128,4096]{0,1:T(8,128)(2,1)}, bf16[128,4096]{0,1:T(8,128)(2,1)S(1)}, u32[]{:S(2)}) copy-start(bf16[128,4096]{0,1:T(8,128)(2,1)S(1)} %copy.105) | copy-start | bytes 3145732
  21.2 2.1 %copy-start.5 = (bf16[8,16,4,256]{3,2,1,0:T(4,128)(2,1)S(1)}, bf16[8,16,4,256]{3,2,1,0:T(4,128)(2,1)}, u32[]{:S(2)}) copy-start(bf16[8,16,4,256]{3,2,1,0:T(4,128)(2,1)} %reshape.368) | copy-start | bytes 786436
  26.6 17.5 %collective-permute-start.1 = (bf16[256,1024]{0,1:T(8,128)(2,1)}, bf16[256,1024]{0,1:T(8,128)(2,1)}, u32[]{:S(2)}, u32[]{:S(2)}) collective-permute-start(bf16[256,1024]{0,1:T(8,128)(2,1)} %pad_maximum_fusion.1), channel_id=1, source_target_pairs={{0,2},{1,3},{2,4},{3,5},{4,6},{5,7},{6,8},{7,9},{8,10},{9,11},{10,... | collective-permute-start | bytes 1572872 | tf_op jit(solution)/shard_map/ppermute | solution.py:23
  32.4 24.4 %all-to-all-start.1 = ((bf16[4,16,8,256]{3,2,0,1:T(8,128)(2,1)}), bf16[4,16,8,256]{3,2,0,1:T(8,128)(2,1)}, u32[]{:S(2)}, u32[]{:S(2)}) async-start(bf16[4,16,8,256]{3,2,0,1:T(8,128)(2,1)} %copy_select_fusion), calls=%async_computation.1 | async-start | bytes 524288 | tf_op jit(solution)/shard_map/all_to_all | solution.py:140
  43.0 7.0 %copy-start.2 = (f32[4,128,8,128]{1,3,2,0:T(8,128)S(1)}, f32[4,128,8,128]{1,3,2,0:T(8,128)}, u32[]{:S(2)}) copy-start(f32[4,128,8,128]{1,3,2,0:T(8,128)} %get-tuple-element.461) | copy-start | bytes 6291460
  43.0 7.5 %copy-start.3 = (f32[4,128,8,128]{1,3,2,0:T(8,128)S(1)}, f32[4,128,8,128]{1,3,2,0:T(8,128)}, u32[]{:S(2)}) copy-start(f32[4,128,8,128]{1,3,2,0:T(8,128)} %get-tuple-element.461) | copy-start | bytes 6291460
  46.4 27.2 %collective-permute-start.2 = (bf16[512,1024]{0,1:T(8,128)(2,1)}, bf16[512,1024]{0,1:T(8,128)(2,1)}, u32[]{:S(2)}, u32[]{:S(2)}) collective-permute-start(bf16[512,1024]{0,1:T(8,128)(2,1)} %pad_maximum_fusion), channel_id=1, source_target_pairs={{0,4},{1,5},{2,6},{3,7},{4,8},{5,9},{6,10},{7,11},{8,12},{9,13},{1... | collective-permute-start | bytes 3145736 | tf_op jit(solution)/shard_map/ppermute | solution.py:23
where the time goes:
time: 106 us; the launch traced here: 105 us
  matrix products  30.1 us (28%)
  local copies, waits for them, and re-layouts  26.9 us (25%)
  starting transfers between devices  21.4 us (20%)
  other arithmetic  17.7 us (17%)
  loops' own time  4.68 us (4%)
  waiting for transfers between devices  2.78 us (3%)
  between operations  1.61 us (2%)
    dot_general x9, matrix products, absorb(): jnp.einsum('gtqk,kgd->gtqd', probabilities.astype(jnp.bfloat16), key_bloc...  16 us
    dot_general x9, matrix products, absorb(): jnp.einsum('tgqd,kgd->gtqk', query_heads, key_block[:, :, :head_size], pr...  14.1 us
    ppermute x3, starting transfers between devices, passed_along(): return lax.ppermute(block, axis, route)  10 us
    all_to_all x1, starting transfers between devices, shards(): lax.all_to_all(outgoing, 'seq', split_axis=0, concat_axis=0, tiled=True)  6.55 us
    reduce_or x7, other arithmetic, visit(): jnp.any(block_mask)  5.27 us
    while x3, local copies, waits for them, and re-layouts, absorb_blocks(): return lax.scan(visit, running, (key_blocks, block_ok))[0]  5.06 us
    all_to_all x1, starting transfers between devices, shards(): lax.all_to_all(outgoing_new, 'seq', split_axis=1, concat_axis=2, tiled=True)  4.87 us
    reduce_sum x9, other arithmetic, absorb(): denom_new = denom_old * factor + jnp.sum(probabilities, axis=-1)  4.69 us
  transfers between devices with their start and end apart: 5, of which 2 were waited for; matrix products, arithmetic and copies ran while one was open for 41% of the time, Pallas kernels for 0%

commit v1 on v0

v1 whole, which is shorter than its diff:
```python
import functools

import jax
import jax.numpy as jnp
from jax import lax
from jax.experimental import pallas as pl
from jax.experimental.pallas import tpu as pltpu
from jax.sharding import PartitionSpec as P

HD = 128
QH = 32
KVH = 4
REQS = 2
PAGE = 8
SLOTS = 32
GQ = QH // KVH

LOG2E = 1.4426950408889634
OUT_OF_REACH = -1e30
CHUNK = 384
VMEM_BYTES = 48 * 1024 * 1024
CONTRACT_LAST = (((1,), (1,)), ((), ()))

IN_VMEM = pl.BlockSpec(memory_space=pltpu.VMEM)
IN_SMEM = pl.BlockSpec(memory_space=pltpu.SMEM)
ANYWHERE = pl.BlockSpec(memory_space=pl.ANY)


def hop_bits(devices):
    bits = []
    bit = 2
    while bit < devices // REQS:
        bits.append(bit)
        bit *= 2
    return (tuple(bits), tuple(reversed(bits)))


def pick(core, pair):
    return jnp.where(core == 0, pair[0], pair[1])


def swap(value, bit):
    route = [(i, i ^ bit) for i in range(lax.axis_size("seq"))]
    return lax.ppermute(value, "seq", route)


def swap_by_core(value, orders, step):
    route = [(i, i ^ orders[i % 2][step]) for i in range(lax.axis_size("seq"))]
    return lax.ppermute(value, "seq", route)


def page_kernel(devices, table_ref, store_ref, own_ref, other_ref, sems):
    me = lax.axis_index("seq")
    request = me // (devices // REQS)

    def slot_of(req):
        def visit(j, found):
            entry = table_ref[req, j]
            return jnp.where(entry // SLOTS == me, entry % SLOTS, found)

        return lax.fori_loop(0, table_ref.shape[1], visit, jnp.int32(0), unroll=True)

    other = pltpu.make_async_copy(store_ref.at[slot_of(1 - request)], other_ref, sems.at[0])
    other.start()
    own = pltpu.make_async_copy(store_ref.at[slot_of(request)], own_ref, sems.at[1])
    own.start()
    other.wait()
    own.wait()


def fetch_pages(page_table, kv_store, devices):
    page = jax.ShapeDtypeStruct(kv_store.shape[1:], kv_store.dtype)
    return pl.pallas_call(
        functools.partial(page_kernel, devices),
        out_shape=(page, page),
        in_specs=[IN_SMEM, ANYWHERE],
        out_specs=(ANYWHERE, ANYWHERE),
        scratch_shapes=[pltpu.SemaphoreType.DMA((2,))],
        name="fetch_pages",
    )(page_table, kv_store)


def source_of(me, swapped, steps, orders):
    at = me ^ 1 if swapped else me
    core = at % 2
    for step in steps:
        at = at ^ pick(core, (orders[0][step], orders[1][step]))
    return at


def prefix_bias(me, devices, orders, table_ref, hit_ref, swapped, rows):
    lane = lax.broadcasted_iota(jnp.int32, (1, rows), 1)
    slot = lane // PAGE
    at = jnp.full((1, rows), me ^ 1 if swapped else me, jnp.int32)
    core = (me ^ 1 if swapped else me) % 2
    hops = [devices // REQS] + [pick(core, (orders[0][s], orders[1][s])) for s in range(len(orders[0]))]
    for n, hop in enumerate(hops):
        at = jnp.where((slot // (2**n)) % 2 == 1, at ^ hop, at)
    request = me // (devices // REQS)

    def visit(j, page):
        return jnp.where(at == table_ref[request, j] // SLOTS, j, page)

    page = lax.fori_loop(0, table_ref.shape[1], visit, jnp.zeros((1, rows), jnp.int32), unroll=True)
    return jnp.where(page * PAGE + lane % PAGE < hit_ref[request], 0.0, OUT_OF_REACH)


def attend_kernel(devices, orders, kinds, first, last, *refs):
    refs = list(refs)
    table_ref, hit_ref, q_ref = refs[:3]
    key_refs = refs[3 : 3 + len(kinds)]
    rest = refs[3 + len(kinds) :]
    if not first:
        top_in, denom_in, sum_in = rest[:3]
        rest = rest[3:]
    if last:
        (out_ref,) = rest
    else:
        top_ref, denom_ref, sum_ref = rest
    me = lax.axis_index("seq")
    rows = q_ref.shape[0]

    pieces = []
    for ref, kind in zip(key_refs, kinds):
        length = ref.shape[0]
        if kind[0] == "own":
            t = lax.broadcasted_iota(jnp.int32, (rows, length), 0)
            k = lax.broadcasted_iota(jnp.int32, (rows, length), 1)
            bias = jnp.where(k <= t, 0.0, OUT_OF_REACH)
        elif kind[0] == "block":
            source = source_of(me, kind[1], kind[2], orders)
            bias = jnp.full((1, length), jnp.where(source < me, 0.0, OUT_OF_REACH), jnp.float32)
        else:
            bias = prefix_bias(me, devices, orders, table_ref, hit_ref, kind[1], length)
        for at in range(0, length, 128):
            size = min(128, length - at)
            pieces.append((ref, at, size, bias[:, at : at + size]))
    chunks = []
    for piece in pieces:
        if chunks and sum(p[2] for p in chunks[-1]) + piece[2] <= CHUNK:
            chunks[-1].append(piece)
        else:
            chunks.append([piece])

    full_biases = []
    for chunk in chunks:
        tall = any(p[3].shape[0] > 1 for p in chunk)
        full_biases.append(
            jnp.concatenate([jnp.broadcast_to(p[3], (rows if tall else 1, p[2])) for p in chunk], axis=1)
        )

    scale = HD**-0.5 * LOG2E
    for g in range(KVH):
        heads = range(g * GQ, (g + 1) * GQ)
        span = pl.ds(g * GQ * rows, GQ * rows)
        q = jnp.concatenate([q_ref[:, h * HD : (h + 1) * HD] for h in heads], axis=0)
        top = denom = total = None
        if not first:
            top, denom, total = top_in[span, 0:1], denom_in[span, 0:1], sum_in[span, :]
        for chunk, bias in zip(chunks, full_biases):
            at = g * 2 * HD
            keys = jnp.concatenate([p[0][p[1] : p[1] + p[2], at : at + HD] for p in chunk], axis=0)
            values = jnp.concatenate([p[0][p[1] : p[1] + p[2], at + HD : at + 2 * HD] for p in chunk], axis=0)
            scores = lax.dot_general(q, keys, CONTRACT_LAST, preferred_element_type=jnp.float32)
            if bias.shape[0] > 1:
                scores = (scores.reshape(GQ, rows, -1) + bias[None]).reshape(GQ * rows, -1)
            else:
                scores = scores + bias
            peak = jnp.max(scores, axis=1, keepdims=True)
            new_top = peak if top is None else jnp.maximum(top, peak)
            probabilities = jnp.exp2((scores - new_top) * scale)
            mass = jnp.sum(probabilities, axis=1, keepdims=True)
            weighted = jnp.dot(probabilities.astype(jnp.bfloat16), values, preferred_element_type=jnp.float32)
            if top is None:
                denom, total = mass, weighted
            else:
                factor = jnp.exp2((top - new_top) * scale)
                denom, total = denom * factor + mass, total * factor + weighted
            top = new_top
        if last:
            attended = (total / denom).astype(out_ref.dtype)
            for n, h in enumerate(heads):
                out_ref[:, h * HD : (h + 1) * HD] = attended[n * rows : (n + 1) * rows]
        else:
            top_ref[span, :] = jnp.broadcast_to(top, (GQ * rows, HD))
            denom_ref[span, :] = jnp.broadcast_to(denom, (GQ * rows, HD))
            sum_ref[span, :] = total


def attend(devices, orders, page_table, hit_tokens, queries, arrays, kinds, running, last):
    rows = queries.shape[0]
    count = len(arrays)
    keys = sum(a.shape[0] for a in arrays)
    if last:
        out_shape = jax.ShapeDtypeStruct((rows, QH * HD), queries.dtype)
        out_specs = IN_VMEM
    else:
        out_shape = (jax.ShapeDtypeStruct((QH * rows, HD), jnp.float32),) * 3
        out_specs = (IN_VMEM,) * 3
    state = () if running is None else tuple(running)
    return pl.pallas_call(
        functools.partial(attend_kernel, devices, orders, tuple(kinds), running is None, last),
        out_shape=out_shape,
        in_specs=[IN_SMEM, IN_SMEM, IN_VMEM] + [IN_VMEM] * (count + len(state)),
        out_specs=out_specs,
        input_output_aliases={} if last or not state else {3 + count + n: n for n in range(3)},
        compiler_params=pltpu.CompilerParams(vmem_limit_bytes=VMEM_BYTES),
        cost_estimate=pl.CostEstimate(
            flops=8 * rows * QH * keys * HD, bytes_accessed=4 * rows * QH * HD, transcendentals=rows * QH * keys
        ),
        name="attend",
    )(page_table, hit_tokens, queries, *arrays, *state)


def owner_kernel(devices, orders, kinds, offset_ref, *refs):
    key_refs = refs[: len(kinds)]
    own_ref, other_ref = refs[len(kinds) :]
    me = lax.axis_index("seq")
    group_size = devices // REQS
    request = me // group_size
    rows = key_refs[0].shape[0]
    kept = own_ref.shape[1]
    targets = []
    row = lax.broadcasted_iota(jnp.int32, (2 * kept, rows), 0)
    lane = lax.broadcasted_iota(jnp.int32, (1, rows), 1)
    half = row >= kept
    for ref, kind in zip(key_refs, kinds):
        source = me if kind[0] == "own" else source_of(me, kind[1], kind[2], orders)
        position = (source % group_size) * rows + lane
        targets.append(position)
    for g in range(KVH):
        turn = (me - offset_ref[request, g] + devices) % devices
        other_turn = turn ^ (devices // REQS)
        total = jnp.zeros((2 * kept, 2 * HD), jnp.float32)
        for ref, position in zip(key_refs, targets):
            m, residue = position // devices, position % devices
            chosen = (jnp.where(half, other_turn, turn) == residue) & (jnp.where(half, row - kept, row) == m)
            total = total + jnp.dot(
                jnp.where(chosen, 1.0, 0.0).astype(jnp.bfloat16),
                ref[:, g * 2 * HD : (g + 1) * 2 * HD],
                preferred_element_type=jnp.float32,
            )
        own_ref[g] = total[:kept].astype(own_ref.dtype)
        other_ref[g] = total[kept:].astype(other_ref.dtype)


def pick_for_owners(devices, orders, owner_offset, arrays, kinds):
    rows, width = arrays[0].shape
    kept = (devices // REQS) * rows // devices
    piece = jax.ShapeDtypeStruct((KVH, kept, 2 * HD), arrays[0].dtype)
    return pl.pallas_call(
        functools.partial(owner_kernel, devices, orders, tuple(kinds)),
        out_shape=(piece, piece),
        in_specs=[IN_SMEM] + [IN_VMEM] * len(arrays),
        out_specs=(IN_VMEM, IN_VMEM),
        compiler_params=pltpu.CompilerParams(vmem_limit_bytes=VMEM_BYTES),
        name="pick_for_owners",
    )(owner_offset, *arrays)


def place_kernel(devices, own_ref, other_ref, out_ref):
    request = lax.axis_index("seq") // (devices // REQS)
    kept = own_ref.shape[1]

    @pl.when(request == 0)
    def _():
        out_ref[0, :, :kept] = own_ref[...]
        out_ref[0, :, kept:] = other_ref[...]

    @pl.when(request == 1)
    def _():
        out_ref[0, :, :kept] = other_ref[...]
        out_ref[0, :, kept:] = own_ref[...]


def place(devices, own, other):
    heads, kept, width = own.shape
    return pl.pallas_call(
        functools.partial(place_kernel, devices),
        out_shape=jax.ShapeDtypeStruct((1, heads, REQS * kept, width), own.dtype),
        in_specs=[IN_VMEM, IN_VMEM],
        out_specs=IN_VMEM,
        name="place",
    )(own, other)


def shards(queries, suffix_kv, kv_store, page_table, hit_tokens, owner_offset):
    devices = lax.axis_size("seq")
    orders = hop_bits(devices)
    steps = len(orders[0])

    held = [((), suffix_kv)]
    moved = []
    for step in range(steps):
        arrived = [(path + (step,), swap_by_core(value, orders, step)) for path, value in held]
        moved.append(arrived)
        held = held + arrived
    own_swapped = swap(suffix_kv, 1)
    moved_swapped = [[(path, swap(value, 1)) for path, value in arrived] for arrived in moved]

    own_page, other_page = fetch_pages(page_table, kv_store, devices)
    pages = jnp.concatenate([own_page, swap(other_page, devices // REQS)], axis=0)
    for step in range(steps):
        pages = jnp.concatenate([pages, swap_by_core(pages, orders, step)], axis=0)
    pages_swapped = swap(pages, 1)

    call = functools.partial(attend, devices, orders, page_table, hit_tokens, queries)
    running = call([suffix_kv, own_swapped], [("own",), ("block", True, ())], None, False)
    arrays, kinds = [], []
    batches = []
    for step in range(steps):
        for (path, value), (_, value_swapped) in zip(reversed(moved[step]), reversed(moved_swapped[step])):
            batches.append(([value, value_swapped], [("block", False, path), ("block", True, path)]))
    everything = [suffix_kv, own_swapped]
    every_kind = [("own",), ("block", True, ())]
    for batch, batch_kinds in batches:
        everything += batch
        every_kind += batch_kinds
    own_piece, other_piece = pick_for_owners(devices, orders, owner_offset, everything, every_kind)
    landed = swap(other_piece, devices // REQS)

    for batch, batch_kinds in batches[:-1]:
        running = call(batch, batch_kinds, running, False)
    batch, batch_kinds = batches[-1]
    attention_out = call(
        batch + [pages, pages_swapped], batch_kinds + [("pages", False), ("pages", True)], running, True
    )
    return (attention_out, place(devices, own_piece, landed))


def solution(mesh):
    in_specs = (
        P(("groups", "seq"), None),
        P(("groups", "seq"), None),
        P(("groups", "seq"), None, None),
        P("groups", None),
        P("groups"),
        P("groups", None),
    )
    out_specs = (P(("groups", "seq"), None), P(("groups", "seq"), None, None, None))
    return jax.shard_map(shards, mesh=mesh, in_specs=in_specs, out_specs=out_specs, check_vma=False)
```

time: 106 us -> 62.4 us (0.59)
  the two profiles are of different devices: /device:TPU:11 before, /device:TPU:0 now
where the time goes in v1:
time: 62.4 us; the launch traced here: 61.9 us
  Pallas kernels  34.8 us (56%)
  starting transfers between devices  12.5 us (20%)
  waiting for transfers between devices  7.56 us (12%)
  local copies, waits for them, and re-layouts  4.88 us (8%)
  other arithmetic  1.44 us (2%)
  between operations  0.71 us (1%)
    pallas_call x4, Pallas kernels, attend(): pl.pallas_call(functools.partial(attend_kernel, devices, orders, tuple(ki...  29 us
    ppermute x5, starting transfers between devices, swap_by_core(): return lax.ppermute(value, 'seq', route)  6.7 us
    ppermute x5, waiting for transfers between devices, swap_by_core(): return lax.ppermute(value, 'seq', route)  5.94 us
    ppermute x7, starting transfers between devices, swap(): return lax.ppermute(value, 'seq', route)  5.78 us
    unnamed x19, local copies, waits for them, and re-layouts  4.88 us
    pallas_call x1, Pallas kernels, fetch_pages(): pl.pallas_call(functools.partial(page_kernel, devices), out_shape=(page,...  2.91 us
    pallas_call x1, Pallas kernels, place(): pl.pallas_call(functools.partial(place_kernel, devices), out_shape=jax.Sh...  1.69 us
    ppermute x7, waiting for transfers between devices, swap(): return lax.ppermute(value, 'seq', route)  1.62 us
  transfers between devices with their start and end apart: 12, of which 4 were waited for; matrix products, arithmetic and copies ran while one was open for 4% of the time, Pallas kernels for 54%

profile of v1, /device:TPU:0, one launch (start us, length us, event | category | flops | bytes accessed | tf_op | source)
XLA Modules:
  0.0 61.9 jit_solution(4616127811169176134)
XLA Ops:
  0.6 3.0 %collective-permute-start.6 = (bf16[128,1024]{1,0:T(8,128)(2,1)}, bf16[128,1024]{1,0:T(8,128)(2,1)S(1)}, u32[]{:S(2)}, u32[]{:S(2)}) collective-permute-start(bf16[128,1024]{1,0:T(8,128)(2,1)} %refs_0_.9), channel_id=1, source_target_pairs={{0,2},{1,5},{2,0},{3,7},{4,6},{5,1},{6,4},{7,3},{8,10},{9,13},{10,... | collective-permute-start | bytes 786440 | tf_op jit(solution)/shard_map/ppermute | solution.py:49
  3.6 0.0 collective-permute-start.10
  3.6 1.6 %collective-permute-start = (bf16[128,1024]{1,0:T(8,128)(2,1)}, bf16[128,1024]{1,0:T(8,128)(2,1)S(1)}, u32[]{:S(2)}, u32[]{:S(2)}) collective-permute-start(bf16[128,1024]{1,0:T(8,128)(2,1)} %refs_0_.9), channel_id=1, source_target_pairs={{0,4},{1,3},{2,6},{3,1},{4,0},{5,7},{6,2},{7,5},{8,12},{9,11},{10,... | collective-permute-start | bytes 786440 | tf_op jit(solution)/shard_map/ppermute | solution.py:49
  5.2 2.9 %fetch_pages.1 = (bf16[8,1024]{1,0:T(8,128)(2,1)}, bf16[8,1024]{1,0:T(8,128)(2,1)}) custom-call(s32[2,16]{1,0:T(2,128)} %refs_0_.8, bf16[32,8,1024]{2,1,0:T(8,128)(2,1)} %store_ref.1), custom_call_target="tpu_custom_call" | custom-call | tf_op jit(solution)/shard_map/fetch_pages/pallas_call | solution.py:73
  8.1 2.7 %collective-permute-start.2 = (bf16[8,1024]{1,0:T(8,128)(2,1)}, bf16[8,1024]{1,0:T(8,128)(2,1)S(1)}, u32[]{:S(2)}, u32[]{:S(2)}) collective-permute-start(bf16[8,1024]{1,0:T(8,128)(2,1)} %get-tuple-element.16), channel_id=1, source_target_pairs={{0,8},{1,9},{2,10},{3,11},{4,12},{5,13},{6,14},{7,15},{8,0},{9,1},... | collective-permute-start | bytes 49160 | tf_op jit(solution)/shard_map/ppermute | solution.py:44
  10.8 0.7 %constant_dynamic-update-slice_fusion.3 = bf16[64,1024]{1,0:T(8,128)(2,1)S(1)} fusion(bf16[8,1024]{1,0:T(8,128)(2,1)} %get-tuple-element.15), kind=kLoop, calls=%fused_computation.5 | loop fusion | bytes 32768
  11.5 1.6 %collective-permute-done.2 = bf16[8,1024]{1,0:T(8,128)(2,1)S(1)} collective-permute-done((bf16[8,1024]{1,0:T(8,128)(2,1)}, bf16[8,1024]{1,0:T(8,128)(2,1)S(1)}, u32[]{:S(2)}, u32[]{:S(2)}) %collective-permute-start.2) | collective-permute-done | bytes 16416 | tf_op jit(solution)/shard_map/ppermute | solution.py:44
  13.1 0.7 %pad_maximum_fusion.1 = bf16[16,1024]{1,0:T(8,128)(2,1)S(1)} fusion(bf16[8,1024]{1,0:T(8,128)(2,1)S(1)} %collective-permute-done.2, bf16[8,1024]{1,0:T(8,128)(2,1)} %get-tuple-element.15), kind=kLoop, calls=%fused_computation.1 | loop fusion | flops 65536 | bytes 65536 | tf_op jit(solution)/shard_map/concatenate | solution.py:302
  13.8 0.5 collective-permute-start.3
  14.3 0.0 collective-permute-done.6.refs_3_.refs_2_
  14.3 1.3 %collective-permute-start.7 = (bf16[128,1024]{1,0:T(8,128)(2,1)S(1)}, bf16[128,1024]{1,0:T(8,128)(2,1)S(1)}, u32[]{:S(2)}, u32[]{:S(2)}) collective-permute-start(bf16[128,1024]{1,0:T(8,128)(2,1)S(1)} %collective-permute-done.6.refs_3_.refs_2_), channel_id=1, source_target_pairs={{0,4},{1,3},{2,6},{3,1},{4,0},{5,7},{6,2},{7,5},{8,12},{9,11},{10,... | collective-permute-start | bytes 786440 | tf_op jit(solution)/shard_map/ppermute | solution.py:49
  15.6 2.6 %collective-permute-done.3 = bf16[16,1024]{1,0:T(8,128)(2,1)S(1)} collective-permute-done((bf16[16,1024]{1,0:T(8,128)(2,1)S(1)}, bf16[16,1024]{1,0:T(8,128)(2,1)S(1)}, u32[]{:S(2)}, u32[]{:S(2)}) %collective-permute-start.3) | collective-permute-done | bytes 32800 | tf_op jit(solution)/shard_map/ppermute | solution.py:49
  18.2 0.7 %pad_maximum_fusion = bf16[32,1024]{1,0:T(8,128)(2,1)S(1)} fusion(bf16[16,1024]{1,0:T(8,128)(2,1)S(1)} %collective-permute-done.3, bf16[8,1024]{1,0:T(8,128)(2,1)S(1)} %collective-permute-done.2, bf16[8,1024]{1,0:T(8,128)(2,1)} %get-tuple-element.15), kind=kLoop, calls=%fused_computation | loop fusion | flops 196608 | bytes 131072 | tf_op jit(solution)/shard_map/concatenate | solution.py:304
  18.9 0.4 collective-permute-start.4
  19.3 0.0 collective-permute-start.9
  19.3 0.0 collective-permute-done.refs_3_.refs_6_
  19.3 0.5 collective-permute-start.1
  19.8 0.9 %collective-permute-done.7.refs_3_.refs_4_ = bf16[128,1024]{1,0:T(8,128)(2,1)S(1)} collective-permute-done((bf16[128,1024]{1,0:T(8,128)(2,1)S(1)}, bf16[128,1024]{1,0:T(8,128)(2,1)S(1)}, u32[]{:S(2)}, u32[]{:S(2)}) %collective-permute-start.7) | collective-permute-done | bytes 262176 | tf_op jit(solution)/shard_map/ppermute | solution.py:49
  20.7 0.0 collective-permute-start.8
  20.7 2.5 %collective-permute-done.4 = bf16[32,1024]{1,0:T(8,128)(2,1)S(1)} collective-permute-done((bf16[32,1024]{1,0:T(8,128)(2,1)S(1)}, bf16[32,1024]{1,0:T(8,128)(2,1)S(1)}, u32[]{:S(2)}, u32[]{:S(2)}) %collective-permute-start.4) | collective-permute-done | bytes 65568 | tf_op jit(solution)/shard_map/ppermute | solution.py:49
  23.1 0.0 collective-permute-start.5
  23.2 0.0 collective-permute-done.10.refs_4_.refs_1_
  23.2 0.0 copy-start
  23.2 1.2 %copy-done = bf16[128,4096]{1,0:T(8,128)(2,1)S(1)} copy-done((bf16[128,4096]{1,0:T(8,128)(2,1)S(1)}, bf16[128,4096]{1,0:T(8,128)(2,1)}, u32[]{:S(2)}) %copy-start) | copy-done | bytes 1048600
  24.4 0.0 copy-start.2
  24.4 0.9 %copy-done.2 = bf16[128,1024]{1,0:T(8,128)(2,1)S(1)} copy-done((bf16[128,1024]{1,0:T(8,128)(2,1)S(1)}, bf16[128,1024]{1,0:T(8,128)(2,1)}, u32[]{:S(2)}) %copy-start.2) | copy-done | bytes 262168
  25.3 0.0 copy-start.4
  25.3 0.7 %copy-done.4 = s32[2,16]{1,0:T(2,128)S(1)} copy-done((s32[2,16]{1,0:T(2,128)S(1)}, s32[2,16]{1,0:T(2,128)}, u32[]{:S(2)}) %copy-start.4) | copy-done | bytes 152
  26.0 0.0 copy-start.5
  26.0 0.7 %copy-done.5 = s32[2]{0:T(128)S(1)} copy-done((s32[2]{0:T(128)S(1)}, s32[2]{0:T(128)}, u32[]{:S(2)}) %copy-start.5) | copy-done | bytes 32
  26.7 3.5 %attend.4 = (f32[4096,128]{1,0:T(8,128)S(1)}, f32[4096,128]{1,0:T(8,128)S(1)}, f32[4096,128]{1,0:T(8,128)}) custom-call(s32[2,16]{1,0:T(2,128)S(1)} %copy-done.4, s32[2]{0:T(128)S(1)} %copy-done.5, bf16[128,4096]{1,0:T(8,128)(2,1)S(1)} %copy-done, bf16[128,1024]{1,0:T(8,128)(2,1)S(1)} %copy-done.2, bf16[128,1024]{1,0:T(8,128)(2,1)S(1)} %collective-permute-done.10.refs_4_.refs_1_), custom_call_target="tpu_custom_call" | custom-call | flops 1073741824 | bytes 2097152 | tf_op jit(solution)/shard_map/attend/pallas_call | solution.py:201
  30.1 0.0 collective-permute-done.9.refs_4_.refs_3_
  30.1 0.0 copy-start.6
  30.1 8.0 %attend.5 = (f32[4096,128]{1,0:T(8,128)S(1)}, f32[4096,128]{1,0:T(8,128)S(1)}, f32[4096,128]{1,0:T(8,128)}) custom-call(s32[2,16]{1,0:T(2,128)S(1)} %copy-done.4, s32[2]{0:T(128)S(1)} %copy-done.5, bf16[128,4096]{1,0:T(8,128)(2,1)S(1)} %copy-done, ...), custom_call_target="tpu_custom_call", output_to_operand_aliasing={{0}: (5, {}), {1}: (6, {}), {2}: (7, {})} | custom-call | flops 1073741824 | bytes 2097152 | tf_op jit(solution)/shard_map/attend/pallas_call | solution.py:201
  38.2 0.0 collective-permute-done.1.refs_4_.refs_7_
  38.2 0.0 collective-permute-done.8.refs_4_.refs_5_
  38.2 0.0 copy-done.6
  38.2 1.3 %pick_for_owners.1 = (bf16[4,64,256]{2,1,0:T(8,128)(2,1)S(1)}, bf16[4,64,256]{2,1,0:T(8,128)(2,1)S(1)}) custom-call(s32[2,4]{1,0:T(2,128)S(1)} %copy-done.6, bf16[128,1024]{1,0:T(8,128)(2,1)S(1)} %copy-done.2, bf16[128,1024]{1,0:T(8,128)(2,1)S(1)} %collective-permute-done.10.refs_4_.refs_1_, bf16[128,1024]{1,0:T(8,128)(2,1)S(1)} %collective-permute-done.6.refs_3_.refs_2_, ...), custom_call_target="tpu_custom_call" | custom-call | tf_op jit(solution)/shard_map/pick_for_owners/pallas_call | solution.py:251
  39.5 0.0 copy-start.3
  39.5 2.6 %collective-permute-start.11 = (bf16[4,64,256]{2,1,0:T(8,128)(2,1)S(1)}, bf16[4,64,256]{2,1,0:T(8,128)(2,1)S(1)}, u32[]{:S(2)}, u32[]{:S(2)}) collective-permute-start(bf16[4,64,256]{2,1,0:T(8,128)(2,1)S(1)} %get-tuple-element.27), channel_id=1, source_target_pairs={{0,8},{1,9},{2,10},{3,11},{4,12},{5,13},{6,14},{7,15},{8,0},{9,1},... | collective-permute-start | bytes 393224 | tf_op jit(solution)/shard_map/ppermute | solution.py:44
  42.1 0.0 copy-done.1
  42.1 8.2 %attend.6 = (f32[4096,128]{1,0:T(8,128)S(1)}, f32[4096,128]{1,0:T(8,128)S(1)}, f32[4096,128]{1,0:T(8,128)}) custom-call(s32[2,16]{1,0:T(2,128)S(1)} %copy-done.4, s32[2]{0:T(128)S(1)} %copy-done.5, bf16[128,4096]{1,0:T(8,128)(2,1)S(1)} %copy-done.1, ...), custom_call_target="tpu_custom_call", output_to_operand_aliasing={{0}: (5, {}), {1}: (6, {}), {2}: (7, {})} | custom-call | flops 1073741824 | bytes 2097152 | tf_op jit(solution)/shard_map/attend/pallas_call | solution.py:201
  50.3 0.0 copy-done.3
  50.3 0.0 collective-permute-done.5.refs_6_
  50.3 9.2 %attend.7 = bf16[128,4096]{1,0:T(8,128)(2,1)} custom-call(s32[2,16]{1,0:T(2,128)S(1)} %copy-done.4, s32[2]{0:T(128)S(1)} %copy-done.5, bf16[128,4096]{1,0:T(8,128)(2,1)S(1)} %copy-done.1, bf16[128,1024]{1,0:T(8,128)(2,1)S(1)} %collective-permute-done.refs_3_.refs_6_, bf16[128,1024]{1,0:T(8,128)(2,1)S(1)} %collective-permute-done.1.refs_4_.refs_7_, ...), custom_call_target="tpu_custom_call" | custom-call | flops 1610612736 | bytes 2097152 | tf_op jit(solution)/shard_map/attend/pallas_call | solution.py:201
  59.6 0.0 collective-permute-done.11.other_ref
  59.6 0.6 %copy-done.7 = bf16[4,64,256]{2,1,0:T(8,128)(2,1)} copy-done((bf16[4,64,256]{2,1,0:T(8,128)(2,1)}, bf16[4,64,256]{2,1,0:T(8,128)(2,1)S(1)}, u32[]{:S(2)}) %copy-start.7) | copy-done | bytes 131096
  60.2 1.7 %place.1 = bf16[1,4,128,256]{3,2,1,0:T(8,128)(2,1)} custom-call(bf16[4,64,256]{2,1,0:T(8,128)(2,1)} %copy-done.3, bf16[4,64,256]{2,1,0:T(8,128)(2,1)} %copy-done.7), custom_call_target="tpu_custom_call" | custom-call | tf_op jit(solution)/shard_map/place/pallas_call | solution.py:278
  (5 shorter events, 0.0 us)
Async XLA Ops:
  0.6 13.7 %collective-permute-start.6 = (bf16[128,1024]{1,0:T(8,128)(2,1)}, bf16[128,1024]{1,0:T(8,128)(2,1)S(1)}, u32[]{:S(2)}, u32[]{:S(2)}) collective-permute-start(bf16[128,1024]{1,0:T(8,128)(2,1)} %refs_0_.9), channel_id=1, source_target_pairs={{0,2},{1,5},{2,0},{3,7},{4,6},{5,1},{6,4},{7,3},{8,10},{9,13},{10,... | collective-permute-start | bytes 786440 | tf_op jit(solution)/shard_map/ppermute | solution.py:49
  3.6 19.5 %collective-permute-start.10 = (bf16[128,1024]{1,0:T(8,128)(2,1)}, bf16[128,1024]{1,0:T(8,128)(2,1)S(1)}, u32[]{:S(2)}, u32[]{:S(2)}) collective-permute-start(bf16[128,1024]{1,0:T(8,128)(2,1)} %refs_0_.9), channel_id=1, source_target_pairs={{0,1},{1,0},{2,3},{3,2},{4,5},{5,4},{6,7},{7,6},{8,9},{9,8},{10,11... | collective-permute-start | bytes 786440 | tf_op jit(solution)/shard_map/ppermute | solution.py:44
  3.6 15.6 %collective-permute-start = (bf16[128,1024]{1,0:T(8,128)(2,1)}, bf16[128,1024]{1,0:T(8,128)(2,1)S(1)}, u32[]{:S(2)}, u32[]{:S(2)}) collective-permute-start(bf16[128,1024]{1,0:T(8,128)(2,1)} %refs_0_.9), channel_id=1, source_target_pairs={{0,4},{1,3},{2,6},{3,1},{4,0},{5,7},{6,2},{7,5},{8,12},{9,11},{10,... | collective-permute-start | bytes 786440 | tf_op jit(solution)/shard_map/ppermute | solution.py:49
  8.1 5.0 %collective-permute-start.2 = (bf16[8,1024]{1,0:T(8,128)(2,1)}, bf16[8,1024]{1,0:T(8,128)(2,1)S(1)}, u32[]{:S(2)}, u32[]{:S(2)}) collective-permute-start(bf16[8,1024]{1,0:T(8,128)(2,1)} %get-tuple-element.16), channel_id=1, source_target_pairs={{0,8},{1,9},{2,10},{3,11},{4,12},{5,13},{6,14},{7,15},{8,0},{9,1},... | collective-permute-start | bytes 49160 | tf_op jit(solution)/shard_map/ppermute | solution.py:44
  13.8 4.3 %collective-permute-start.3 = (bf16[16,1024]{1,0:T(8,128)(2,1)S(1)}, bf16[16,1024]{1,0:T(8,128)(2,1)S(1)}, u32[]{:S(2)}, u32[]{:S(2)}) collective-permute-start(bf16[16,1024]{1,0:T(8,128)(2,1)S(1)} %pad_maximum_fusion.1), channel_id=1, source_target_pairs={{0,2},{1,5},{2,0},{3,7},{4,6},{5,1},{6,4},{7,3},{8,10},{9,13},{10,... | collective-permute-start | bytes 98312 | tf_op jit(solution)/shard_map/ppermute | solution.py:49
  14.3 6.4 %collective-permute-start.7 = (bf16[128,1024]{1,0:T(8,128)(2,1)S(1)}, bf16[128,1024]{1,0:T(8,128)(2,1)S(1)}, u32[]{:S(2)}, u32[]{:S(2)}) collective-permute-start(bf16[128,1024]{1,0:T(8,128)(2,1)S(1)} %collective-permute-done.6.refs_3_.refs_2_), channel_id=1, source_target_pairs={{0,4},{1,3},{2,6},{3,1},{4,0},{5,7},{6,2},{7,5},{8,12},{9,11},{10,... | collective-permute-start | bytes 786440 | tf_op jit(solution)/shard_map/ppermute | solution.py:49
  18.9 4.3 %collective-permute-start.4 = (bf16[32,1024]{1,0:T(8,128)(2,1)S(1)}, bf16[32,1024]{1,0:T(8,128)(2,1)S(1)}, u32[]{:S(2)}, u32[]{:S(2)}) collective-permute-start(bf16[32,1024]{1,0:T(8,128)(2,1)S(1)} %pad_maximum_fusion), channel_id=1, source_target_pairs={{0,4},{1,3},{2,6},{3,1},{4,0},{5,7},{6,2},{7,5},{8,12},{9,11},{10,... | collective-permute-start | bytes 196616 | tf_op jit(solution)/shard_map/ppermute | solution.py:49
  19.3 10.9 %collective-permute-start.9 = (bf16[128,1024]{1,0:T(8,128)(2,1)S(1)}, bf16[128,1024]{1,0:T(8,128)(2,1)S(1)}, u32[]{:S(2)}, u32[]{:S(2)}) collective-permute-start(bf16[128,1024]{1,0:T(8,128)(2,1)S(1)} %collective-permute-done.6.refs_3_.refs_2_), channel_id=1, source_target_pairs={{0,1},{1,0},{2,3},{3,2},{4,5},{5,4},{6,7},{7,6},{8,9},{9,8},{10,11... | collective-permute-start | bytes 786440 | tf_op jit(solution)/shard_map/ppermute | solution.py:44
  19.3 18.9 %collective-permute-start.1 = (bf16[128,1024]{1,0:T(8,128)(2,1)S(1)}, bf16[128,1024]{1,0:T(8,128)(2,1)S(1)}, u32[]{:S(2)}, u32[]{:S(2)}) collective-permute-start(bf16[128,1024]{1,0:T(8,128)(2,1)S(1)} %collective-permute-done.refs_3_.refs_6_), channel_id=1, source_target_pairs={{0,1},{1,0},{2,3},{3,2},{4,5},{5,4},{6,7},{7,6},{8,9},{9,8},{10,11... | collective-permute-start | bytes 786440 | tf_op jit(solution)/shard_map/ppermute | solution.py:44
  20.7 17.5 %collective-permute-start.8 = (bf16[128,1024]{1,0:T(8,128)(2,1)S(1)}, bf16[128,1024]{1,0:T(8,128)(2,1)S(1)}, u32[]{:S(2)}, u32[]{:S(2)}) collective-permute-start(bf16[128,1024]{1,0:T(8,128)(2,1)S(1)} %collective-permute-done.7.refs_3_.refs_4_), channel_id=1, source_target_pairs={{0,1},{1,0},{2,3},{3,2},{4,5},{5,4},{6,7},{7,6},{8,9},{9,8},{10,11... | collective-permute-start | bytes 786440 | tf_op jit(solution)/shard_map/ppermute | solution.py:44
  23.1 27.2 %collective-permute-start.5 = (bf16[64,1024]{1,0:T(8,128)(2,1)S(1)}, bf16[64,1024]{1,0:T(8,128)(2,1)S(1)}, u32[]{:S(2)}, u32[]{:S(2)}) collective-permute-start(bf16[64,1024]{1,0:T(8,128)(2,1)S(1)} %constant_dynamic-update-slice_fusion.refs_5_), channel_id=1, source_target_pairs={{0,1},{1,0},{2,3},{3,2},{4,5},{5,4},{6,7},{7,6},{8,9},{9,8},{10,11... | collective-permute-start | bytes 393224 | tf_op jit(solution)/shard_map/ppermute | solution.py:44
  23.2 1.2 %copy-start = (bf16[128,4096]{1,0:T(8,128)(2,1)S(1)}, bf16[128,4096]{1,0:T(8,128)(2,1)}, u32[]{:S(2)}) copy-start(bf16[128,4096]{1,0:T(8,128)(2,1)} %refs_2_.7) | copy-start | bytes 3145732
  24.4 0.9 %copy-start.2 = (bf16[128,1024]{1,0:T(8,128)(2,1)S(1)}, bf16[128,1024]{1,0:T(8,128)(2,1)}, u32[]{:S(2)}) copy-start(bf16[128,1024]{1,0:T(8,128)(2,1)} %refs_0_.9) | copy-start | bytes 786436
  25.3 0.7 %copy-start.4 = (s32[2,16]{1,0:T(2,128)S(1)}, s32[2,16]{1,0:T(2,128)}, u32[]{:S(2)}) copy-start(s32[2,16]{1,0:T(2,128)} %refs_0_.8) | copy-start | bytes 388
  26.0 0.7 %copy-start.5 = (s32[2]{0:T(128)S(1)}, s32[2]{0:T(128)}, u32[]{:S(2)}) copy-start(s32[2]{0:T(128)} %refs_1_.7) | copy-start | bytes 28
  30.1 8.1 %copy-start.6 = (s32[2,4]{1,0:T(2,128)S(1)}, s32[2,4]{1,0:T(2,128)}, u32[]{:S(2)}) copy-start(s32[2,4]{1,0:T(2,128)} %offset_ref.1) | copy-start | bytes 100
  38.2 3.9 %copy-start.1 = (bf16[128,4096]{1,0:T(8,128)(2,1)S(1)}, bf16[128,4096]{1,0:T(8,128)(2,1)}, u32[]{:S(2)}) copy-start(bf16[128,4096]{1,0:T(8,128)(2,1)} %refs_2_.7) | copy-start | bytes 3145732
  39.5 10.9 %copy-start.3 = (bf16[4,64,256]{2,1,0:T(8,128)(2,1)}, bf16[4,64,256]{2,1,0:T(8,128)(2,1)S(1)}, u32[]{:S(2)}) copy-start(bf16[4,64,256]{2,1,0:T(8,128)(2,1)S(1)} %get-tuple-element.26.own_ref) | copy-start | bytes 393220
  39.5 20.1 %collective-permute-start.11 = (bf16[4,64,256]{2,1,0:T(8,128)(2,1)S(1)}, bf16[4,64,256]{2,1,0:T(8,128)(2,1)S(1)}, u32[]{:S(2)}, u32[]{:S(2)}) collective-permute-start(bf16[4,64,256]{2,1,0:T(8,128)(2,1)S(1)} %get-tuple-element.27), channel_id=1, source_target_pairs={{0,8},{1,9},{2,10},{3,11},{4,12},{5,13},{6,14},{7,15},{8,0},{9,1},... | collective-permute-start | bytes 393224 | tf_op jit(solution)/shard_map/ppermute | solution.py:44
  59.6 0.6 %copy-start.7 = (bf16[4,64,256]{2,1,0:T(8,128)(2,1)}, bf16[4,64,256]{2,1,0:T(8,128)(2,1)S(1)}, u32[]{:S(2)}) copy-start(bf16[4,64,256]{2,1,0:T(8,128)(2,1)S(1)} %collective-permute-done.11.other_ref) | copy-start | bytes 393220

commit v2 on v1

v2 whole, which is shorter than its diff:
```python
import functools

import jax
import jax.numpy as jnp
from jax import lax
from jax.experimental import pallas as pl
from jax.experimental.pallas import tpu as pltpu
from jax.sharding import PartitionSpec as P

HD = 128
QH = 32
KVH = 4
REQS = 2
PAGE = 8
SLOTS = 32
GQ = QH // KVH

LOG2E = 1.4426950408889634
OUT_OF_REACH = -1e30
CHUNK = 512
VMEM_BYTES = 16 * 1024 * 1024
SAFE_MASS = 1e36
CONTRACT_LAST = (((1,), (1,)), ((), ()))

IN_VMEM = pl.BlockSpec(memory_space=pltpu.VMEM)
IN_SMEM = pl.BlockSpec(memory_space=pltpu.SMEM)
ANYWHERE = pl.BlockSpec(memory_space=pl.ANY)


def hop_bits(devices):
    bits = []
    bit = 2
    while bit < devices // REQS:
        bits.append(bit)
        bit *= 2
    return (tuple(bits), tuple(reversed(bits)))


def pick(core, pair):
    return jnp.where(core == 0, pair[0], pair[1])


def swap(value, bit):
    route = [(i, i ^ bit) for i in range(lax.axis_size("seq"))]
    return lax.ppermute(value, "seq", route)


def swap_by_core(value, orders, step):
    route = [(i, i ^ orders[i % 2][step]) for i in range(lax.axis_size("seq"))]
    return lax.ppermute(value, "seq", route)


def swap_wide(value, orders, bit):
    route = [(i, i ^ bit ^ orders[i % 2][0]) for i in range(lax.axis_size("seq"))]
    return lax.ppermute(value, "seq", route)


def after(value, *earlier):
    return lax.optimization_barrier((value,) + earlier)[0]


def page_kernel(devices, table_ref, store_ref, own_ref, other_ref, sems):
    me = lax.axis_index("seq")
    request = me // (devices // REQS)
    copies = []
    for n, (req, page_ref) in enumerate(((1 - request, other_ref), (request, own_ref))):
        slot = jnp.int32(0)
        for j in range(table_ref.shape[1]):
            away = table_ref[req, j] - me * SLOTS
            slot = jnp.where((away >= 0) & (away < SLOTS), away, slot)
        copy = pltpu.make_async_copy(store_ref.at[slot], page_ref, sems.at[n])
        copy.start()
        copies.append(copy)
    for copy in copies:
        copy.wait()


def fetch_pages(page_table, kv_store, devices):
    page = jax.ShapeDtypeStruct(kv_store.shape[1:], kv_store.dtype)
    return pl.pallas_call(
        functools.partial(page_kernel, devices),
        out_shape=(page, page),
        in_specs=[IN_SMEM, ANYWHERE],
        out_specs=(IN_VMEM, IN_VMEM),
        scratch_shapes=[pltpu.SemaphoreType.DMA((2,))],
        name="fetch_pages",
    )(page_table, kv_store)


def source_of(me, swapped, path, orders):
    at = me ^ 1 if swapped else me
    core = at % 2
    for step in path:
        at = at ^ pick(core, (orders[0][step], orders[1][step]))
    return at


def page_bias(me, devices, orders, table_ref, hit_ref, swapped, path, place):
    base = source_of(me, swapped, path, orders)
    hop = pick(base % 2, (orders[0][0], orders[1][0]))
    slot = place // PAGE
    at = jnp.where(slot >= 2, base ^ hop, base)
    at = jnp.where(slot % 2 == 1, at ^ (devices // REQS), at)
    request = me // (devices // REQS)
    page = jnp.zeros_like(place)
    for j in range(table_ref.shape[1]):
        page = jnp.where(at == table_ref[request, j] // SLOTS, j, page)
    return jnp.where(page * PAGE + place % PAGE < hit_ref[request], 0.0, OUT_OF_REACH)


def key_bias(me, devices, orders, table_ref, hit_ref, kind, shape, dim):
    if kind[0] == "own":
        return jnp.zeros(shape, jnp.float32)
    if kind[0] == "block":
        source = source_of(me, kind[1], kind[2], orders)
        return jnp.full(shape, jnp.where(source < me, 0.0, OUT_OF_REACH), jnp.float32)
    place = lax.broadcasted_iota(jnp.int32, shape, dim)
    return page_bias(me, devices, orders, table_ref, hit_ref, kind[1], kind[2], place)


def stack(refs, at):
    return jnp.concatenate([ref[:, at : at + HD] for ref in refs], axis=0)


def head_rows(q_ref, g):
    heads = range(g * GQ, (g + 1) * GQ)
    return jnp.concatenate([q_ref[:, h * HD : (h + 1) * HD] for h in heads], axis=0)


def with_ones(values):
    return jnp.concatenate([values, jnp.ones_like(values)], axis=1)


def shift_lanes(shift):
    lane = lax.broadcasted_iota(jnp.int32, shift.shape, 1)
    return jnp.where(lane == 0, -shift, jnp.where(lane == 1, 1.0, 0.0)).astype(jnp.bfloat16)


def bias_lanes(bias):
    lane = lax.broadcasted_iota(jnp.int32, bias.shape, 1)
    return jnp.where(lane == 0, 1.0, jnp.where(lane == 1, bias, 0.0)).astype(jnp.bfloat16)


def causal_bias(rows):
    t = lax.broadcasted_iota(jnp.int32, (rows, rows), 0)
    k = lax.broadcasted_iota(jnp.int32, (rows, rows), 1)
    return jnp.where(k <= t, 0.0, OUT_OF_REACH)


SCALE = HD**-0.5 * LOG2E


def first_kernel(orders, q_ref, own_ref, mate_ref, mass_ref, shift_ref):
    me = lax.axis_index("seq")
    rows = q_ref.shape[0]
    mate_bias = jnp.where(me % 2 == 1, 0.0, OUT_OF_REACH)
    bias = jnp.concatenate([causal_bias(rows), jnp.full((rows, rows), mate_bias, jnp.float32)], axis=1)
    refs = (own_ref, mate_ref)
    for g in range(KVH):
        at = g * 2 * HD
        scores = lax.dot_general(head_rows(q_ref, g), stack(refs, at), CONTRACT_LAST, preferred_element_type=jnp.float32)
        scores = (scores.reshape(GQ, rows, -1) + bias[None]).reshape(GQ * rows, -1)
        peak = jnp.max(scores, axis=1, keepdims=True)
        shift = jnp.broadcast_to(peak, (GQ * rows, HD)).astype(jnp.bfloat16).astype(jnp.float32)
        weights = jnp.exp2((scores - jnp.concatenate([shift, shift], axis=1)) * SCALE).astype(jnp.bfloat16)
        span = pl.ds(g * GQ * rows, GQ * rows)
        mass_ref[span, :] = jnp.dot(weights, with_ones(stack(refs, at + HD)), preferred_element_type=jnp.float32)
        shift_ref[span, :] = shift_lanes(shift)


def attend_first(orders, queries, own, mate):
    rows = queries.shape[0]
    return pl.pallas_call(
        functools.partial(first_kernel, orders),
        out_shape=(
            jax.ShapeDtypeStruct((QH * rows, 2 * HD), jnp.float32),
            jax.ShapeDtypeStruct((QH * rows, HD), jnp.bfloat16),
        ),
        in_specs=[IN_VMEM] * 3,
        out_specs=(IN_VMEM, IN_VMEM),
        compiler_params=pltpu.CompilerParams(vmem_limit_bytes=VMEM_BYTES),
        cost_estimate=pl.CostEstimate(
            flops=16 * rows * QH * rows * HD, bytes_accessed=4 * rows * QH * HD, transcendentals=2 * rows * QH * rows
        ),
        name="attend_first",
    )(queries, own, mate)


def more_kernel(devices, orders, kinds, extra_kinds, *refs):
    refs = list(refs)
    table_ref, hit_ref, q_ref, shift_ref, mass_ref = refs[:5]
    key_refs = refs[5 : 5 + len(kinds)]
    if extra_kinds is None:
        out_ref = refs[-1]
    else:
        out_ref, wrong_ref, top_ref, denominator_ref, total_ref, block_ref, sem = refs[-7:]
    me = lax.axis_index("seq")
    rows = q_ref.shape[0]
    span_rows = GQ * rows

    def bias_of(kind, ref):
        shape = (ref.shape[0], HD)
        return bias_lanes(key_bias(me, devices, orders, table_ref, hit_ref, kind, shape, 0))

    def add_up(q_wide, group, bias, at):
        keys = jnp.concatenate([stack(group, at), bias], axis=1)
        scores = lax.dot_general(q_wide, keys, CONTRACT_LAST, preferred_element_type=jnp.float32)
        weights = jnp.exp2(scores * SCALE).astype(jnp.bfloat16)
        return jnp.dot(weights, with_ones(stack(group, at + HD)), preferred_element_type=jnp.float32)

    bias = jnp.concatenate([bias_of(kind, ref) for kind, ref in zip(kinds, key_refs)], axis=0)
    if extra_kinds is not None:
        wrong_ref[...] = jnp.zeros_like(wrong_ref)
    for g in range(KVH):
        span = pl.ds(g * span_rows, span_rows)
        q_wide = jnp.concatenate([head_rows(q_ref, g), shift_ref[span, :]], axis=1)
        mass = mass_ref[span, :] + add_up(q_wide, key_refs, bias, g * 2 * HD)
        if extra_kinds is None:
            out_ref[span, :] = mass
            continue
        total, denominator = mass[:, :HD], mass[:, HD:]
        good = jnp.where(denominator < SAFE_MASS, 0.0, 1.0)
        wrong_ref[...] = jnp.maximum(wrong_ref[...], jnp.max(good.reshape(-1, 8, HD), axis=0))
        attended = (total / denominator).astype(out_ref.dtype)
        for n in range(GQ):
            h = g * GQ + n
            out_ref[:, h * HD : (h + 1) * HD] = attended[n * rows : (n + 1) * rows]
    if extra_kinds is None:
        return

    @pl.when(jnp.max(wrong_ref[...]) > 0.0)
    def _():
        top_ref[...] = jnp.full_like(top_ref, OUT_OF_REACH)
        denominator_ref[...] = jnp.zeros_like(denominator_ref)
        total_ref[...] = jnp.zeros_like(total_ref)

        def take(kind, ref):
            bias = key_bias(me, devices, orders, table_ref, hit_ref, kind, (1, ref.shape[0]), 1)
            if kind[0] == "own":
                bias = causal_bias(rows)

            def one_head(h, carried):
                column = pl.ds(pl.multiple_of(h * HD, HD), HD)
                at = pl.multiple_of(h // GQ * 2 * HD, 2 * HD)
                span = pl.ds(pl.multiple_of(h * rows, rows), rows)
                scores = lax.dot_general(
                    q_ref[:, column], ref[:, pl.ds(at, HD)], CONTRACT_LAST, preferred_element_type=jnp.float32
                )
                scores = scores + bias
                top = top_ref[span, :]
                new_top = jnp.maximum(top, jnp.max(scores, axis=1, keepdims=True))
                weights = jnp.exp2((scores - new_top[:, : scores.shape[1]]) * SCALE)
                factor = jnp.exp2((top - new_top) * SCALE)
                top_ref[span, :] = new_top
                denominator_ref[span, :] = denominator_ref[span, :] * factor + jnp.sum(weights, axis=1, keepdims=True)
                total_ref[span, :] = total_ref[span, :] * factor + jnp.dot(
                    weights.astype(jnp.bfloat16), ref[:, pl.ds(at + HD, HD)], preferred_element_type=jnp.float32
                )
                return carried

            lax.fori_loop(0, QH, one_head, 0)

        for kind, ref in zip(extra_kinds, refs[5 + len(kinds) :]):
            copy = pltpu.make_async_copy(ref, block_ref, sem)
            copy.start()
            copy.wait()
            take(kind, block_ref)
        for kind, ref in zip(kinds, key_refs):
            take(kind, ref)

        def write(h, carried):
            span = pl.ds(pl.multiple_of(h * rows, rows), rows)
            attended = total_ref[span, :] / denominator_ref[span, :]
            out_ref[:, pl.ds(pl.multiple_of(h * HD, HD), HD)] = attended.astype(out_ref.dtype)
            return carried

        lax.fori_loop(0, QH, write, 0)


def attend_more(devices, orders, page_table, hit_tokens, queries, shift, mass, batch, extra):
    rows = queries.shape[0]
    keys = sum(value.shape[0] for _, value in batch)
    last = extra is not None
    if last:
        out_shape = jax.ShapeDtypeStruct((rows, QH * HD), queries.dtype)
    else:
        out_shape = jax.ShapeDtypeStruct(mass.shape, mass.dtype)
    arrays = [value for _, value in batch] + [value for _, value in extra or ()]
    scratch = [
        pltpu.VMEM((8, HD), jnp.float32),
        *[pltpu.VMEM((QH * rows, HD), jnp.float32)] * 3,
        pltpu.VMEM((rows, 2 * KVH * HD), jnp.bfloat16),
        pltpu.SemaphoreType.DMA,
    ]
    return pl.pallas_call(
        functools.partial(
            more_kernel,
            devices,
            orders,
            tuple(kind for kind, _ in batch),
            tuple(kind for kind, _ in extra) if last else None,
        ),
        out_shape=out_shape,
        in_specs=[IN_SMEM, IN_SMEM] + [IN_VMEM] * (3 + len(batch)) + [ANYWHERE] * (len(arrays) - len(batch)),
        out_specs=IN_VMEM,
        scratch_shapes=scratch if last else [],
        input_output_aliases={} if last else {4: 0},
        compiler_params=pltpu.CompilerParams(vmem_limit_bytes=VMEM_BYTES),
        cost_estimate=pl.CostEstimate(
            flops=8 * rows * QH * keys * HD, bytes_accessed=4 * rows * QH * HD, transcendentals=rows * QH * keys
        ),
        name="attend_last" if last else "attend_more",
    )(page_table, hit_tokens, queries, shift, mass, *arrays)


def owner_kernel(devices, orders, kinds, hops, offset_ref, *refs):
    key_refs = refs[: len(kinds)]
    own_ref, other_ref = refs[len(kinds) :]
    me = lax.axis_index("seq")
    group_size = devices // REQS
    request = me // group_size
    rows = key_refs[0].shape[0]
    each = rows // devices
    kept = own_ref.shape[1]
    lane = lax.broadcasted_iota(jnp.int32, (1, rows), 1)
    row = lax.broadcasted_iota(jnp.int32, (2 * kept, rows), 0)
    wanted_row = jnp.where(row >= kept, row - kept, row)
    residue, landing = lane % devices, lane // devices
    bases = []
    for kind in kinds:
        source = me if kind[0] == "own" else source_of(me, kind[1], kind[2], orders)
        place = source % group_size
        if hops[0] is not None:
            place = source % 2
            for n, hop in enumerate(hops):
                place = place + jnp.where((source ^ me) // 2 == hop // 2, 2 * n, 0)
        bases.append(place * each)
    for g in range(KVH):
        turn = (me - offset_ref[request, g] + devices) % devices
        mine = jnp.where(residue == turn, landing, -kept - rows)
        others = jnp.where(residue == turn ^ (devices // REQS), landing, -kept - rows)
        wanted = jnp.where(row >= kept, others, mine)
        total = jnp.zeros((2 * kept, 2 * HD), jnp.float32)
        for ref, base in zip(key_refs, bases):
            chosen = wanted_row == wanted + base
            total = total + jnp.dot(
                jnp.where(chosen, 1.0, 0.0).astype(jnp.bfloat16),
                ref[:, g * 2 * HD : (g + 1) * 2 * HD],
                preferred_element_type=jnp.float32,
            )
        own_ref[g] = total[:kept].astype(own_ref.dtype)
        other_ref[g] = total[kept:].astype(other_ref.dtype)


def pick_for_owners(devices, orders, owner_offset, batch, hops):
    rows, _ = batch[0][1].shape
    kept = len(batch) * rows // devices
    piece = jax.ShapeDtypeStruct((KVH, kept, 2 * HD), batch[0][1].dtype)
    return pl.pallas_call(
        functools.partial(owner_kernel, devices, orders, tuple(kind for kind, _ in batch), hops),
        out_shape=(piece, piece),
        in_specs=[IN_SMEM] + [IN_VMEM] * len(batch),
        out_specs=(IN_VMEM, IN_VMEM),
        compiler_params=pltpu.CompilerParams(vmem_limit_bytes=VMEM_BYTES),
        name="pick_for_owners",
    )(owner_offset, *[value for _, value in batch])


def place_kernel(devices, spans, size, *refs):
    me = lax.axis_index("seq")
    group_size = devices // REQS
    request = me // group_size
    chip = (me % group_size) // 2
    kept = size // REQS
    out_ref = refs[-1]
    for n, hops in enumerate(spans):
        for side, req in enumerate((request, 1 - request)):
            ref = refs[2 * n + side]
            height = ref.shape[1] // len(hops)
            for k, hop in enumerate(hops):
                start = req * kept
                if hop is not None:
                    start = start + (chip ^ (hop // 2)) * height
                rows = pl.ds(pl.multiple_of(start, height), height)
                out_ref[0, :, rows] = ref[:, k * height : (k + 1) * height]


def place(devices, pieces, spans, size):
    flat = [array for pair in pieces for array in pair]
    heads, _, width = flat[0].shape
    return pl.pallas_call(
        functools.partial(place_kernel, devices, tuple(spans), size),
        out_shape=jax.ShapeDtypeStruct((1, heads, size, width), flat[0].dtype),
        in_specs=[IN_VMEM] * len(flat),
        out_specs=IN_VMEM,
        name="place",
    )(*flat)


def shards(queries, suffix_kv, kv_store, page_table, hit_tokens, owner_offset):
    devices = lax.axis_size("seq")
    orders = hop_bits(devices)
    steps = len(orders[0])
    partner = devices // REQS
    rows = suffix_kv.shape[0]

    held = [((), suffix_kv)]
    first_hop = swap_by_core(suffix_kv, orders, 0)
    own_page, other_page = fetch_pages(page_table, kv_store, devices)
    mate = swap(suffix_kv, 1)
    page_set = [
        own_page,
        swap(other_page, partner),
        swap_by_core(own_page, orders, 0),
        swap_wide(other_page, orders, partner),
    ]
    mass, shift = attend_first(orders, queries, suffix_kv, mate)
    quad = jnp.concatenate(page_set, axis=0)
    pages = [((), quad)]
    held.append(((0,), after(first_hop, shift)))
    for step in range(1, steps):
        held = held + [(path + (step,), swap_by_core(value, orders, step)) for path, value in held]
        pages = pages + [(path + (step,), swap_by_core(value, orders, step)) for path, value in pages]

    own_kind, mate_kind = ("own",), ("block", True, ())
    arrivals = []
    for path, value in held[1:]:
        arrivals.append([(("block", False, path), value), (("block", True, path), swap(value, 1))])
    page_arrivals = []
    for path, value in pages:
        page_arrivals += [(("pages", False, path), value), (("pages", True, path), swap(value, 1))]
    home = [(own_kind, suffix_kv), (mate_kind, mate)]

    each = 2 * rows // devices
    if steps == 2 and each % 16 == 0:
        x, z = orders[0]
        batches = [(home + arrivals[0] + arrivals[1], (0, x, z)), (arrivals[2], (x ^ z,))]
    else:
        batches = [(home + sum(arrivals, []), (None,))]
    pieces, spans = [], []
    for batch, hops in batches:
        mine, theirs = pick_for_owners(devices, orders, owner_offset, batch, hops)
        pieces.append((mine, swap(theirs, partner)))
        spans.append(hops)

    more = functools.partial(attend_more, devices, orders, page_table, hit_tokens, queries, shift)
    for n in range(0, len(arrivals) - 1, 2):
        mass = more(mass, sum(arrivals[n : min(n + 2, len(arrivals) - 1)], []), None)
    attention_out = more(mass, arrivals[-1] + page_arrivals, home + sum(arrivals[:-1], []))
    return (attention_out, place(devices, pieces, spans, REQS * partner * rows // devices))


def solution(mesh):
    in_specs = (
        P(("groups", "seq"), None),
        P(("groups", "seq"), None),
        P(("groups", "seq"), None, None),
        P("groups", None),
        P("groups"),
        P("groups", None),
    )
    out_specs = (P(("groups", "seq"), None), P(("groups", "seq"), None, None, None))
    return jax.shard_map(shards, mesh=mesh, in_specs=in_specs, out_specs=out_specs, check_vma=False)
```

time: 62.4 us -> 39.2 us (0.63)
  Pallas kernels: 34.8 us -> 14.6 us
  waiting for transfers between devices: 7.56 us -> 4.39 us
  starting transfers between devices: 12.5 us -> 15.3 us
  other arithmetic: 1.44 us -> 0 us
  local copies, waits for them, and re-layouts: 4.88 us -> 3.56 us
    pallas_call x6, Pallas kernels: 31.9 us -> 12.5 us  [the longest x2 7.61 us: attend_more(): pl.pallas_call(functools.partial(more_kernel, devices, orders, tuple((kin...]
    ppermute x5, waiting for transfers between devices: 5.94 us -> 3.93 us  [swap_by_core(): return lax.ppermute(value, 'seq', route)]
    ppermute x7 -> x9, starting transfers between devices: 5.78 us -> 7.24 us  [swap(): return lax.ppermute(value, 'seq', route)]
    concatenate x2 -> x0, other arithmetic: 1.44 us -> none  [the longest x1 0.72 us: shards(): pages = jnp.concatenate([pages, swap_by_core(pages, orders, step)], axis=0)]
    unnamed x19 -> x23, local copies, waits for them, and re-layouts: 4.88 us -> 3.56 us
    ppermute x0 -> x1, starting transfers between devices: none -> 1.26 us  [swap_wide(): return lax.ppermute(value, 'seq', route)]
    ppermute x7 -> x9, waiting for transfers between devices: 1.62 us -> 0.45 us  [swap(): return lax.ppermute(value, 'seq', route)]
    pallas_call x1, Pallas kernels: 2.91 us -> 2.11 us  [fetch_pages(): pl.pallas_call(functools.partial(page_kernel, devices), out_shape=(page,...]
  transfers between devices with their start and end apart: 12 -> 15, of which waited for: 4 -> 3; matrix products, arithmetic and copies ran while one was open for 4% -> 2% of each run, Pallas kernels for 54% -> 33%
where the time goes in v2:
time: 39.2 us; the launch traced here: 38.7 us
  starting transfers between devices  15.3 us (39%)
  Pallas kernels  14.6 us (37%)
  waiting for transfers between devices  4.39 us (11%)
  local copies, waits for them, and re-layouts  3.56 us (9%)
  between operations  0.81 us (2%)
    pallas_call x2, Pallas kernels, attend_more(): pl.pallas_call(functools.partial(more_kernel, devices, orders, tuple((kin...  7.61 us
    ppermute x9, starting transfers between devices, swap(): return lax.ppermute(value, 'seq', route)  7.24 us
    ppermute x5, starting transfers between devices, swap_by_core(): return lax.ppermute(value, 'seq', route)  6.83 us
    ppermute x5, waiting for transfers between devices, swap_by_core(): return lax.ppermute(value, 'seq', route)  3.93 us
    unnamed x23, local copies, waits for them, and re-layouts  3.56 us
    pallas_call x1, Pallas kernels, fetch_pages(): pl.pallas_call(functools.partial(page_kernel, devices), out_shape=(page,...  2.11 us
    pallas_call x2, Pallas kernels, pick_for_owners(): pl.pallas_call(functools.partial(owner_kernel, devices, orders, tuple((ki...  1.78 us
    pallas_call x1, Pallas kernels, place(): pl.pallas_call(functools.partial(place_kernel, devices, tuple(spans), siz...  1.68 us
  transfers between devices with their start and end apart: 15, of which 3 were waited for; matrix products, arithmetic and copies ran while one was open for 2% of the time, Pallas kernels for 33%

profile of v2, /device:TPU:0, one launch (start us, length us, event | category | flops | bytes accessed | tf_op | source)
XLA Modules:
  0.0 38.7 jit_solution(11291721431622590295)
XLA Ops:
  0.6 0.0 copy-start.5
  0.6 0.0 copy-start.6
  0.7 0.0 copy-start.7
  0.7 0.5 %collective-permute-start = (bf16[128,1024]{1,0:T(8,128)(2,1)}, bf16[128,1024]{1,0:T(8,128)(2,1)S(1)}, u32[]{:S(2)}, u32[]{:S(2)}) collective-permute-start(bf16[128,1024]{1,0:T(8,128)(2,1)} %refs_0_.5), channel_id=1, source_target_pairs={{0,1},{1,0},{2,3},{3,2},{4,5},{5,4},{6,7},{7,6},{8,9},{9,8},{10,11... | collective-permute-start | bytes 786440 | tf_op jit(solution)/shard_map/ppermute | solution.py:45
  1.2 2.6 %collective-permute-start.1 = (bf16[128,1024]{1,0:T(8,128)(2,1)}, bf16[128,1024]{1,0:T(8,128)(2,1)S(1)}, u32[]{:S(2)}, u32[]{:S(2)}) collective-permute-start(bf16[128,1024]{1,0:T(8,128)(2,1)} %refs_0_.5), channel_id=1, source_target_pairs={{0,2},{1,5},{2,0},{3,7},{4,6},{5,1},{6,4},{7,3},{8,10},{9,13},{10,... | collective-permute-start | bytes 786440 | tf_op jit(solution)/shard_map/ppermute | solution.py:50
  3.7 1.6 %collective-permute-start.3 = (bf16[128,1024]{1,0:T(8,128)(2,1)}, bf16[128,1024]{1,0:T(8,128)(2,1)S(1)}, u32[]{:S(2)}, u32[]{:S(2)}) collective-permute-start(bf16[128,1024]{1,0:T(8,128)(2,1)} %refs_0_.5), channel_id=1, source_target_pairs={{0,4},{1,3},{2,6},{3,1},{4,0},{5,7},{6,2},{7,5},{8,12},{9,11},{10,... | collective-permute-start | bytes 786440 | tf_op jit(solution)/shard_map/ppermute | solution.py:50
  5.3 2.1 %fetch_pages.1 = (bf16[8,1024]{1,0:T(8,128)(2,1)}, bf16[8,1024]{1,0:T(8,128)(2,1)}) custom-call(s32[2,16]{1,0:T(2,128)} %refs_0_.4, bf16[32,8,1024]{2,1,0:T(8,128)(2,1)} %store_ref.1), custom_call_target="tpu_custom_call" | custom-call | tf_op jit(solution)/shard_map/fetch_pages/pallas_call | solution.py:80
  7.4 2.7 %collective-permute-start.7 = (bf16[8,1024]{1,0:T(8,128)(2,1)}, bf16[8,1024]{1,0:T(8,128)(2,1)S(1)}, u32[]{:S(2)}, u32[]{:S(2)}) collective-permute-start(bf16[8,1024]{1,0:T(8,128)(2,1)} %get-tuple-element.15), channel_id=1, source_target_pairs={{0,8},{1,9},{2,10},{3,11},{4,12},{5,13},{6,14},{7,15},{8,0},{9,1},... | collective-permute-start | bytes 49160 | tf_op jit(solution)/shard_map/ppermute | solution.py:45
  10.1 0.5 %collective-permute-start.8 = (bf16[8,1024]{1,0:T(8,128)(2,1)}, bf16[8,1024]{1,0:T(8,128)(2,1)S(1)}, u32[]{:S(2)}, u32[]{:S(2)}) collective-permute-start(bf16[8,1024]{1,0:T(8,128)(2,1)} %get-tuple-element.14), channel_id=1, source_target_pairs={{0,2},{1,5},{2,0},{3,7},{4,6},{5,1},{6,4},{7,3},{8,10},{9,13},{10,... | collective-permute-start | bytes 49160 | tf_op jit(solution)/shard_map/ppermute | solution.py:50
  10.6 0.8 %constant_dynamic-update-slice_fusion.3 = bf16[32,1024]{1,0:T(8,128)(2,1)S(1)} fusion(bf16[8,1024]{1,0:T(8,128)(2,1)} %get-tuple-element.14), kind=kLoop, calls=%fused_computation.3 | loop fusion | bytes 32768
  11.4 0.0 collective-permute-done.mate_ref.refs_12_.refs_1_
  11.4 1.3 %collective-permute-start.9 = (bf16[8,1024]{1,0:T(8,128)(2,1)}, bf16[8,1024]{1,0:T(8,128)(2,1)S(1)}, u32[]{:S(2)}, u32[]{:S(2)}) collective-permute-start(bf16[8,1024]{1,0:T(8,128)(2,1)} %get-tuple-element.15), channel_id=1, source_target_pairs={{0,10},{1,13},{2,8},{3,15},{4,14},{5,9},{6,12},{7,11},{8,2},{9,5},... | collective-permute-start | bytes 49160 | tf_op jit(solution)/shard_map/ppermute | solution.py:55
  12.7 1.2 %copy-done = bf16[128,4096]{1,0:T(8,128)(2,1)S(1)} copy-done((bf16[128,4096]{1,0:T(8,128)(2,1)S(1)}, bf16[128,4096]{1,0:T(8,128)(2,1)}, u32[]{:S(2)}) %copy-start) | copy-done | bytes 1048600
  13.9 0.9 %copy-done.2 = bf16[128,1024]{1,0:T(8,128)(2,1)S(1)} copy-done((bf16[128,1024]{1,0:T(8,128)(2,1)S(1)}, bf16[128,1024]{1,0:T(8,128)(2,1)}, u32[]{:S(2)}) %copy-start.2) | copy-done | bytes 262168
  14.8 1.5 %attend_first.1 = (f32[4096,256]{1,0:T(8,128)S(1)}, bf16[4096,128]{1,0:T(8,128)(2,1)S(1)}) custom-call(bf16[128,4096]{1,0:T(8,128)(2,1)S(1)} %copy-done, bf16[128,1024]{1,0:T(8,128)(2,1)S(1)} %copy-done.2, bf16[128,1024]{1,0:T(8,128)(2,1)S(1)} %collective-permute-done.mate_ref.refs_12_.refs_1_), custom_call_target="tpu_custom_call" | custom-call | flops 1073741824 | bytes 2097152 | tf_op jit(solution)/shard_map/attend_first/pallas_call | solution.py:173
  16.3 0.0 collective-permute-done.1.refs_5_.refs_13_.refs_2_
  16.3 0.5 %collective-permute-start.5 = (bf16[128,1024]{1,0:T(8,128)(2,1)S(1)}, bf16[128,1024]{1,0:T(8,128)(2,1)S(1)}, u32[]{:S(2)}, u32[]{:S(2)}) collective-permute-start(bf16[128,1024]{1,0:T(8,128)(2,1)S(1)} %collective-permute-done.1.refs_5_.refs_13_.refs_2_), channel_id=1, source_target_pairs={{0,4},{1,3},{2,6},{3,1},{4,0},{5,7},{6,2},{7,5},{8,12},{9,11},{10,... | collective-permute-start | bytes 786440 | tf_op jit(solution)/shard_map/ppermute | solution.py:50
  16.8 0.0 collective-permute-done.7
  16.8 0.0 collective-permute-start.2
  16.8 0.0 collective-permute-done.3.refs_7_.refs_15_.refs_4_
  16.8 0.5 %collective-permute-start.4 = (bf16[128,1024]{1,0:T(8,128)(2,1)S(1)}, bf16[128,1024]{1,0:T(8,128)(2,1)S(1)}, u32[]{:S(2)}, u32[]{:S(2)}) collective-permute-start(bf16[128,1024]{1,0:T(8,128)(2,1)S(1)} %collective-permute-done.3.refs_7_.refs_15_.refs_4_), channel_id=1, source_target_pairs={{0,1},{1,0},{2,3},{3,2},{4,5},{5,4},{6,7},{7,6},{8,9},{9,8},{10,11... | collective-permute-start | bytes 786440 | tf_op jit(solution)/shard_map/ppermute | solution.py:45
  17.3 0.0 collective-permute-done.8
  17.3 0.0 collective-permute-done.9
  17.4 1.6 %collective-permute-start.11 = (bf16[32,1024]{1,0:T(8,128)(2,1)S(1)}, bf16[32,1024]{1,0:T(8,128)(2,1)S(1)}, u32[]{:S(2)}, u32[]{:S(2)}) collective-permute-start(bf16[32,1024]{1,0:T(8,128)(2,1)S(1)} %constant_dynamic-update-slice_fusion.refs_7_), channel_id=1, source_target_pairs={{0,4},{1,3},{2,6},{3,1},{4,0},{5,7},{6,2},{7,5},{8,12},{9,11},{10,... | collective-permute-start | bytes 196616 | tf_op jit(solution)/shard_map/ppermute | solution.py:50
  19.0 3.7 %collective-permute-done.5.refs_5_.refs_0_ = bf16[128,1024]{1,0:T(8,128)(2,1)S(1)} collective-permute-done((bf16[128,1024]{1,0:T(8,128)(2,1)S(1)}, bf16[128,1024]{1,0:T(8,128)(2,1)S(1)}, u32[]{:S(2)}, u32[]{:S(2)}) %collective-permute-start.5) | collective-permute-done | bytes 262176 | tf_op jit(solution)/shard_map/ppermute | solution.py:50
  22.7 0.0 collective-permute-start.6
  22.7 0.5 %collective-permute-start.10 = (bf16[32,1024]{1,0:T(8,128)(2,1)S(1)}, bf16[32,1024]{1,0:T(8,128)(2,1)S(1)}, u32[]{:S(2)}, u32[]{:S(2)}) collective-permute-start(bf16[32,1024]{1,0:T(8,128)(2,1)S(1)} %constant_dynamic-update-slice_fusion.refs_7_), channel_id=1, source_target_pairs={{0,1},{1,0},{2,3},{3,2},{4,5},{5,4},{6,7},{7,6},{8,9},{9,8},{10,11... | collective-permute-start | bytes 196616 | tf_op jit(solution)/shard_map/ppermute | solution.py:45
  23.2 0.2 collective-permute-done.11.refs_9_
  23.4 0.0 collective-permute-start.12
  23.4 0.0 collective-permute-done.2.refs_6_.refs_14_.refs_3_
  23.4 0.0 collective-permute-done.4.refs_8_.refs_16_.refs_5_
  23.4 0.0 copy-done.6
  23.5 1.0 %pick_for_owners.2 = (bf16[4,48,256]{2,1,0:T(8,128)(2,1)S(1)}, bf16[4,48,256]{2,1,0:T(8,128)(2,1)S(1)}) custom-call(s32[2,4]{1,0:T(2,128)S(1)} %copy-done.6, bf16[128,1024]{1,0:T(8,128)(2,1)S(1)} %copy-done.2, bf16[128,1024]{1,0:T(8,128)(2,1)S(1)} %collective-permute-done.mate_ref.refs_12_.refs_1_, ...), custom_call_target="tpu_custom_call" | custom-call | tf_op jit(solution)/shard_map/pick_for_owners/pallas_call | solution.py:359
  24.5 0.0 copy-start.3
  24.5 2.7 %collective-permute-start.13 = (bf16[4,48,256]{2,1,0:T(8,128)(2,1)S(1)}, bf16[4,48,256]{2,1,0:T(8,128)(2,1)S(1)}, u32[]{:S(2)}, u32[]{:S(2)}) collective-permute-start(bf16[4,48,256]{2,1,0:T(8,128)(2,1)S(1)} %get-tuple-element.17), channel_id=1, source_target_pairs={{0,8},{1,9},{2,10},{3,11},{4,12},{5,13},{6,14},{7,15},{8,0},{9,1},... | collective-permute-start | bytes 294920 | tf_op jit(solution)/shard_map/ppermute | solution.py:45
  27.2 0.0 copy-done.5
  27.2 3.4 %attend_more.1.refs_4_ = f32[4096,256]{1,0:T(8,128)S(1)} custom-call(s32[2,16]{1,0:T(2,128)S(1)} %copy-done.5, s32[2]{0:T(128)S(1)} %copy-done.7, bf16[128,4096]{1,0:T(8,128)(2,1)S(1)} %copy-done.1, bf16[4096,128]{1,0:T(8,128)(2,1)S(1)} %get-tuple-element.11.refs_3_, f32[4096,256]{1,0:T(8,128)S(1)} %get-tuple-element.12.refs_4_, ...), custom_call_target="tpu_custom_call", output_to_operand_aliasing={{}: (4, {})} | custom-call | flops 2147483648 | bytes 2097152 | tf_op jit(solution)/shard_map/attend_more/pallas_call | solution.py:295
  30.6 0.0 collective-permute-done.6.refs_6_.refs_1_
  30.6 0.8 %pick_for_owners.3 = (bf16[4,16,256]{2,1,0:T(8,128)(2,1)S(1)}, bf16[4,16,256]{2,1,0:T(8,128)(2,1)S(1)}) custom-call(s32[2,4]{1,0:T(2,128)S(1)} %copy-done.6, bf16[128,1024]{1,0:T(8,128)(2,1)S(1)} %collective-permute-done.5.refs_5_.refs_0_, bf16[128,1024]{1,0:T(8,128)(2,1)S(1)} %collective-permute-done.6.refs_6_.refs_1_), custom_call_target="tpu_custom_call" | custom-call | tf_op jit(solution)/shard_map/pick_for_owners/pallas_call | solution.py:359
  31.3 0.4 %collective-permute-start.14 = (bf16[4,16,256]{2,1,0:T(8,128)(2,1)S(1)}, bf16[4,16,256]{2,1,0:T(8,128)(2,1)S(1)}, u32[]{:S(2)}, u32[]{:S(2)}) collective-permute-start(bf16[4,16,256]{2,1,0:T(8,128)(2,1)S(1)} %get-tuple-element.19), channel_id=1, source_target_pairs={{0,8},{1,9},{2,10},{3,11},{4,12},{5,13},{6,14},{7,15},{8,0},{9,1},... | collective-permute-start | bytes 98312 | tf_op jit(solution)/shard_map/ppermute | solution.py:45
  31.7 0.0 collective-permute-done.10.refs_8_
  31.7 0.0 collective-permute-done.12.refs_10_
  31.7 4.2 %attend_last.1 = bf16[128,4096]{1,0:T(8,128)(2,1)} custom-call(s32[2,16]{1,0:T(2,128)S(1)} %copy-done.5, s32[2]{0:T(128)S(1)} %copy-done.7, bf16[128,4096]{1,0:T(8,128)(2,1)S(1)} %copy-done.1, bf16[4096,128]{1,0:T(8,128)(2,1)S(1)} %get-tuple-element.11.refs_3_, f32[4096,256]{1,0:T(8,128)S(1)} %attend_more.1.refs_4_, ...), custom_call_target="tpu_custom_call" | custom-call | flops 1610612736 | bytes 2097152 | tf_op jit(solution)/shard_map/attend_last/pallas_call | solution.py:295
  36.0 0.0 collective-permute-done.13.refs_1_
  36.0 0.4 %collective-permute-done.14.refs_3_ = bf16[4,16,256]{2,1,0:T(8,128)(2,1)S(1)} collective-permute-done((bf16[4,16,256]{2,1,0:T(8,128)(2,1)S(1)}, bf16[4,16,256]{2,1,0:T(8,128)(2,1)S(1)}, u32[]{:S(2)}, u32[]{:S(2)}) %collective-permute-start.14) | collective-permute-done | bytes 32800 | tf_op jit(solution)/shard_map/ppermute | solution.py:45
  36.5 0.2 copy-done.8
  36.7 0.4 %copy-done.9 = bf16[4,16,256]{2,1,0:T(8,128)(2,1)} copy-done((bf16[4,16,256]{2,1,0:T(8,128)(2,1)}, bf16[4,16,256]{2,1,0:T(8,128)(2,1)S(1)}, u32[]{:S(2)}) %copy-start.9) | copy-done | bytes 32792
  37.1 1.7 %place.1 = bf16[1,4,128,256]{3,2,1,0:T(8,128)(2,1)} custom-call(bf16[4,48,256]{2,1,0:T(8,128)(2,1)} %copy-done.3, bf16[4,48,256]{2,1,0:T(8,128)(2,1)} %copy-done.8, bf16[4,16,256]{2,1,0:T(8,128)(2,1)} %copy-done.4, bf16[4,16,256]{2,1,0:T(8,128)(2,1)} %copy-done.9), custom_call_target="tpu_custom_call" | custom-call | tf_op jit(solution)/shard_map/place/pallas_call | solution.py:391
  (13 shorter events, 0.0 us)
Async XLA Ops:
  0.6 26.5 %copy-start.5 = (s32[2,16]{1,0:T(2,128)S(1)}, s32[2,16]{1,0:T(2,128)}, u32[]{:S(2)}) copy-start(s32[2,16]{1,0:T(2,128)} %refs_0_.4) | copy-start | bytes 388
  0.6 22.8 %copy-start.6 = (s32[2,4]{1,0:T(2,128)S(1)}, s32[2,4]{1,0:T(2,128)}, u32[]{:S(2)}) copy-start(s32[2,4]{1,0:T(2,128)} %offset_ref.3) | copy-start | bytes 100
  0.7 26.5 %copy-start.7 = (s32[2]{0:T(128)S(1)}, s32[2]{0:T(128)}, u32[]{:S(2)}) copy-start(s32[2]{0:T(128)} %refs_1_.3) | copy-start | bytes 28
  0.7 10.7 %collective-permute-start = (bf16[128,1024]{1,0:T(8,128)(2,1)}, bf16[128,1024]{1,0:T(8,128)(2,1)S(1)}, u32[]{:S(2)}, u32[]{:S(2)}) collective-permute-start(bf16[128,1024]{1,0:T(8,128)(2,1)} %refs_0_.5), channel_id=1, source_target_pairs={{0,1},{1,0},{2,3},{3,2},{4,5},{5,4},{6,7},{7,6},{8,9},{9,8},{10,11... | collective-permute-start | bytes 786440 | tf_op jit(solution)/shard_map/ppermute | solution.py:45
  1.2 15.1 %collective-permute-start.1 = (bf16[128,1024]{1,0:T(8,128)(2,1)}, bf16[128,1024]{1,0:T(8,128)(2,1)S(1)}, u32[]{:S(2)}, u32[]{:S(2)}) collective-permute-start(bf16[128,1024]{1,0:T(8,128)(2,1)} %refs_0_.5), channel_id=1, source_target_pairs={{0,2},{1,5},{2,0},{3,7},{4,6},{5,1},{6,4},{7,3},{8,10},{9,13},{10,... | collective-permute-start | bytes 786440 | tf_op jit(solution)/shard_map/ppermute | solution.py:50
  3.7 13.1 %collective-permute-start.3 = (bf16[128,1024]{1,0:T(8,128)(2,1)}, bf16[128,1024]{1,0:T(8,128)(2,1)S(1)}, u32[]{:S(2)}, u32[]{:S(2)}) collective-permute-start(bf16[128,1024]{1,0:T(8,128)(2,1)} %refs_0_.5), channel_id=1, source_target_pairs={{0,4},{1,3},{2,6},{3,1},{4,0},{5,7},{6,2},{7,5},{8,12},{9,11},{10,... | collective-permute-start | bytes 786440 | tf_op jit(solution)/shard_map/ppermute | solution.py:50
  7.4 9.4 %collective-permute-start.7 = (bf16[8,1024]{1,0:T(8,128)(2,1)}, bf16[8,1024]{1,0:T(8,128)(2,1)S(1)}, u32[]{:S(2)}, u32[]{:S(2)}) collective-permute-start(bf16[8,1024]{1,0:T(8,128)(2,1)} %get-tuple-element.15), channel_id=1, source_target_pairs={{0,8},{1,9},{2,10},{3,11},{4,12},{5,13},{6,14},{7,15},{8,0},{9,1},... | collective-permute-start | bytes 49160 | tf_op jit(solution)/shard_map/ppermute | solution.py:45
  10.1 7.2 %collective-permute-start.8 = (bf16[8,1024]{1,0:T(8,128)(2,1)}, bf16[8,1024]{1,0:T(8,128)(2,1)S(1)}, u32[]{:S(2)}, u32[]{:S(2)}) collective-permute-start(bf16[8,1024]{1,0:T(8,128)(2,1)} %get-tuple-element.14), channel_id=1, source_target_pairs={{0,2},{1,5},{2,0},{3,7},{4,6},{5,1},{6,4},{7,3},{8,10},{9,13},{10,... | collective-permute-start | bytes 49160 | tf_op jit(solution)/shard_map/ppermute | solution.py:50
  11.4 6.0 %collective-permute-start.9 = (bf16[8,1024]{1,0:T(8,128)(2,1)}, bf16[8,1024]{1,0:T(8,128)(2,1)S(1)}, u32[]{:S(2)}, u32[]{:S(2)}) collective-permute-start(bf16[8,1024]{1,0:T(8,128)(2,1)} %get-tuple-element.15), channel_id=1, source_target_pairs={{0,10},{1,13},{2,8},{3,15},{4,14},{5,9},{6,12},{7,11},{8,2},{9,5},... | collective-permute-start | bytes 49160 | tf_op jit(solution)/shard_map/ppermute | solution.py:55
  12.6 1.2 %copy-start = (bf16[128,4096]{1,0:T(8,128)(2,1)S(1)}, bf16[128,4096]{1,0:T(8,128)(2,1)}, u32[]{:S(2)}) copy-start(bf16[128,4096]{1,0:T(8,128)(2,1)} %refs_2_.3) | copy-start | bytes 3145732
  13.9 0.9 %copy-start.2 = (bf16[128,1024]{1,0:T(8,128)(2,1)S(1)}, bf16[128,1024]{1,0:T(8,128)(2,1)}, u32[]{:S(2)}) copy-start(bf16[128,1024]{1,0:T(8,128)(2,1)} %refs_0_.5) | copy-start | bytes 786436
  14.8 12.3 %copy-start.1 = (bf16[128,4096]{1,0:T(8,128)(2,1)S(1)}, bf16[128,4096]{1,0:T(8,128)(2,1)}, u32[]{:S(2)}) copy-start(bf16[128,4096]{1,0:T(8,128)(2,1)} %refs_2_.3) | copy-start | bytes 3145732
  16.3 6.4 %collective-permute-start.5 = (bf16[128,1024]{1,0:T(8,128)(2,1)S(1)}, bf16[128,1024]{1,0:T(8,128)(2,1)S(1)}, u32[]{:S(2)}, u32[]{:S(2)}) collective-permute-start(bf16[128,1024]{1,0:T(8,128)(2,1)S(1)} %collective-permute-done.1.refs_5_.refs_13_.refs_2_), channel_id=1, source_target_pairs={{0,4},{1,3},{2,6},{3,1},{4,0},{5,7},{6,2},{7,5},{8,12},{9,11},{10,... | collective-permute-start | bytes 786440 | tf_op jit(solution)/shard_map/ppermute | solution.py:50
  16.8 6.6 %collective-permute-start.2 = (bf16[128,1024]{1,0:T(8,128)(2,1)S(1)}, bf16[128,1024]{1,0:T(8,128)(2,1)S(1)}, u32[]{:S(2)}, u32[]{:S(2)}) collective-permute-start(bf16[128,1024]{1,0:T(8,128)(2,1)S(1)} %collective-permute-done.1.refs_5_.refs_13_.refs_2_), channel_id=1, source_target_pairs={{0,1},{1,0},{2,3},{3,2},{4,5},{5,4},{6,7},{7,6},{8,9},{9,8},{10,11... | collective-permute-start | bytes 786440 | tf_op jit(solution)/shard_map/ppermute | solution.py:45
  16.8 6.6 %collective-permute-start.4 = (bf16[128,1024]{1,0:T(8,128)(2,1)S(1)}, bf16[128,1024]{1,0:T(8,128)(2,1)S(1)}, u32[]{:S(2)}, u32[]{:S(2)}) collective-permute-start(bf16[128,1024]{1,0:T(8,128)(2,1)S(1)} %collective-permute-done.3.refs_7_.refs_15_.refs_4_), channel_id=1, source_target_pairs={{0,1},{1,0},{2,3},{3,2},{4,5},{5,4},{6,7},{7,6},{8,9},{9,8},{10,11... | collective-permute-start | bytes 786440 | tf_op jit(solution)/shard_map/ppermute | solution.py:45
  17.4 6.1 %collective-permute-start.11 = (bf16[32,1024]{1,0:T(8,128)(2,1)S(1)}, bf16[32,1024]{1,0:T(8,128)(2,1)S(1)}, u32[]{:S(2)}, u32[]{:S(2)}) collective-permute-start(bf16[32,1024]{1,0:T(8,128)(2,1)S(1)} %constant_dynamic-update-slice_fusion.refs_7_), channel_id=1, source_target_pairs={{0,4},{1,3},{2,6},{3,1},{4,0},{5,7},{6,2},{7,5},{8,12},{9,11},{10,... | collective-permute-start | bytes 196616 | tf_op jit(solution)/shard_map/ppermute | solution.py:50
  22.7 7.8 %collective-permute-start.6 = (bf16[128,1024]{1,0:T(8,128)(2,1)S(1)}, bf16[128,1024]{1,0:T(8,128)(2,1)S(1)}, u32[]{:S(2)}, u32[]{:S(2)}) collective-permute-start(bf16[128,1024]{1,0:T(8,128)(2,1)S(1)} %collective-permute-done.5.refs_5_.refs_0_), channel_id=1, source_target_pairs={{0,1},{1,0},{2,3},{3,2},{4,5},{5,4},{6,7},{7,6},{8,9},{9,8},{10,11... | collective-permute-start | bytes 786440 | tf_op jit(solution)/shard_map/ppermute | solution.py:45
  22.7 9.0 %collective-permute-start.10 = (bf16[32,1024]{1,0:T(8,128)(2,1)S(1)}, bf16[32,1024]{1,0:T(8,128)(2,1)S(1)}, u32[]{:S(2)}, u32[]{:S(2)}) collective-permute-start(bf16[32,1024]{1,0:T(8,128)(2,1)S(1)} %constant_dynamic-update-slice_fusion.refs_7_), channel_id=1, source_target_pairs={{0,1},{1,0},{2,3},{3,2},{4,5},{5,4},{6,7},{7,6},{8,9},{9,8},{10,11... | collective-permute-start | bytes 196616 | tf_op jit(solution)/shard_map/ppermute | solution.py:45
  23.4 8.3 %collective-permute-start.12 = (bf16[32,1024]{1,0:T(8,128)(2,1)S(1)}, bf16[32,1024]{1,0:T(8,128)(2,1)S(1)}, u32[]{:S(2)}, u32[]{:S(2)}) collective-permute-start(bf16[32,1024]{1,0:T(8,128)(2,1)S(1)} %collective-permute-done.11.refs_9_), channel_id=1, source_target_pairs={{0,1},{1,0},{2,3},{3,2},{4,5},{5,4},{6,7},{7,6},{8,9},{9,8},{10,11... | collective-permute-start | bytes 196616 | tf_op jit(solution)/shard_map/ppermute | solution.py:45
  24.5 6.1 %copy-start.3 = (bf16[4,48,256]{2,1,0:T(8,128)(2,1)}, bf16[4,48,256]{2,1,0:T(8,128)(2,1)S(1)}, u32[]{:S(2)}) copy-start(bf16[4,48,256]{2,1,0:T(8,128)(2,1)S(1)} %get-tuple-element.16.refs_0_) | copy-start | bytes 294916
  24.5 11.5 %collective-permute-start.13 = (bf16[4,48,256]{2,1,0:T(8,128)(2,1)S(1)}, bf16[4,48,256]{2,1,0:T(8,128)(2,1)S(1)}, u32[]{:S(2)}, u32[]{:S(2)}) collective-permute-start(bf16[4,48,256]{2,1,0:T(8,128)(2,1)S(1)} %get-tuple-element.17), channel_id=1, source_target_pairs={{0,8},{1,9},{2,10},{3,11},{4,12},{5,13},{6,14},{7,15},{8,0},{9,1},... | collective-permute-start | bytes 294920 | tf_op jit(solution)/shard_map/ppermute | solution.py:45
  31.3 4.7 %copy-start.4 = (bf16[4,16,256]{2,1,0:T(8,128)(2,1)}, bf16[4,16,256]{2,1,0:T(8,128)(2,1)S(1)}, u32[]{:S(2)}) copy-start(bf16[4,16,256]{2,1,0:T(8,128)(2,1)S(1)} %get-tuple-element.18.refs_2_) | copy-start | bytes 98308
  31.3 5.1 %collective-permute-start.14 = (bf16[4,16,256]{2,1,0:T(8,128)(2,1)S(1)}, bf16[4,16,256]{2,1,0:T(8,128)(2,1)S(1)}, u32[]{:S(2)}, u32[]{:S(2)}) collective-permute-start(bf16[4,16,256]{2,1,0:T(8,128)(2,1)S(1)} %get-tuple-element.19), channel_id=1, source_target_pairs={{0,8},{1,9},{2,10},{3,11},{4,12},{5,13},{6,14},{7,15},{8,0},{9,1},... | collective-permute-start | bytes 98312 | tf_op jit(solution)/shard_map/ppermute | solution.py:45
  36.0 0.6 %copy-start.8 = (bf16[4,48,256]{2,1,0:T(8,128)(2,1)}, bf16[4,48,256]{2,1,0:T(8,128)(2,1)S(1)}, u32[]{:S(2)}) copy-start(bf16[4,48,256]{2,1,0:T(8,128)(2,1)S(1)} %collective-permute-done.13.refs_1_) | copy-start | bytes 294916
  36.5 0.6 %copy-start.9 = (bf16[4,16,256]{2,1,0:T(8,128)(2,1)}, bf16[4,16,256]{2,1,0:T(8,128)(2,1)S(1)}, u32[]{:S(2)}) copy-start(bf16[4,16,256]{2,1,0:T(8,128)(2,1)S(1)} %collective-permute-done.14.refs_3_) | copy-start | bytes 98308

commit v3 on v2

v3 whole, which is shorter than its diff:
```python
import functools

import jax
import jax.numpy as jnp
from jax import lax
from jax.experimental import pallas as pl
from jax.experimental.pallas import tpu as pltpu
from jax.sharding import PartitionSpec as P

HD = 128
QH = 32
KVH = 4
REQS = 2
PAGE = 8
SLOTS = 32
GQ = QH // KVH

LOG2E = 1.4426950408889634
OUT_OF_REACH = -1e30
CHUNK = 512
VMEM_BYTES = 16 * 1024 * 1024
OPEN_VMEM_BYTES = 58 * 1024 * 1024
SMALL_VMEM_BYTES = 6 * 1024 * 1024
SAFE_MASS = 1e36
CONTRACT_LAST = (((1,), (1,)), ((), ()))

IN_VMEM = pl.BlockSpec(memory_space=pltpu.VMEM)
IN_SMEM = pl.BlockSpec(memory_space=pltpu.SMEM)
ANYWHERE = pl.BlockSpec(memory_space=pl.ANY)
IN_HBM = pl.BlockSpec(memory_space=pltpu.HBM)


def hop_bits(devices):
    bits = []
    bit = 2
    while bit < devices // REQS:
        bits.append(bit)
        bit *= 2
    return (tuple(bits), tuple(reversed(bits)))


def pick(core, pair):
    return jnp.where(core == 0, pair[0], pair[1])


def swap(value, bit):
    route = [(i, i ^ bit) for i in range(lax.axis_size("seq"))]
    return lax.ppermute(value, "seq", route)


def swap_by_core(value, orders, step):
    route = [(i, i ^ orders[i % 2][step]) for i in range(lax.axis_size("seq"))]
    return lax.ppermute(value, "seq", route)


def swap_wide(value, orders, bit):
    route = [(i, i ^ bit ^ orders[i % 2][0]) for i in range(lax.axis_size("seq"))]
    return lax.ppermute(value, "seq", route)


def after(value, *earlier):
    return lax.optimization_barrier((value,) + earlier)[0]


def source_of(me, swapped, path, orders):
    at = me ^ 1 if swapped else me
    core = at % 2
    for step in path:
        at = at ^ pick(core, (orders[0][step], orders[1][step]))
    return at


def page_bias(me, devices, orders, places, table_ref, hit_ref):
    shape = (4 * PAGE, HD)
    token = lax.broadcasted_iota(jnp.int32, shape, 0)
    slot = token >> (PAGE.bit_length() - 1)
    stores = []
    for swapped, path in places:
        base = source_of(me, swapped, path, orders)
        hop = pick(base & 1, (orders[0][0], orders[1][0]))
        at = jnp.where(slot >= 2, base ^ hop, base)
        stores.append(jnp.where((slot & 1) == 1, at ^ (devices // REQS), at))
    store = jnp.concatenate(stores, axis=0)
    inside = jnp.concatenate([token & (PAGE - 1)] * len(places), axis=0)
    request = me // (devices // REQS)
    position = jnp.zeros_like(store)
    for j in range(table_ref.shape[1]):
        position = jnp.where(store == table_ref[request, j] >> (SLOTS.bit_length() - 1), j * PAGE, position)
    return bias_lanes(jnp.where(position + inside < hit_ref[request], 0.0, OUT_OF_REACH))


def open_kernel(devices, orders, places, table_hbm, hit_hbm, store_ref, *refs):
    own_ref, other_ref, bias_ref, table_ref, hit_ref, sems = refs
    table = pltpu.make_async_copy(table_hbm, table_ref, sems.at[2])
    hits = pltpu.make_async_copy(hit_hbm, hit_ref, sems.at[3])
    table.start()
    hits.start()
    me = lax.axis_index("seq")
    request = me // (devices // REQS)
    copies = []
    table.wait()
    for n, (req, page_ref) in enumerate(((1 - request, other_ref), (request, own_ref))):
        slot = jnp.int32(0)
        for j in range(table_ref.shape[1]):
            away = table_ref[req, j] - me * SLOTS
            slot = jnp.where((away >= 0) & (away < SLOTS), away, slot)
        copies.append(pltpu.make_async_copy(store_ref.at[slot], page_ref, sems.at[n]))
        copies[-1].start()
    hits.wait()
    bias_ref[...] = page_bias(me, devices, orders, places, table_ref, hit_ref)
    for copy in copies:
        copy.wait()


def open_up(devices, orders, places, page_table, hit_tokens, kv_store):
    page = jax.ShapeDtypeStruct(kv_store.shape[1:], kv_store.dtype)
    return pl.pallas_call(
        functools.partial(open_kernel, devices, orders, places),
        out_shape=(
            page,
            page,
            jax.ShapeDtypeStruct((4 * PAGE * len(places), HD), jnp.bfloat16),
        ),
        in_specs=[IN_HBM] * 3,
        out_specs=(IN_VMEM,) * 3,
        scratch_shapes=[
            pltpu.SMEM(page_table.shape, jnp.int32),
            pltpu.SMEM(hit_tokens.shape, jnp.int32),
            pltpu.SemaphoreType.DMA((4,)),
        ],
        compiler_params=pltpu.CompilerParams(vmem_limit_bytes=OPEN_VMEM_BYTES),
        name="open_up",
    )(page_table, hit_tokens, kv_store)


def pack_kernel(block_ref, *refs):
    page_refs, out_ref = refs[:-1], refs[-1]
    rows = block_ref.shape[0]
    out_ref[:rows] = block_ref[...]
    out_ref[rows:] = jnp.concatenate([ref[...] for ref in page_refs], axis=0)


def pack(block, pages):
    rows = block.shape[0] + sum(page.shape[0] for page in pages)
    return pl.pallas_call(
        pack_kernel,
        out_shape=jax.ShapeDtypeStruct((rows, block.shape[1]), block.dtype),
        in_specs=[IN_VMEM] * (1 + len(pages)),
        out_specs=IN_VMEM,
        compiler_params=pltpu.CompilerParams(vmem_limit_bytes=SMALL_VMEM_BYTES),
        name="pack",
    )(block, *pages)


def stack(refs, at):
    return jnp.concatenate([ref[first : first + count, at : at + HD] for ref, first, count in refs], axis=0)


def head_rows(q_ref, g):
    heads = range(g * GQ, (g + 1) * GQ)
    return jnp.concatenate([q_ref[:, h * HD : (h + 1) * HD] for h in heads], axis=0)


def with_ones(values):
    return jnp.concatenate([values, jnp.ones_like(values)], axis=1)


def shift_lanes(shift):
    lane = lax.broadcasted_iota(jnp.int32, shift.shape, 1)
    return jnp.where(lane == 0, -shift, jnp.where(lane == 1, 1.0, 0.0)).astype(jnp.bfloat16)


def bias_lanes(bias):
    lane = lax.broadcasted_iota(jnp.int32, bias.shape, 1)
    return jnp.where(lane == 0, 1.0, jnp.where(lane == 1, bias, 0.0)).astype(jnp.bfloat16)


def causal_bias(rows):
    t = lax.broadcasted_iota(jnp.int32, (rows, rows), 0)
    k = lax.broadcasted_iota(jnp.int32, (rows, rows), 1)
    return jnp.where(k <= t, 0.0, OUT_OF_REACH)


SCALE = HD**-0.5 * LOG2E


def first_kernel(orders, q_ref, own_ref, mate_ref, mass_ref, shift_ref):
    me = lax.axis_index("seq")
    rows = q_ref.shape[0]
    mate_bias = jnp.where(me % 2 == 1, 0.0, OUT_OF_REACH)
    bias = jnp.concatenate([causal_bias(rows), jnp.full((rows, rows), mate_bias, jnp.float32)], axis=1)
    refs = ((own_ref, 0, rows), (mate_ref, 0, rows))
    for g in range(KVH):
        at = g * 2 * HD
        scores = lax.dot_general(head_rows(q_ref, g), stack(refs, at), CONTRACT_LAST, preferred_element_type=jnp.float32)
        scores = (scores.reshape(GQ, rows, -1) + bias[None]).reshape(GQ * rows, -1)
        peak = jnp.max(scores, axis=1, keepdims=True)
        shift = jnp.broadcast_to(peak, (GQ * rows, HD)).astype(jnp.bfloat16).astype(jnp.float32)
        weights = jnp.exp2((scores - jnp.concatenate([shift, shift], axis=1)) * SCALE).astype(jnp.bfloat16)
        span = pl.ds(g * GQ * rows, GQ * rows)
        mass_ref[span, :] = jnp.dot(weights, with_ones(stack(refs, at + HD)), preferred_element_type=jnp.float32)
        shift_ref[span, :] = shift_lanes(shift)


def attend_first(orders, queries, own, mate):
    rows = queries.shape[0]
    return pl.pallas_call(
        functools.partial(first_kernel, orders),
        out_shape=(
            jax.ShapeDtypeStruct((QH * rows, 2 * HD), jnp.float32),
            jax.ShapeDtypeStruct((QH * rows, HD), jnp.bfloat16),
        ),
        in_specs=[IN_VMEM] * 3,
        out_specs=(IN_VMEM, IN_VMEM),
        compiler_params=pltpu.CompilerParams(vmem_limit_bytes=VMEM_BYTES),
        cost_estimate=pl.CostEstimate(
            flops=16 * rows * QH * rows * HD, bytes_accessed=4 * rows * QH * HD, transcendentals=2 * rows * QH * rows
        ),
        name="attend_first",
    )(queries, own, mate)


def block_bias(me, orders, kind, rows):
    if kind[0] == "own":
        return bias_lanes(jnp.zeros((rows, HD), jnp.float32))
    source = source_of(me, kind[1], kind[2], orders)
    return bias_lanes(jnp.full((rows, HD), jnp.where(source < me, 0.0, OUT_OF_REACH), jnp.float32))


def add_up(q_wide, group, bias, at):
    keys = jnp.concatenate([stack(group, at), bias], axis=1)
    scores = lax.dot_general(q_wide, keys, CONTRACT_LAST, preferred_element_type=jnp.float32)
    weights = jnp.exp2(scores * SCALE).astype(jnp.bfloat16)
    return jnp.dot(weights, with_ones(stack(group, at + HD)), preferred_element_type=jnp.float32)


def more_kernel(orders, kinds, q_ref, shift_ref, mass_ref, *refs):
    out_ref = refs[-1]
    me = lax.axis_index("seq")
    rows = q_ref.shape[0]
    group = [(ref, 0, rows) for ref in refs[:-1]]
    bias = jnp.concatenate([block_bias(me, orders, kind, rows) for kind in kinds], axis=0)
    for g in range(KVH):
        span = pl.ds(g * GQ * rows, GQ * rows)
        q_wide = jnp.concatenate([head_rows(q_ref, g), shift_ref[span, :]], axis=1)
        out_ref[span, :] = mass_ref[span, :] + add_up(q_wide, group, bias, g * 2 * HD)


def attend_more(orders, queries, shift, mass, batch):
    rows = queries.shape[0]
    keys = rows * len(batch)
    return pl.pallas_call(
        functools.partial(more_kernel, orders, tuple(kind for kind, _ in batch)),
        out_shape=jax.ShapeDtypeStruct(mass.shape, mass.dtype),
        in_specs=[IN_VMEM] * (3 + len(batch)),
        out_specs=IN_VMEM,
        input_output_aliases={2: 0},
        compiler_params=pltpu.CompilerParams(vmem_limit_bytes=VMEM_BYTES),
        cost_estimate=pl.CostEstimate(
            flops=8 * rows * QH * keys * HD, bytes_accessed=4 * rows * QH * HD, transcendentals=rows * QH * keys
        ),
        name="attend_more",
    )(queries, shift, mass, *[value for _, value in batch])


def last_kernel(orders, kinds, page_count, other_kinds, q_ref, shift_ref, mass_ref, bias_ref, *refs):
    me = lax.axis_index("seq")
    rows = q_ref.shape[0]
    block_refs = refs[: len(kinds)]
    page_refs = refs[len(kinds) : len(kinds) + page_count]
    other_refs = refs[len(kinds) + page_count : -9]
    out_ref, kept_ref, wrong_ref, top_ref, denominator_ref, total_ref, block_ref, sems, sem = refs[-9:]
    held = 4 * PAGE
    group = [(ref, 0, rows) for ref in block_refs] + [(ref, rows, held) for ref in page_refs]
    biases = [block_bias(me, orders, kind, rows) for kind in kinds] + [bias_ref[...]]
    bias = jnp.concatenate(biases, axis=0)
    wrong_ref[...] = jnp.zeros_like(wrong_ref)
    width = GQ * HD

    def write(g):
        return pltpu.make_async_copy(kept_ref.at[g], out_ref.at[:, pl.ds(g * width, width)], sems.at[g])

    for g in range(KVH):
        span = pl.ds(g * GQ * rows, GQ * rows)
        q_wide = jnp.concatenate([head_rows(q_ref, g), shift_ref[span, :]], axis=1)
        mass = mass_ref[span, :] + add_up(q_wide, group, bias, g * 2 * HD)
        total, denominator = mass[:, :HD], mass[:, HD:]
        wrong = jnp.where(denominator < SAFE_MASS, 0.0, 1.0)
        wrong_ref[...] = jnp.maximum(wrong_ref[...], jnp.max(wrong.reshape(-1, 8, HD), axis=0))
        attended = (total / denominator).astype(kept_ref.dtype)
        for n in range(GQ):
            kept_ref[g, :, n * HD : (n + 1) * HD] = attended[n * rows : (n + 1) * rows]
        write(g).start()
    for g in range(KVH):
        write(g).wait()

    @pl.when(jnp.max(wrong_ref[...]) > 0.0)
    def _():
        top_ref[...] = jnp.full_like(top_ref, OUT_OF_REACH)
        denominator_ref[...] = jnp.zeros_like(denominator_ref)
        total_ref[...] = jnp.zeros_like(total_ref)
        no_shift = shift_lanes(jnp.zeros((rows, HD), jnp.float32))

        def take(ref, first, count, lanes, causal):
            def one_head(n, carried):
                g, h = n // GQ, n % GQ
                at = pl.multiple_of(g * 2 * HD, 2 * HD)
                span = pl.ds(pl.multiple_of(n * rows, rows), rows)
                q = q_ref[:, pl.ds(pl.multiple_of(n * HD, HD), HD)]
                keys = jnp.concatenate([ref[first : first + count, pl.ds(at, HD)], lanes], axis=1)
                scores = lax.dot_general(
                    jnp.concatenate([q, no_shift], axis=1), keys, CONTRACT_LAST, preferred_element_type=jnp.float32
                )
                if causal:
                    scores = scores + causal_bias(rows)
                top = top_ref[span, :]
                new_top = jnp.maximum(top, jnp.max(scores, axis=1, keepdims=True))
                weights = jnp.exp2((scores - new_top[:, :count]) * SCALE)
                factor = jnp.exp2((top - new_top) * SCALE)
                top_ref[span, :] = new_top
                denominator_ref[span, :] = denominator_ref[span, :] * factor + jnp.sum(weights, axis=1, keepdims=True)
                total_ref[span, :] = total_ref[span, :] * factor + jnp.dot(
                    weights.astype(jnp.bfloat16),
                    ref[first : first + count, pl.ds(at + HD, HD)],
                    preferred_element_type=jnp.float32,
                )
                return carried

            lax.fori_loop(0, QH, one_head, 0)

        for kind, ref in zip(other_kinds, other_refs):
            copy = pltpu.make_async_copy(ref.at[pl.ds(0, rows)], block_ref, sem)
            copy.start()
            copy.wait()
            take(block_ref, 0, rows, block_bias(me, orders, kind, rows), kind[0] == "own")
        for kind, ref in zip(kinds, block_refs):
            take(ref, 0, rows, block_bias(me, orders, kind, rows), False)
        for n, ref in enumerate(page_refs):
            take(ref, rows, held, bias_ref[n * held : (n + 1) * held], False)
        for g in range(KVH):
            for n in range(GQ):
                span = pl.ds((g * GQ + n) * rows, rows)
                attended = total_ref[span, :] / denominator_ref[span, :]
                kept_ref[g, :, n * HD : (n + 1) * HD] = attended.astype(kept_ref.dtype)
            write(g).start()
        for g in range(KVH):
            write(g).wait()


def attend_last(orders, queries, shift, mass, bias, batch, pages, others):
    rows = queries.shape[0]
    keys = rows * len(batch) + bias.shape[0]
    width = 2 * KVH * HD
    return pl.pallas_call(
        functools.partial(
            last_kernel, orders, tuple(kind for kind, _ in batch), len(pages), tuple(kind for kind, _ in others)
        ),
        out_shape=jax.ShapeDtypeStruct((rows, QH * HD), queries.dtype),
        in_specs=[IN_VMEM] * (4 + len(batch) + len(pages)) + [ANYWHERE] * len(others),
        out_specs=ANYWHERE,
        scratch_shapes=[
            pltpu.VMEM((KVH, rows, GQ * HD), queries.dtype),
            pltpu.VMEM((8, HD), jnp.float32),
            *[pltpu.VMEM((QH * rows, HD), jnp.float32)] * 3,
            pltpu.VMEM((rows, width), jnp.bfloat16),
            pltpu.SemaphoreType.DMA((KVH,)),
            pltpu.SemaphoreType.DMA,
        ],
        compiler_params=pltpu.CompilerParams(vmem_limit_bytes=VMEM_BYTES),
        cost_estimate=pl.CostEstimate(
            flops=8 * rows * QH * keys * HD, bytes_accessed=4 * rows * QH * HD, transcendentals=rows * QH * keys
        ),
        name="attend_last",
    )(queries, shift, mass, bias, *[value for _, value in batch], *pages, *[value for _, value in others])


def owner_kernel(devices, orders, rows, kinds, hops, offset_ref, *refs):
    key_refs = refs[: len(kinds)]
    own_ref, other_ref = refs[len(kinds) :]
    me = lax.axis_index("seq")
    group_size = devices // REQS
    request = me // group_size
    each = rows // devices
    kept = own_ref.shape[1]
    lane = lax.broadcasted_iota(jnp.int32, (1, rows), 1)
    row = lax.broadcasted_iota(jnp.int32, (2 * kept, rows), 0)
    wanted_row = jnp.where(row >= kept, row - kept, row)
    residue, landing = lane % devices, lane // devices
    bases = []
    for kind in kinds:
        source = me if kind[0] == "own" else source_of(me, kind[1], kind[2], orders)
        place = source % group_size
        if hops[0] is not None:
            place = source % 2
            for n, hop in enumerate(hops):
                place = place + jnp.where((source ^ me) // 2 == hop // 2, 2 * n, 0)
        bases.append(place * each)
    for g in range(KVH):
        turn = (me - offset_ref[request, g] + devices) % devices
        mine = jnp.where(residue == turn, landing, -kept - rows)
        others = jnp.where(residue == turn ^ (devices // REQS), landing, -kept - rows)
        wanted = jnp.where(row >= kept, others, mine)
        total = jnp.zeros((2 * kept, 2 * HD), jnp.float32)
        for ref, base in zip(key_refs, bases):
            chosen = wanted_row == wanted + base
            total = total + jnp.dot(
                jnp.where(chosen, 1.0, 0.0).astype(jnp.bfloat16),
                ref[:rows, g * 2 * HD : (g + 1) * 2 * HD],
                preferred_element_type=jnp.float32,
            )
        own_ref[g] = total[:kept].astype(own_ref.dtype)
        other_ref[g] = total[kept:].astype(other_ref.dtype)


def pick_for_owners(devices, orders, owner_offset, rows, batch, hops):
    kept = len(batch) * rows // devices
    piece = jax.ShapeDtypeStruct((KVH, kept, 2 * HD), batch[0][1].dtype)
    return pl.pallas_call(
        functools.partial(owner_kernel, devices, orders, rows, tuple(kind for kind, _ in batch), hops),
        out_shape=(piece, piece),
        in_specs=[IN_SMEM] + [IN_VMEM] * len(batch),
        out_specs=(IN_VMEM, IN_VMEM),
        compiler_params=pltpu.CompilerParams(vmem_limit_bytes=SMALL_VMEM_BYTES),
        name="pick_for_owners",
    )(owner_offset, *[value for _, value in batch])


def place_kernel(devices, spans, size, *refs):
    me = lax.axis_index("seq")
    group_size = devices // REQS
    request = me // group_size
    chip = (me % group_size) // 2
    kept = size // REQS
    out_ref = refs[-1]
    for n, hops in enumerate(spans):
        for side, req in enumerate((request, 1 - request)):
            ref = refs[2 * n + side]
            height = ref.shape[1] // len(hops)
            for k, hop in enumerate(hops):
                start = req * kept
                if hop is not None:
                    start = start + (chip ^ (hop // 2)) * height
                rows = pl.ds(pl.multiple_of(start, height), height)
                out_ref[0, :, rows] = ref[:, k * height : (k + 1) * height]


def place(devices, pieces, spans, size):
    flat = [array for pair in pieces for array in pair]
    heads, _, width = flat[0].shape
    return pl.pallas_call(
        functools.partial(place_kernel, devices, tuple(spans), size),
        out_shape=jax.ShapeDtypeStruct((1, heads, size, width), flat[0].dtype),
        in_specs=[IN_VMEM] * len(flat),
        out_specs=IN_VMEM,
        compiler_params=pltpu.CompilerParams(vmem_limit_bytes=SMALL_VMEM_BYTES),
        name="place",
    )(*flat)


def shards(queries, suffix_kv, kv_store, page_table, hit_tokens, owner_offset):
    devices = lax.axis_size("seq")
    orders = hop_bits(devices)
    steps = len(orders[0])
    partner = devices // REQS
    rows = suffix_kv.shape[0]

    page_paths = [()]
    for step in range(1, steps):
        page_paths = page_paths + [path + (step,) for path in page_paths]
    places = tuple((swapped, path) for path in page_paths for swapped in (False, True))

    first_hop = swap_by_core(suffix_kv, orders, 0)
    mate = swap(suffix_kv, 1)
    own_page, other_page, bias = open_up(devices, orders, places, page_table, hit_tokens, kv_store)
    page_set = [
        own_page,
        swap(other_page, partner),
        swap_by_core(own_page, orders, 0),
        swap_wide(after(other_page, mate), orders, partner),
    ]
    mass, shift = attend_first(orders, queries, suffix_kv, mate)
    held = [((), suffix_kv), ((0,), pack(first_hop, page_set))]
    for step in range(1, steps):
        held = held + [(path + (step,), swap_by_core(value, orders, step)) for path, value in held]

    arrivals, pages = [], {}

    def exchange(moved, *earlier):
        for path, value in moved:
            swapped_value = swap(after(value, *earlier) if earlier else value, 1)
            arrivals.append([(("block", False, path), value), (("block", True, path), swapped_value)])
            if path[0] == 0:
                pages[(False, path[1:])], pages[(True, path[1:])] = value, swapped_value

    def to_owners(batch, hops):
        mine, theirs = pick_for_owners(devices, orders, owner_offset, rows, batch, hops)
        spans.append(hops)
        pieces.append((mine, swap(theirs, partner)))
        return theirs

    home = [(("own",), suffix_kv), (("block", True, ()), after(mate, shift))]
    pieces, spans = [], []
    if steps == 2 and (2 * rows // devices) % 16 == 0:
        near, across = orders[0], orders[0][0] ^ orders[0][1]
        exchange(held[1:3])
        sent = to_owners(home + arrivals[0] + arrivals[1], (0,) + near)
        exchange(held[3:], sent)
        to_owners(arrivals[2], (across,))
    else:
        exchange(held[1:])
        to_owners(home + sum(arrivals, []), (None,))

    for n in range(0, len(arrivals) - 1, 2):
        mass = attend_more(orders, queries, shift, mass, sum(arrivals[n : min(n + 2, len(arrivals) - 1)], []))
    attention_out = attend_last(
        orders,
        queries,
        shift,
        mass,
        bias,
        arrivals[-1],
        [pages[place] for place in places],
        home + sum(arrivals[:-1], []),
    )
    return (attention_out, place(devices, pieces, spans, REQS * partner * rows // devices))


def solution(mesh):
    in_specs = (
        P(("groups", "seq"), None),
        P(("groups", "seq"), None),
        P(("groups", "seq"), None, None),
        P("groups", None),
        P("groups"),
        P("groups", None),
    )
    out_specs = (P(("groups", "seq"), None), P(("groups", "seq"), None, None, None))
    return jax.shard_map(shards, mesh=mesh, in_specs=in_specs, out_specs=out_specs, check_vma=False)
```

time: 39.2 us -> 35.4 us (0.903)
  Pallas kernels: 14.6 us -> 12.3 us
  starting transfers between devices: 15.3 us -> 13.9 us
  waiting for transfers between devices: 4.39 us -> 5.29 us
  local copies, waits for them, and re-layouts: 3.56 us -> 2.9 us
    ppermute x1, waiting for transfers between devices: 0.01 us -> 2.39 us  [swap_wide(): return lax.ppermute(value, 'seq', route)]
    ppermute x5 -> x4, starting transfers between devices: 6.83 us -> 5.14 us  [swap_by_core(): return lax.ppermute(value, 'seq', route)]
    ppermute x5 -> x4, waiting for transfers between devices: 3.93 us -> 2.43 us  [swap_by_core(): return lax.ppermute(value, 'seq', route)]
    pallas_call x5 -> x6, Pallas kernels: 11.5 us -> 10.1 us  [the longest x1 3.33 us: attend_last(): pl.pallas_call(functools.partial(last_kernel, orders, tuple((kind for kin...]
    pallas_call x1, Pallas kernels: 1.68 us -> 0.75 us  [place(): pl.pallas_call(functools.partial(place_kernel, devices, tuple(spans), siz...]
    unnamed x23 -> x10, local copies, waits for them, and re-layouts: 3.56 us -> 2.9 us
    ppermute x9 -> x7, starting transfers between devices: 7.24 us -> 7.49 us  [swap(): return lax.ppermute(value, 'seq', route)]
  transfers between devices with their start and end apart: 15 -> 12, of which waited for: 3 -> 4; matrix products, arithmetic and copies ran while one was open for 2% -> 0% of each run, Pallas kernels for 33% -> 33%
where the time goes in v3:
time: 35.4 us; the launch traced here: 35.1 us
  starting transfers between devices  13.9 us (39%)
  Pallas kernels  12.3 us (35%)
  waiting for transfers between devices  5.29 us (15%)
  local copies, waits for them, and re-layouts  2.9 us (8%)
  between operations  0.75 us (2%)
    ppermute x7, starting transfers between devices, swap(): return lax.ppermute(value, 'seq', route)  7.49 us
    ppermute x4, starting transfers between devices, swap_by_core(): return lax.ppermute(value, 'seq', route)  5.14 us
    pallas_call x1, Pallas kernels, attend_last(): pl.pallas_call(functools.partial(last_kernel, orders, tuple((kind for kin...  3.33 us
    unnamed x10, local copies, waits for them, and re-layouts  2.9 us
    pallas_call x1, Pallas kernels, attend_more(): pl.pallas_call(functools.partial(more_kernel, orders, tuple((kind for kin...  2.8 us
    ppermute x4, waiting for transfers between devices, swap_by_core(): return lax.ppermute(value, 'seq', route)  2.43 us
    ppermute x1, waiting for transfers between devices, swap_wide(): return lax.ppermute(value, 'seq', route)  2.39 us
    pallas_call x1, Pallas kernels, open_up(): pl.pallas_call(functools.partial(open_kernel, devices, orders, places), o...  2.13 us
  transfers between devices with their start and end apart: 12, of which 4 were waited for; matrix products, arithmetic and copies ran while one was open for 0% of the time, Pallas kernels for 33%

profile of v3, /device:TPU:0, one launch (start us, length us, event | category | flops | bytes accessed | tf_op | source)
XLA Modules:
  0.0 35.1 jit_solution(13171836717787521395)
XLA Ops:
  0.6 0.0 copy-start.4
  0.6 0.5 %collective-permute-start = (bf16[128,1024]{1,0:T(8,128)(2,1)}, bf16[128,1024]{1,0:T(8,128)(2,1)S(1)}, u32[]{:S(2)}, u32[]{:S(2)}) collective-permute-start(bf16[128,1024]{1,0:T(8,128)(2,1)} %refs_6_.1), channel_id=1, source_target_pairs={{0,1},{1,0},{2,3},{3,2},{4,5},{5,4},{6,7},{7,6},{8,9},{9,8},{10,11... | collective-permute-start | bytes 786440 | tf_op jit(solution)/shard_map/ppermute | solution.py:48
  1.2 2.6 %collective-permute-start.1 = (bf16[128,1024]{1,0:T(8,128)(2,1)}, bf16[128,1024]{1,0:T(8,128)(2,1)S(1)}, u32[]{:S(2)}, u32[]{:S(2)}) collective-permute-start(bf16[128,1024]{1,0:T(8,128)(2,1)} %refs_6_.1), channel_id=1, source_target_pairs={{0,2},{1,5},{2,0},{3,7},{4,6},{5,1},{6,4},{7,3},{8,10},{9,13},{10,... | collective-permute-start | bytes 786440 | tf_op jit(solution)/shard_map/ppermute | solution.py:53
  3.7 1.6 %collective-permute-start.6 = (bf16[128,1024]{1,0:T(8,128)(2,1)}, bf16[128,1024]{1,0:T(8,128)(2,1)S(1)}, u32[]{:S(2)}, u32[]{:S(2)}) collective-permute-start(bf16[128,1024]{1,0:T(8,128)(2,1)} %refs_6_.1), channel_id=1, source_target_pairs={{0,4},{1,3},{2,6},{3,1},{4,0},{5,7},{6,2},{7,5},{8,12},{9,11},{10,... | collective-permute-start | bytes 786440 | tf_op jit(solution)/shard_map/ppermute | solution.py:53
  5.3 2.1 %open_up.1 = (bf16[8,1024]{1,0:T(8,128)(2,1)}, bf16[8,1024]{1,0:T(8,128)(2,1)}, bf16[128,128]{1,0:T(8,128)(2,1)}) custom-call(s32[2,16]{1,0:T(2,128)} %table_hbm.1, s32[2]{0:T(128)} %hit_hbm.1, bf16[32,8,1024]{2,1,0:T(8,128)(2,1)} %store_ref.1), custom_call_target="tpu_custom_call" | custom-call | tf_op jit(solution)/shard_map/open_up/pallas_call | solution.py:117
  7.4 2.7 %collective-permute-start.2 = (bf16[8,1024]{1,0:T(8,128)(2,1)}, bf16[8,1024]{1,0:T(8,128)(2,1)S(1)}, u32[]{:S(2)}, u32[]{:S(2)}) collective-permute-start(bf16[8,1024]{1,0:T(8,128)(2,1)} %get-tuple-element.18), channel_id=1, source_target_pairs={{0,8},{1,9},{2,10},{3,11},{4,12},{5,13},{6,14},{7,15},{8,0},{9,1},... | collective-permute-start | bytes 49160 | tf_op jit(solution)/shard_map/ppermute | solution.py:48
  10.1 0.5 %collective-permute-start.3 = (bf16[8,1024]{1,0:T(8,128)(2,1)}, bf16[8,1024]{1,0:T(8,128)(2,1)S(1)}, u32[]{:S(2)}, u32[]{:S(2)}) collective-permute-start(bf16[8,1024]{1,0:T(8,128)(2,1)} %get-tuple-element.16.refs_0_), channel_id=1, source_target_pairs={{0,2},{1,5},{2,0},{3,7},{4,6},{5,1},{6,4},{7,3},{8,10},{9,13},{10,... | collective-permute-start | bytes 49160 | tf_op jit(solution)/shard_map/ppermute | solution.py:53
  10.6 0.0 collective-permute-done.mate_ref.refs_1_.refs_7_
  10.6 1.3 %collective-permute-start.4 = (bf16[8,1024]{1,0:T(8,128)(2,1)}, bf16[8,1024]{1,0:T(8,128)(2,1)S(1)}, u32[]{:S(2)}, u32[]{:S(2)}) collective-permute-start(bf16[8,1024]{1,0:T(8,128)(2,1)} %get-tuple-element.18), channel_id=1, source_target_pairs={{0,10},{1,13},{2,8},{3,15},{4,14},{5,9},{6,12},{7,11},{8,2},{9,5},... | collective-permute-start | bytes 49160 | tf_op jit(solution)/shard_map/ppermute | solution.py:58
  11.9 0.5 %collective-permute-done.2.refs_1_ = bf16[8,1024]{1,0:T(8,128)(2,1)S(1)} collective-permute-done((bf16[8,1024]{1,0:T(8,128)(2,1)}, bf16[8,1024]{1,0:T(8,128)(2,1)S(1)}, u32[]{:S(2)}, u32[]{:S(2)}) %collective-permute-start.2) | collective-permute-done | bytes 16416 | tf_op jit(solution)/shard_map/ppermute | solution.py:48
  12.4 1.7 %collective-permute-done.3.refs_2_ = bf16[8,1024]{1,0:T(8,128)(2,1)S(1)} collective-permute-done((bf16[8,1024]{1,0:T(8,128)(2,1)}, bf16[8,1024]{1,0:T(8,128)(2,1)S(1)}, u32[]{:S(2)}, u32[]{:S(2)}) %collective-permute-start.3) | collective-permute-done | bytes 16416 | tf_op jit(solution)/shard_map/ppermute | solution.py:53
  14.0 0.0 collective-permute-done.1.block_ref
  14.0 2.4 %collective-permute-done.4.refs_3_ = bf16[8,1024]{1,0:T(8,128)(2,1)S(1)} collective-permute-done((bf16[8,1024]{1,0:T(8,128)(2,1)}, bf16[8,1024]{1,0:T(8,128)(2,1)S(1)}, u32[]{:S(2)}, u32[]{:S(2)}) %collective-permute-start.4) | collective-permute-done | bytes 16416 | tf_op jit(solution)/shard_map/ppermute | solution.py:58
  16.4 0.0 copy-start.3
  16.4 0.7 %copy-done.3 = bf16[8,1024]{1,0:T(8,128)(2,1)S(1)} copy-done((bf16[8,1024]{1,0:T(8,128)(2,1)S(1)}, bf16[8,1024]{1,0:T(8,128)(2,1)}, u32[]{:S(2)}) %copy-start.3) | copy-done | bytes 16408
  17.2 0.1 collective-permute-start.5
  17.3 0.5 %collective-permute-start.8 = (bf16[160,1024]{1,0:T(8,128)(2,1)S(1)}, bf16[160,1024]{1,0:T(8,128)(2,1)S(1)}, u32[]{:S(2)}, u32[]{:S(2)}) collective-permute-start(bf16[160,1024]{1,0:T(8,128)(2,1)S(1)} %pack.1.refs_0_.refs_2_.refs_8_), channel_id=1, source_target_pairs={{0,4},{1,3},{2,6},{3,1},{4,0},{5,7},{6,2},{7,5},{8,12},{9,11},{10,... | collective-permute-start | bytes 983048 | tf_op jit(solution)/shard_map/ppermute | solution.py:53
  17.7 0.0 collective-permute-done.6.refs_2_.refs_4_.refs_10_
  17.7 1.2 %collective-permute-start.7 = (bf16[128,1024]{1,0:T(8,128)(2,1)S(1)}, bf16[128,1024]{1,0:T(8,128)(2,1)S(1)}, u32[]{:S(2)}, u32[]{:S(2)}) collective-permute-start(bf16[128,1024]{1,0:T(8,128)(2,1)S(1)} %collective-permute-done.6.refs_2_.refs_4_.refs_10_), channel_id=1, source_target_pairs={{0,1},{1,0},{2,3},{3,2},{4,5},{5,4},{6,7},{7,6},{8,9},{9,8},{10,11... | collective-permute-start | bytes 786440 | tf_op jit(solution)/shard_map/ppermute | solution.py:48
  19.0 0.0 copy-start
  19.0 1.2 %copy-done = bf16[128,4096]{1,0:T(8,128)(2,1)S(1)} copy-done((bf16[128,4096]{1,0:T(8,128)(2,1)S(1)}, bf16[128,4096]{1,0:T(8,128)(2,1)}, u32[]{:S(2)}) %copy-start) | copy-done | bytes 1048600
  20.2 0.0 copy-start.1
  20.2 0.9 %copy-done.1 = bf16[128,1024]{1,0:T(8,128)(2,1)S(1)} copy-done((bf16[128,1024]{1,0:T(8,128)(2,1)S(1)}, bf16[128,1024]{1,0:T(8,128)(2,1)}, u32[]{:S(2)}) %copy-start.1) | copy-done | bytes 262168
  21.2 1.5 %attend_first.1 = (f32[4096,256]{1,0:T(8,128)S(1)}, bf16[4096,128]{1,0:T(8,128)(2,1)S(1)}) custom-call(bf16[128,4096]{1,0:T(8,128)(2,1)S(1)} %copy-done, bf16[128,1024]{1,0:T(8,128)(2,1)S(1)} %copy-done.1, bf16[128,1024]{1,0:T(8,128)(2,1)S(1)} %collective-permute-done.mate_ref.refs_1_.refs_7_), custom_call_target="tpu_custom_call" | custom-call | flops 1073741824 | bytes 2097152 | tf_op jit(solution)/shard_map/attend_first/pallas_call | solution.py:207
  22.6 0.0 collective-permute-done.7.refs_3_.refs_5_.refs_11_
  22.6 0.0 collective-permute-done.5.refs_1_.refs_3_.refs_9_
  22.6 0.0 copy-done.4
  22.6 1.0 %pick_for_owners.2 = (bf16[4,48,256]{2,1,0:T(8,128)(2,1)S(1)}, bf16[4,48,256]{2,1,0:T(8,128)(2,1)S(1)}) custom-call(s32[2,4]{1,0:T(2,128)S(1)} %copy-done.4, bf16[128,1024]{1,0:T(8,128)(2,1)S(1)} %copy-done.1, bf16[128,1024]{1,0:T(8,128)(2,1)S(1)} %collective-permute-done.mate_ref.refs_1_.refs_7_, bf16[160,1024]{1,0:T(8,128)(2,1)S(1)} %pack.1.refs_0_.refs_2_.refs_8_, ...), custom_call_target="tpu_custom_call" | custom-call | tf_op jit(solution)/shard_map/pick_for_owners/pallas_call | solution.py:418
  23.7 0.7 %collective-permute-done.8.refs_0_.refs_4_ = bf16[160,1024]{1,0:T(8,128)(2,1)S(1)} collective-permute-done((bf16[160,1024]{1,0:T(8,128)(2,1)S(1)}, bf16[160,1024]{1,0:T(8,128)(2,1)S(1)}, u32[]{:S(2)}, u32[]{:S(2)}) %collective-permute-start.8) | collective-permute-done | bytes 327712 | tf_op jit(solution)/shard_map/ppermute | solution.py:53
  24.4 0.0 collective-permute-start.9
  24.4 0.3 collective-permute-start.10
  24.7 0.0 copy-start.2
  24.7 2.8 %attend_more.1.mass_ref = f32[4096,256]{1,0:T(8,128)S(1)} custom-call(bf16[128,4096]{1,0:T(8,128)(2,1)S(1)} %copy-done, bf16[4096,128]{1,0:T(8,128)(2,1)S(1)} %get-tuple-element.14.shift_ref, f32[4096,256]{1,0:T(8,128)S(1)} %get-tuple-element.15.mass_ref, bf16[160,1024]{1,0:T(8,128)(2,1)S(1)} %pack.1.refs_0_.refs_2_.refs_8_, ...), custom_call_target="tpu_custom_call", output_to_operand_aliasing={{}: (2, {})} | custom-call | flops 2147483648 | bytes 2097152 | tf_op jit(solution)/shard_map/attend_more/pallas_call | solution.py:252
  27.5 0.0 collective-permute-done.9.refs_1_.refs_5_
  27.5 0.8 %pick_for_owners.3 = (bf16[4,16,256]{2,1,0:T(8,128)(2,1)S(1)}, bf16[4,16,256]{2,1,0:T(8,128)(2,1)S(1)}) custom-call(s32[2,4]{1,0:T(2,128)S(1)} %copy-done.4, bf16[160,1024]{1,0:T(8,128)(2,1)S(1)} %collective-permute-done.8.refs_0_.refs_4_, bf16[160,1024]{1,0:T(8,128)(2,1)S(1)} %collective-permute-done.9.refs_1_.refs_5_), custom_call_target="tpu_custom_call" | custom-call | tf_op jit(solution)/shard_map/pick_for_owners/pallas_call | solution.py:418
  28.3 2.7 %collective-permute-start.11 = (bf16[4,16,256]{2,1,0:T(8,128)(2,1)S(1)}, bf16[4,16,256]{2,1,0:T(8,128)(2,1)S(1)}, u32[]{:S(2)}, u32[]{:S(2)}) collective-permute-start(bf16[4,16,256]{2,1,0:T(8,128)(2,1)S(1)} %get-tuple-element.25), channel_id=1, source_target_pairs={{0,8},{1,9},{2,10},{3,11},{4,12},{5,13},{6,14},{7,15},{8,0},{9,1},... | collective-permute-start | bytes 98312 | tf_op jit(solution)/shard_map/ppermute | solution.py:48
  31.0 0.0 copy-done.2
  31.0 3.3 %attend_last.1 = bf16[128,4096]{1,0:T(8,128)(2,1)} custom-call(bf16[128,4096]{1,0:T(8,128)(2,1)S(1)} %copy-done, bf16[4096,128]{1,0:T(8,128)(2,1)S(1)} %get-tuple-element.14.shift_ref, f32[4096,256]{1,0:T(8,128)S(1)} %attend_more.1.mass_ref, bf16[128,128]{1,0:T(8,128)(2,1)S(1)} %copy-done.2, bf16[160,1024]{1,0:T(8,128)(2,1)S(1)} %collective-permute-done.8.refs_0_.refs_4_, ...), custom_call_target="tpu_custom_call" | custom-call | flops 1610612736 | bytes 2097152 | tf_op jit(solution)/shard_map/attend_last/pallas_call | solution.py:354
  34.3 0.0 collective-permute-done.10.refs_1_
  34.3 0.0 collective-permute-done.11.refs_3_
  34.4 0.7 %place.1 = bf16[1,4,128,256]{3,2,1,0:T(8,128)(2,1)} custom-call(bf16[4,48,256]{2,1,0:T(8,128)(2,1)S(1)} %get-tuple-element.23.refs_0_, bf16[4,48,256]{2,1,0:T(8,128)(2,1)S(1)} %collective-permute-done.10.refs_1_, bf16[4,16,256]{2,1,0:T(8,128)(2,1)S(1)} %get-tuple-element.24.refs_2_, bf16[4,16,256]{2,1,0:T(8,128)(2,1)S(1)} %collective-permute-done.11.refs_3_), custom_call_target="tpu_custom_call" | custom-call | tf_op jit(solution)/shard_map/place/pallas_call | solution.py:450
  (1 shorter events, 0.0 us)
Async XLA Ops:
  0.6 22.0 %copy-start.4 = (s32[2,4]{1,0:T(2,128)S(1)}, s32[2,4]{1,0:T(2,128)}, u32[]{:S(2)}) copy-start(s32[2,4]{1,0:T(2,128)} %offset_ref.3) | copy-start | bytes 100
  0.6 10.0 %collective-permute-start = (bf16[128,1024]{1,0:T(8,128)(2,1)}, bf16[128,1024]{1,0:T(8,128)(2,1)S(1)}, u32[]{:S(2)}, u32[]{:S(2)}) collective-permute-start(bf16[128,1024]{1,0:T(8,128)(2,1)} %refs_6_.1), channel_id=1, source_target_pairs={{0,1},{1,0},{2,3},{3,2},{4,5},{5,4},{6,7},{7,6},{8,9},{9,8},{10,11... | collective-permute-start | bytes 786440 | tf_op jit(solution)/shard_map/ppermute | solution.py:48
  1.2 12.9 %collective-permute-start.1 = (bf16[128,1024]{1,0:T(8,128)(2,1)}, bf16[128,1024]{1,0:T(8,128)(2,1)S(1)}, u32[]{:S(2)}, u32[]{:S(2)}) collective-permute-start(bf16[128,1024]{1,0:T(8,128)(2,1)} %refs_6_.1), channel_id=1, source_target_pairs={{0,2},{1,5},{2,0},{3,7},{4,6},{5,1},{6,4},{7,3},{8,10},{9,13},{10,... | collective-permute-start | bytes 786440 | tf_op jit(solution)/shard_map/ppermute | solution.py:53
  3.7 14.0 %collective-permute-start.6 = (bf16[128,1024]{1,0:T(8,128)(2,1)}, bf16[128,1024]{1,0:T(8,128)(2,1)S(1)}, u32[]{:S(2)}, u32[]{:S(2)}) collective-permute-start(bf16[128,1024]{1,0:T(8,128)(2,1)} %refs_6_.1), channel_id=1, source_target_pairs={{0,4},{1,3},{2,6},{3,1},{4,0},{5,7},{6,2},{7,5},{8,12},{9,11},{10,... | collective-permute-start | bytes 786440 | tf_op jit(solution)/shard_map/ppermute | solution.py:53
  7.4 4.9 %collective-permute-start.2 = (bf16[8,1024]{1,0:T(8,128)(2,1)}, bf16[8,1024]{1,0:T(8,128)(2,1)S(1)}, u32[]{:S(2)}, u32[]{:S(2)}) collective-permute-start(bf16[8,1024]{1,0:T(8,128)(2,1)} %get-tuple-element.18), channel_id=1, source_target_pairs={{0,8},{1,9},{2,10},{3,11},{4,12},{5,13},{6,14},{7,15},{8,0},{9,1},... | collective-permute-start | bytes 49160 | tf_op jit(solution)/shard_map/ppermute | solution.py:48
  10.1 3.9 %collective-permute-start.3 = (bf16[8,1024]{1,0:T(8,128)(2,1)}, bf16[8,1024]{1,0:T(8,128)(2,1)S(1)}, u32[]{:S(2)}, u32[]{:S(2)}) collective-permute-start(bf16[8,1024]{1,0:T(8,128)(2,1)} %get-tuple-element.16.refs_0_), channel_id=1, source_target_pairs={{0,2},{1,5},{2,0},{3,7},{4,6},{5,1},{6,4},{7,3},{8,10},{9,13},{10,... | collective-permute-start | bytes 49160 | tf_op jit(solution)/shard_map/ppermute | solution.py:53
  10.6 5.8 %collective-permute-start.4 = (bf16[8,1024]{1,0:T(8,128)(2,1)}, bf16[8,1024]{1,0:T(8,128)(2,1)S(1)}, u32[]{:S(2)}, u32[]{:S(2)}) collective-permute-start(bf16[8,1024]{1,0:T(8,128)(2,1)} %get-tuple-element.18), channel_id=1, source_target_pairs={{0,10},{1,13},{2,8},{3,15},{4,14},{5,9},{6,12},{7,11},{8,2},{9,5},... | collective-permute-start | bytes 49160 | tf_op jit(solution)/shard_map/ppermute | solution.py:58
  16.4 0.7 %copy-start.3 = (bf16[8,1024]{1,0:T(8,128)(2,1)S(1)}, bf16[8,1024]{1,0:T(8,128)(2,1)}, u32[]{:S(2)}) copy-start(bf16[8,1024]{1,0:T(8,128)(2,1)} %get-tuple-element.16.refs_0_) | copy-start | bytes 49156
  17.2 5.4 %collective-permute-start.5 = (bf16[160,1024]{1,0:T(8,128)(2,1)S(1)}, bf16[160,1024]{1,0:T(8,128)(2,1)S(1)}, u32[]{:S(2)}, u32[]{:S(2)}) collective-permute-start(bf16[160,1024]{1,0:T(8,128)(2,1)S(1)} %pack.1.refs_0_.refs_2_.refs_8_), channel_id=1, source_target_pairs={{0,1},{1,0},{2,3},{3,2},{4,5},{5,4},{6,7},{7,6},{8,9},{9,8},{10,11... | collective-permute-start | bytes 983048 | tf_op jit(solution)/shard_map/ppermute | solution.py:48
  17.3 7.1 %collective-permute-start.8 = (bf16[160,1024]{1,0:T(8,128)(2,1)S(1)}, bf16[160,1024]{1,0:T(8,128)(2,1)S(1)}, u32[]{:S(2)}, u32[]{:S(2)}) collective-permute-start(bf16[160,1024]{1,0:T(8,128)(2,1)S(1)} %pack.1.refs_0_.refs_2_.refs_8_), channel_id=1, source_target_pairs={{0,4},{1,3},{2,6},{3,1},{4,0},{5,7},{6,2},{7,5},{8,12},{9,11},{10,... | collective-permute-start | bytes 983048 | tf_op jit(solution)/shard_map/ppermute | solution.py:53
  17.7 4.9 %collective-permute-start.7 = (bf16[128,1024]{1,0:T(8,128)(2,1)S(1)}, bf16[128,1024]{1,0:T(8,128)(2,1)S(1)}, u32[]{:S(2)}, u32[]{:S(2)}) collective-permute-start(bf16[128,1024]{1,0:T(8,128)(2,1)S(1)} %collective-permute-done.6.refs_2_.refs_4_.refs_10_), channel_id=1, source_target_pairs={{0,1},{1,0},{2,3},{3,2},{4,5},{5,4},{6,7},{7,6},{8,9},{9,8},{10,11... | collective-permute-start | bytes 786440 | tf_op jit(solution)/shard_map/ppermute | solution.py:48
  19.0 1.2 %copy-start = (bf16[128,4096]{1,0:T(8,128)(2,1)S(1)}, bf16[128,4096]{1,0:T(8,128)(2,1)}, u32[]{:S(2)}) copy-start(bf16[128,4096]{1,0:T(8,128)(2,1)} %q_ref.5) | copy-start | bytes 3145732
  20.2 0.9 %copy-start.1 = (bf16[128,1024]{1,0:T(8,128)(2,1)S(1)}, bf16[128,1024]{1,0:T(8,128)(2,1)}, u32[]{:S(2)}) copy-start(bf16[128,1024]{1,0:T(8,128)(2,1)} %refs_6_.1) | copy-start | bytes 786436
  24.4 3.1 %collective-permute-start.9 = (bf16[160,1024]{1,0:T(8,128)(2,1)S(1)}, bf16[160,1024]{1,0:T(8,128)(2,1)S(1)}, u32[]{:S(2)}, u32[]{:S(2)}) collective-permute-start(bf16[160,1024]{1,0:T(8,128)(2,1)S(1)} %collective-permute-done.8.refs_0_.refs_4_), channel_id=1, source_target_pairs={{0,1},{1,0},{2,3},{3,2},{4,5},{5,4},{6,7},{7,6},{8,9},{9,8},{10,11... | collective-permute-start | bytes 983048 | tf_op jit(solution)/shard_map/ppermute | solution.py:48
  24.4 9.9 %collective-permute-start.10 = (bf16[4,48,256]{2,1,0:T(8,128)(2,1)S(1)}, bf16[4,48,256]{2,1,0:T(8,128)(2,1)S(1)}, u32[]{:S(2)}, u32[]{:S(2)}) collective-permute-start(bf16[4,48,256]{2,1,0:T(8,128)(2,1)S(1)} %get-tuple-element.21), channel_id=1, source_target_pairs={{0,8},{1,9},{2,10},{3,11},{4,12},{5,13},{6,14},{7,15},{8,0},{9,1},... | collective-permute-start | bytes 294920 | tf_op jit(solution)/shard_map/ppermute | solution.py:48
  24.7 6.3 %copy-start.2 = (bf16[128,128]{1,0:T(8,128)(2,1)S(1)}, bf16[128,128]{1,0:T(8,128)(2,1)}, u32[]{:S(2)}) copy-start(bf16[128,128]{1,0:T(8,128)(2,1)} %get-tuple-element.19.bias_ref) | copy-start | bytes 98308
  28.3 6.1 %collective-permute-start.11 = (bf16[4,16,256]{2,1,0:T(8,128)(2,1)S(1)}, bf16[4,16,256]{2,1,0:T(8,128)(2,1)S(1)}, u32[]{:S(2)}, u32[]{:S(2)}) collective-permute-start(bf16[4,16,256]{2,1,0:T(8,128)(2,1)S(1)} %get-tuple-element.25), channel_id=1, source_target_pairs={{0,8},{1,9},{2,10},{3,11},{4,12},{5,13},{6,14},{7,15},{8,0},{9,1},... | collective-permute-start | bytes 98312 | tf_op jit(solution)/shard_map/ppermute | solution.py:48

commit v4 on v3

--- a/solution.py
+++ b/solution.py
@@ -50,11 +50,6 @@
 
 def swap_by_core(value, orders, step):
     route = [(i, i ^ orders[i % 2][step]) for i in range(lax.axis_size("seq"))]
-    return lax.ppermute(value, "seq", route)
-
-
-def swap_wide(value, orders, bit):
-    route = [(i, i ^ bit ^ orders[i % 2][0]) for i in range(lax.axis_size("seq"))]
     return lax.ppermute(value, "seq", route)
 
 
@@ -133,23 +128,20 @@
     )(page_table, hit_tokens, kv_store)
 
 
-def pack_kernel(block_ref, *refs):
-    page_refs, out_ref = refs[:-1], refs[-1]
-    rows = block_ref.shape[0]
-    out_ref[:rows] = block_ref[...]
-    out_ref[rows:] = jnp.concatenate([ref[...] for ref in page_refs], axis=0)
-
-
-def pack(block, pages):
-    rows = block.shape[0] + sum(page.shape[0] for page in pages)
+def pack_kernel(*refs):
+    refs[-1][...] = jnp.concatenate([ref[...] for ref in refs[:-1]], axis=0)
+
+
+def pack(pages):
+    rows = sum(page.shape[0] for page in pages)
     return pl.pallas_call(
         pack_kernel,
-        out_shape=jax.ShapeDtypeStruct((rows, block.shape[1]), block.dtype),
-        in_specs=[IN_VMEM] * (1 + len(pages)),
+        out_shape=jax.ShapeDtypeStruct((rows, pages[0].shape[1]), pages[0].dtype),
+        in_specs=[IN_VMEM] * len(pages),
         out_specs=IN_VMEM,
         compiler_params=pltpu.CompilerParams(vmem_limit_bytes=SMALL_VMEM_BYTES),
         name="pack",
-    )(block, *pages)
+    )(*pages)
 
 
 def stack(refs, at):
@@ -271,7 +263,7 @@
     other_refs = refs[len(kinds) + page_count : -9]
     out_ref, kept_ref, wrong_ref, top_ref, denominator_ref, total_ref, block_ref, sems, sem = refs[-9:]
     held = 4 * PAGE
-    group = [(ref, 0, rows) for ref in block_refs] + [(ref, rows, held) for ref in page_refs]
+    group = [(ref, 0, rows) for ref in block_refs] + [(ref, 0, held) for ref in page_refs]
     biases = [block_bias(me, orders, kind, rows) for kind in kinds] + [bias_ref[...]]
     bias = jnp.concatenate(biases, axis=0)
     wrong_ref[...] = jnp.zeros_like(wrong_ref)
@@ -336,7 +328,7 @@
         for kind, ref in zip(kinds, block_refs):
             take(ref, 0, rows, block_bias(me, orders, kind, rows), False)
         for n, ref in enumerate(page_refs):
-            take(ref, rows, held, bias_ref[n * held : (n + 1) * held], False)
+            take(ref, 0, held, bias_ref[n * held : (n + 1) * held], False)
         for g in range(KVH):
             for n in range(GQ):
                 span = pl.ds((g * GQ + n) * rows, rows)
@@ -472,46 +464,38 @@
     first_hop = swap_by_core(suffix_kv, orders, 0)
     mate = swap(suffix_kv, 1)
     own_page, other_page, bias = open_up(devices, orders, places, page_table, hit_tokens, kv_store)
-    page_set = [
-        own_page,
-        swap(other_page, partner),
-        swap_by_core(own_page, orders, 0),
-        swap_wide(after(other_page, mate), orders, partner),
-    ]
+    partner_page = swap(after(other_page, mate), partner)
     mass, shift = attend_first(orders, queries, suffix_kv, mate)
-    held = [((), suffix_kv), ((0,), pack(first_hop, page_set))]
+    held = [((), suffix_kv), ((0,), after(first_hop, shift, partner_page))]
     for step in range(1, steps):
         held = held + [(path + (step,), swap_by_core(value, orders, step)) for path, value in held]
+    pair = pack([own_page, partner_page])
+    pair_hop = swap_by_core(pair, orders, 0)
+    page_held = [((), pack([pair, pair_hop]))]
+    for step in range(1, steps):
+        page_held = page_held + [(path + (step,), swap_by_core(value, orders, step)) for path, value in page_held]
 
     arrivals, pages = [], {}
-
-    def exchange(moved, *earlier):
-        for path, value in moved:
-            swapped_value = swap(after(value, *earlier) if earlier else value, 1)
-            arrivals.append([(("block", False, path), value), (("block", True, path), swapped_value)])
-            if path[0] == 0:
-                pages[(False, path[1:])], pages[(True, path[1:])] = value, swapped_value
-
-    def to_owners(batch, hops):
-        mine, theirs = pick_for_owners(devices, orders, owner_offset, rows, batch, hops)
-        spans.append(hops)
-        pieces.append((mine, swap(theirs, partner)))
-        return theirs
-
-    home = [(("own",), suffix_kv), (("block", True, ()), after(mate, shift))]
-    pieces, spans = [], []
+    for path, value in held[1:]:
+        value = after(value, shift) if len(path) == 2 else value
+        arrivals.append([(("block", False, path), value), (("block", True, path), swap(value, 1))])
+    home = [(("own",), suffix_kv), (("block", True, ()), mate)]
     if steps == 2 and (2 * rows // devices) % 16 == 0:
         near, across = orders[0], orders[0][0] ^ orders[0][1]
-        exchange(held[1:3])
-        sent = to_owners(home + arrivals[0] + arrivals[1], (0,) + near)
-        exchange(held[3:], sent)
-        to_owners(arrivals[2], (across,))
+        batches = [(home + arrivals[0] + arrivals[1], (0,) + near), (arrivals[2], (across,))]
     else:
-        exchange(held[1:])
-        to_owners(home + sum(arrivals, []), (None,))
-
+        batches = [(home + sum(arrivals, []), (None,))]
+    pieces, spans = [], []
+    for batch, hops in batches:
+        mine, theirs = pick_for_owners(devices, orders, owner_offset, rows, batch, hops)
+        pieces.append((mine, swap(theirs, partner)))
+        spans.append(hops)
+        if len(pieces) == 1:
+            mass, first_sent = after(mass, theirs), theirs
     for n in range(0, len(arrivals) - 1, 2):
         mass = attend_more(orders, queries, shift, mass, sum(arrivals[n : min(n + 2, len(arrivals) - 1)], []))
+    for path, value in page_held:
+        pages[(False, path)], pages[(True, path)] = value, swap(after(value, first_sent) if path else value, 1)
     attention_out = attend_last(
         orders,
         queries,

time: 35.4 us -> 33.7 us (0.952)
  waiting for transfers between devices: 5.29 us -> 2.7 us
  starting transfers between devices: 13.9 us -> 14.8 us
    ppermute x4 -> x5, starting transfers between devices: 5.14 us -> 7.54 us  [swap_by_core(): return lax.ppermute(value, 'seq', route)]
    ppermute x1 -> x0, waiting for transfers between devices: 2.39 us -> none  [swap_wide(): return lax.ppermute(value, 'seq', route)]
    ppermute x1 -> x0, starting transfers between devices: 1.26 us -> none  [swap_wide(): return lax.ppermute(value, 'seq', route)]
    ppermute x7 -> x9, waiting for transfers between devices: 0.47 us -> 0.02 us  [swap(): return lax.ppermute(value, 'seq', route)]
    ppermute x4 -> x5, waiting for transfers between devices: 2.43 us -> 2.68 us  [swap_by_core(): return lax.ppermute(value, 'seq', route)]
    ppermute x7 -> x9, starting transfers between devices: 7.49 us -> 7.25 us  [swap(): return lax.ppermute(value, 'seq', route)]
  transfers between devices with their start and end apart: 12 -> 14, of which waited for: 4 -> 1; matrix products, arithmetic and copies ran while one was open for 0% -> 0% of each run, Pallas kernels for 33% -> 34%
where the time goes in v4:
time: 33.7 us; the launch traced here: 33.4 us
  starting transfers between devices  14.8 us (44%)
  Pallas kernels  12.3 us (36%)
  local copies, waits for them, and re-layouts  2.9 us (9%)
  waiting for transfers between devices  2.7 us (8%)
  between operations  0.75 us (2%)
    ppermute x5, starting transfers between devices, swap_by_core(): return lax.ppermute(value, 'seq', route)  7.54 us
    ppermute x9, starting transfers between devices, swap(): return lax.ppermute(value, 'seq', route)  7.25 us
    pallas_call x1, Pallas kernels, attend_last(): pl.pallas_call(functools.partial(last_kernel, orders, tuple((kind for kin...  3.34 us
    unnamed x10, local copies, waits for them, and re-layouts  2.9 us
    pallas_call x1, Pallas kernels, attend_more(): pl.pallas_call(functools.partial(more_kernel, orders, tuple((kind for kin...  2.8 us
    ppermute x5, waiting for transfers between devices, swap_by_core(): return lax.ppermute(value, 'seq', route)  2.68 us
    pallas_call x1, Pallas kernels, open_up(): pl.pallas_call(functools.partial(open_kernel, devices, orders, places), o...  2.13 us
    pallas_call x2, Pallas kernels, pick_for_owners(): pl.pallas_call(functools.partial(owner_kernel, devices, orders, rows, tup...  1.78 us
  transfers between devices with their start and end apart: 14, of which 1 were waited for; matrix products, arithmetic and copies ran while one was open for 0% of the time, Pallas kernels for 34%

profile of v4, /device:TPU:0, one launch (start us, length us, event | category | flops | bytes accessed | tf_op | source)
XLA Modules:
  0.0 33.4 jit_solution(5458382374948018696)
XLA Ops:
  0.6 0.0 copy-start.4
  0.6 0.5 %collective-permute-start = (bf16[128,1024]{1,0:T(8,128)(2,1)}, bf16[128,1024]{1,0:T(8,128)(2,1)S(1)}, u32[]{:S(2)}, u32[]{:S(2)}) collective-permute-start(bf16[128,1024]{1,0:T(8,128)(2,1)} %refs_6_.1), channel_id=1, source_target_pairs={{0,1},{1,0},{2,3},{3,2},{4,5},{5,4},{6,7},{7,6},{8,9},{9,8},{10,11... | collective-permute-start | bytes 786440 | tf_op jit(solution)/shard_map/ppermute | solution.py:48
  1.2 2.6 %collective-permute-start.1 = (bf16[128,1024]{1,0:T(8,128)(2,1)}, bf16[128,1024]{1,0:T(8,128)(2,1)S(1)}, u32[]{:S(2)}, u32[]{:S(2)}) collective-permute-start(bf16[128,1024]{1,0:T(8,128)(2,1)} %refs_6_.1), channel_id=1, source_target_pairs={{0,2},{1,5},{2,0},{3,7},{4,6},{5,1},{6,4},{7,3},{8,10},{9,13},{10,... | collective-permute-start | bytes 786440 | tf_op jit(solution)/shard_map/ppermute | solution.py:53
  3.7 1.6 %collective-permute-start.4 = (bf16[128,1024]{1,0:T(8,128)(2,1)}, bf16[128,1024]{1,0:T(8,128)(2,1)S(1)}, u32[]{:S(2)}, u32[]{:S(2)}) collective-permute-start(bf16[128,1024]{1,0:T(8,128)(2,1)} %refs_6_.1), channel_id=1, source_target_pairs={{0,4},{1,3},{2,6},{3,1},{4,0},{5,7},{6,2},{7,5},{8,12},{9,11},{10,... | collective-permute-start | bytes 786440 | tf_op jit(solution)/shard_map/ppermute | solution.py:53
  5.3 2.1 %open_up.1 = (bf16[8,1024]{1,0:T(8,128)(2,1)}, bf16[8,1024]{1,0:T(8,128)(2,1)}, bf16[128,128]{1,0:T(8,128)(2,1)}) custom-call(s32[2,16]{1,0:T(2,128)} %table_hbm.1, s32[2]{0:T(128)} %hit_hbm.1, bf16[32,8,1024]{2,1,0:T(8,128)(2,1)} %store_ref.1), custom_call_target="tpu_custom_call" | custom-call | tf_op jit(solution)/shard_map/open_up/pallas_call | solution.py:112
  7.4 0.0 collective-permute-done.mate_ref.refs_1_.refs_7_
  7.4 2.7 %collective-permute-start.2 = (bf16[8,1024]{1,0:T(8,128)(2,1)}, bf16[8,1024]{1,0:T(8,128)(2,1)S(1)}, u32[]{:S(2)}, u32[]{:S(2)}) collective-permute-start(bf16[8,1024]{1,0:T(8,128)(2,1)} %get-tuple-element.19), channel_id=1, source_target_pairs={{0,8},{1,9},{2,10},{3,11},{4,12},{5,13},{6,14},{7,15},{8,0},{9,1},... | collective-permute-start | bytes 49160 | tf_op jit(solution)/shard_map/ppermute | solution.py:48
  10.1 0.0 copy-start
  10.1 1.2 %copy-done = bf16[128,4096]{1,0:T(8,128)(2,1)S(1)} copy-done((bf16[128,4096]{1,0:T(8,128)(2,1)S(1)}, bf16[128,4096]{1,0:T(8,128)(2,1)}, u32[]{:S(2)}) %copy-start) | copy-done | bytes 1048600
  11.3 0.0 copy-start.1
  11.3 0.9 %copy-done.1 = bf16[128,1024]{1,0:T(8,128)(2,1)S(1)} copy-done((bf16[128,1024]{1,0:T(8,128)(2,1)S(1)}, bf16[128,1024]{1,0:T(8,128)(2,1)}, u32[]{:S(2)}) %copy-start.1) | copy-done | bytes 262168
  12.3 1.5 %attend_first.1 = (f32[4096,256]{1,0:T(8,128)S(1)}, bf16[4096,128]{1,0:T(8,128)(2,1)S(1)}) custom-call(bf16[128,4096]{1,0:T(8,128)(2,1)S(1)} %copy-done, bf16[128,1024]{1,0:T(8,128)(2,1)S(1)} %copy-done.1, bf16[128,1024]{1,0:T(8,128)(2,1)S(1)} %collective-permute-done.mate_ref.refs_1_.refs_7_), custom_call_target="tpu_custom_call" | custom-call | flops 1073741824 | bytes 2097152 | tf_op jit(solution)/shard_map/attend_first/pallas_call | solution.py:199
  13.7 0.0 collective-permute-done.1.refs_2_.refs_0_.refs_8_
  13.7 0.0 collective-permute-done.2.refs_1_
  13.8 0.5 %collective-permute-start.6 = (bf16[128,1024]{1,0:T(8,128)(2,1)S(1)}, bf16[128,1024]{1,0:T(8,128)(2,1)S(1)}, u32[]{:S(2)}, u32[]{:S(2)}) collective-permute-start(bf16[128,1024]{1,0:T(8,128)(2,1)S(1)} %collective-permute-done.1.refs_2_.refs_0_.refs_8_), channel_id=1, source_target_pairs={{0,4},{1,3},{2,6},{3,1},{4,0},{5,7},{6,2},{7,5},{8,12},{9,11},{10,... | collective-permute-start | bytes 786440 | tf_op jit(solution)/shard_map/ppermute | solution.py:53
  14.3 0.0 collective-permute-done.4.refs_4_.refs_2_.refs_10_
  14.3 0.0 collective-permute-start.5
  14.3 0.5 %collective-permute-start.3 = (bf16[128,1024]{1,0:T(8,128)(2,1)S(1)}, bf16[128,1024]{1,0:T(8,128)(2,1)S(1)}, u32[]{:S(2)}, u32[]{:S(2)}) collective-permute-start(bf16[128,1024]{1,0:T(8,128)(2,1)S(1)} %collective-permute-done.1.refs_2_.refs_0_.refs_8_), channel_id=1, source_target_pairs={{0,1},{1,0},{2,3},{3,2},{4,5},{5,4},{6,7},{7,6},{8,9},{9,8},{10,11... | collective-permute-start | bytes 786440 | tf_op jit(solution)/shard_map/ppermute | solution.py:48
  14.8 0.0 copy-start.3
  14.8 0.7 %copy-done.3 = bf16[8,1024]{1,0:T(8,128)(2,1)S(1)} copy-done((bf16[8,1024]{1,0:T(8,128)(2,1)S(1)}, bf16[8,1024]{1,0:T(8,128)(2,1)}, u32[]{:S(2)}) %copy-start.3) | copy-done | bytes 16408
  15.5 1.3 %collective-permute-start.8 = (bf16[16,1024]{1,0:T(8,128)(2,1)S(1)}, bf16[16,1024]{1,0:T(8,128)(2,1)S(1)}, u32[]{:S(2)}, u32[]{:S(2)}) collective-permute-start(bf16[16,1024]{1,0:T(8,128)(2,1)S(1)} %pack.2.refs_0_), channel_id=1, source_target_pairs={{0,2},{1,5},{2,0},{3,7},{4,6},{5,1},{6,4},{7,3},{8,10},{9,13},{10,... | collective-permute-start | bytes 98312 | tf_op jit(solution)/shard_map/ppermute | solution.py:53
  16.8 2.7 %collective-permute-done.8.refs_1_ = bf16[16,1024]{1,0:T(8,128)(2,1)S(1)} collective-permute-done((bf16[16,1024]{1,0:T(8,128)(2,1)S(1)}, bf16[16,1024]{1,0:T(8,128)(2,1)S(1)}, u32[]{:S(2)}, u32[]{:S(2)}) %collective-permute-start.8) | collective-permute-done | bytes 32800 | tf_op jit(solution)/shard_map/ppermute | solution.py:53
  19.5 1.6 %collective-permute-start.10 = (bf16[32,1024]{1,0:T(8,128)(2,1)S(1)}, bf16[32,1024]{1,0:T(8,128)(2,1)S(1)}, u32[]{:S(2)}, u32[]{:S(2)}) collective-permute-start(bf16[32,1024]{1,0:T(8,128)(2,1)S(1)} %pack.3.refs_2_), channel_id=1, source_target_pairs={{0,4},{1,3},{2,6},{3,1},{4,0},{5,7},{6,2},{7,5},{8,12},{9,11},{10,... | collective-permute-start | bytes 196616 | tf_op jit(solution)/shard_map/ppermute | solution.py:53
  21.1 0.0 collective-permute-done.6.refs_0_
  21.1 0.0 collective-permute-start.7
  21.1 0.5 %collective-permute-start.9 = (bf16[32,1024]{1,0:T(8,128)(2,1)S(1)}, bf16[32,1024]{1,0:T(8,128)(2,1)S(1)}, u32[]{:S(2)}, u32[]{:S(2)}) collective-permute-start(bf16[32,1024]{1,0:T(8,128)(2,1)S(1)} %pack.3.refs_2_), channel_id=1, source_target_pairs={{0,1},{1,0},{2,3},{3,2},{4,5},{5,4},{6,7},{7,6},{8,9},{9,8},{10,11... | collective-permute-start | bytes 196616 | tf_op jit(solution)/shard_map/ppermute | solution.py:48
  21.6 0.0 collective-permute-done.5.refs_5_.refs_3_.refs_11_
  21.6 0.0 collective-permute-done.3.refs_3_.refs_1_.refs_9_
  21.6 0.0 copy-done.4
  21.6 1.0 %pick_for_owners.2 = (bf16[4,48,256]{2,1,0:T(8,128)(2,1)S(1)}, bf16[4,48,256]{2,1,0:T(8,128)(2,1)S(1)}) custom-call(s32[2,4]{1,0:T(2,128)S(1)} %copy-done.4, bf16[128,1024]{1,0:T(8,128)(2,1)S(1)} %copy-done.1, bf16[128,1024]{1,0:T(8,128)(2,1)S(1)} %collective-permute-done.mate_ref.refs_1_.refs_7_, ...), custom_call_target="tpu_custom_call" | custom-call | tf_op jit(solution)/shard_map/pick_for_owners/pallas_call | solution.py:410
  22.6 1.2 %collective-permute-start.12 = (bf16[4,48,256]{2,1,0:T(8,128)(2,1)S(1)}, bf16[4,48,256]{2,1,0:T(8,128)(2,1)S(1)}, u32[]{:S(2)}, u32[]{:S(2)}) collective-permute-start(bf16[4,48,256]{2,1,0:T(8,128)(2,1)S(1)} %get-tuple-element.21), channel_id=1, source_target_pairs={{0,8},{1,9},{2,10},{3,11},{4,12},{5,13},{6,14},{7,15},{8,0},{9,1},... | collective-permute-start | bytes 294920 | tf_op jit(solution)/shard_map/ppermute | solution.py:48
  23.8 0.0 copy-start.2
  23.8 0.0 collective-permute-done.10.refs_4_
  23.8 0.0 collective-permute-start.11
  23.8 2.8 %attend_more.1.mass_ref = f32[4096,256]{1,0:T(8,128)S(1)} custom-call(bf16[128,4096]{1,0:T(8,128)(2,1)S(1)} %copy-done, bf16[4096,128]{1,0:T(8,128)(2,1)S(1)} %get-tuple-element.16.shift_ref, f32[4096,256]{1,0:T(8,128)S(1)} %get-tuple-element.22.mass_ref, ...), custom_call_target="tpu_custom_call", output_to_operand_aliasing={{}: (2, {})} | custom-call | flops 2147483648 | bytes 2097152 | tf_op jit(solution)/shard_map/attend_more/pallas_call | solution.py:244
  26.6 0.0 collective-permute-done.7.refs_1_
  26.6 0.8 %pick_for_owners.3 = (bf16[4,16,256]{2,1,0:T(8,128)(2,1)S(1)}, bf16[4,16,256]{2,1,0:T(8,128)(2,1)S(1)}) custom-call(s32[2,4]{1,0:T(2,128)S(1)} %copy-done.4, bf16[128,1024]{1,0:T(8,128)(2,1)S(1)} %collective-permute-done.6.refs_0_, bf16[128,1024]{1,0:T(8,128)(2,1)S(1)} %collective-permute-done.7.refs_1_), custom_call_target="tpu_custom_call" | custom-call | tf_op jit(solution)/shard_map/pick_for_owners/pallas_call | solution.py:410
  27.4 1.9 %collective-permute-start.13 = (bf16[4,16,256]{2,1,0:T(8,128)(2,1)S(1)}, bf16[4,16,256]{2,1,0:T(8,128)(2,1)S(1)}, u32[]{:S(2)}, u32[]{:S(2)}) collective-permute-start(bf16[4,16,256]{2,1,0:T(8,128)(2,1)S(1)} %get-tuple-element.29), channel_id=1, source_target_pairs={{0,8},{1,9},{2,10},{3,11},{4,12},{5,13},{6,14},{7,15},{8,0},{9,1},... | collective-permute-start | bytes 98312 | tf_op jit(solution)/shard_map/ppermute | solution.py:48
  29.3 0.0 collective-permute-done.9.refs_3_
  29.3 0.0 collective-permute-done.11.refs_5_
  29.3 0.0 copy-done.2
  29.3 3.3 %attend_last.1 = bf16[128,4096]{1,0:T(8,128)(2,1)} custom-call(bf16[128,4096]{1,0:T(8,128)(2,1)S(1)} %copy-done, bf16[4096,128]{1,0:T(8,128)(2,1)S(1)} %get-tuple-element.16.shift_ref, f32[4096,256]{1,0:T(8,128)S(1)} %attend_more.1.mass_ref, bf16[128,128]{1,0:T(8,128)(2,1)S(1)} %copy-done.2, bf16[128,1024]{1,0:T(8,128)(2,1)S(1)} %collective-permute-done.6.refs_0_, ...), custom_call_target="tpu_custom_call" | custom-call | flops 1610612736 | bytes 2097152 | tf_op jit(solution)/shard_map/attend_last/pallas_call | solution.py:346
  32.6 0.0 collective-permute-done.12.refs_1_
  32.6 0.0 collective-permute-done.13.refs_3_
  32.7 0.7 %place.1 = bf16[1,4,128,256]{3,2,1,0:T(8,128)(2,1)} custom-call(bf16[4,48,256]{2,1,0:T(8,128)(2,1)S(1)} %get-tuple-element.27.refs_0_, bf16[4,48,256]{2,1,0:T(8,128)(2,1)S(1)} %collective-permute-done.12.refs_1_, bf16[4,16,256]{2,1,0:T(8,128)(2,1)S(1)} %get-tuple-element.28.refs_2_, bf16[4,16,256]{2,1,0:T(8,128)(2,1)S(1)} %collective-permute-done.13.refs_3_), custom_call_target="tpu_custom_call" | custom-call | tf_op jit(solution)/shard_map/place/pallas_call | solution.py:442
  (2 shorter events, 0.0 us)
Async XLA Ops:
  0.6 21.0 %copy-start.4 = (s32[2,4]{1,0:T(2,128)S(1)}, s32[2,4]{1,0:T(2,128)}, u32[]{:S(2)}) copy-start(s32[2,4]{1,0:T(2,128)} %offset_ref.3) | copy-start | bytes 100
  0.6 6.8 %collective-permute-start = (bf16[128,1024]{1,0:T(8,128)(2,1)}, bf16[128,1024]{1,0:T(8,128)(2,1)S(1)}, u32[]{:S(2)}, u32[]{:S(2)}) collective-permute-start(bf16[128,1024]{1,0:T(8,128)(2,1)} %refs_6_.1), channel_id=1, source_target_pairs={{0,1},{1,0},{2,3},{3,2},{4,5},{5,4},{6,7},{7,6},{8,9},{9,8},{10,11... | collective-permute-start | bytes 786440 | tf_op jit(solution)/shard_map/ppermute | solution.py:48
  1.2 12.6 %collective-permute-start.1 = (bf16[128,1024]{1,0:T(8,128)(2,1)}, bf16[128,1024]{1,0:T(8,128)(2,1)S(1)}, u32[]{:S(2)}, u32[]{:S(2)}) collective-permute-start(bf16[128,1024]{1,0:T(8,128)(2,1)} %refs_6_.1), channel_id=1, source_target_pairs={{0,2},{1,5},{2,0},{3,7},{4,6},{5,1},{6,4},{7,3},{8,10},{9,13},{10,... | collective-permute-start | bytes 786440 | tf_op jit(solution)/shard_map/ppermute | solution.py:53
  3.7 10.6 %collective-permute-start.4 = (bf16[128,1024]{1,0:T(8,128)(2,1)}, bf16[128,1024]{1,0:T(8,128)(2,1)S(1)}, u32[]{:S(2)}, u32[]{:S(2)}) collective-permute-start(bf16[128,1024]{1,0:T(8,128)(2,1)} %refs_6_.1), channel_id=1, source_target_pairs={{0,4},{1,3},{2,6},{3,1},{4,0},{5,7},{6,2},{7,5},{8,12},{9,11},{10,... | collective-permute-start | bytes 786440 | tf_op jit(solution)/shard_map/ppermute | solution.py:53
  7.4 6.3 %collective-permute-start.2 = (bf16[8,1024]{1,0:T(8,128)(2,1)}, bf16[8,1024]{1,0:T(8,128)(2,1)S(1)}, u32[]{:S(2)}, u32[]{:S(2)}) collective-permute-start(bf16[8,1024]{1,0:T(8,128)(2,1)} %get-tuple-element.19), channel_id=1, source_target_pairs={{0,8},{1,9},{2,10},{3,11},{4,12},{5,13},{6,14},{7,15},{8,0},{9,1},... | collective-permute-start | bytes 49160 | tf_op jit(solution)/shard_map/ppermute | solution.py:48
  10.1 1.2 %copy-start = (bf16[128,4096]{1,0:T(8,128)(2,1)S(1)}, bf16[128,4096]{1,0:T(8,128)(2,1)}, u32[]{:S(2)}) copy-start(bf16[128,4096]{1,0:T(8,128)(2,1)} %q_ref.5) | copy-start | bytes 3145732
  11.3 0.9 %copy-start.1 = (bf16[128,1024]{1,0:T(8,128)(2,1)S(1)}, bf16[128,1024]{1,0:T(8,128)(2,1)}, u32[]{:S(2)}) copy-start(bf16[128,1024]{1,0:T(8,128)(2,1)} %refs_6_.1) | copy-start | bytes 786436
  13.8 7.3 %collective-permute-start.6 = (bf16[128,1024]{1,0:T(8,128)(2,1)S(1)}, bf16[128,1024]{1,0:T(8,128)(2,1)S(1)}, u32[]{:S(2)}, u32[]{:S(2)}) collective-permute-start(bf16[128,1024]{1,0:T(8,128)(2,1)S(1)} %collective-permute-done.1.refs_2_.refs_0_.refs_8_), channel_id=1, source_target_pairs={{0,4},{1,3},{2,6},{3,1},{4,0},{5,7},{6,2},{7,5},{8,12},{9,11},{10,... | collective-permute-start | bytes 786440 | tf_op jit(solution)/shard_map/ppermute | solution.py:53
  14.3 7.3 %collective-permute-start.5 = (bf16[128,1024]{1,0:T(8,128)(2,1)S(1)}, bf16[128,1024]{1,0:T(8,128)(2,1)S(1)}, u32[]{:S(2)}, u32[]{:S(2)}) collective-permute-start(bf16[128,1024]{1,0:T(8,128)(2,1)S(1)} %collective-permute-done.4.refs_4_.refs_2_.refs_10_), channel_id=1, source_target_pairs={{0,1},{1,0},{2,3},{3,2},{4,5},{5,4},{6,7},{7,6},{8,9},{9,8},{10,11... | collective-permute-start | bytes 786440 | tf_op jit(solution)/shard_map/ppermute | solution.py:48
  14.3 7.3 %collective-permute-start.3 = (bf16[128,1024]{1,0:T(8,128)(2,1)S(1)}, bf16[128,1024]{1,0:T(8,128)(2,1)S(1)}, u32[]{:S(2)}, u32[]{:S(2)}) collective-permute-start(bf16[128,1024]{1,0:T(8,128)(2,1)S(1)} %collective-permute-done.1.refs_2_.refs_0_.refs_8_), channel_id=1, source_target_pairs={{0,1},{1,0},{2,3},{3,2},{4,5},{5,4},{6,7},{7,6},{8,9},{9,8},{10,11... | collective-permute-start | bytes 786440 | tf_op jit(solution)/shard_map/ppermute | solution.py:48
  14.8 0.7 %copy-start.3 = (bf16[8,1024]{1,0:T(8,128)(2,1)S(1)}, bf16[8,1024]{1,0:T(8,128)(2,1)}, u32[]{:S(2)}) copy-start(bf16[8,1024]{1,0:T(8,128)(2,1)} %get-tuple-element.25.refs_0_) | copy-start | bytes 49156
  15.5 4.0 %collective-permute-start.8 = (bf16[16,1024]{1,0:T(8,128)(2,1)S(1)}, bf16[16,1024]{1,0:T(8,128)(2,1)S(1)}, u32[]{:S(2)}, u32[]{:S(2)}) collective-permute-start(bf16[16,1024]{1,0:T(8,128)(2,1)S(1)} %pack.2.refs_0_), channel_id=1, source_target_pairs={{0,2},{1,5},{2,0},{3,7},{4,6},{5,1},{6,4},{7,3},{8,10},{9,13},{10,... | collective-permute-start | bytes 98312 | tf_op jit(solution)/shard_map/ppermute | solution.py:53
  19.5 4.3 %collective-permute-start.10 = (bf16[32,1024]{1,0:T(8,128)(2,1)S(1)}, bf16[32,1024]{1,0:T(8,128)(2,1)S(1)}, u32[]{:S(2)}, u32[]{:S(2)}) collective-permute-start(bf16[32,1024]{1,0:T(8,128)(2,1)S(1)} %pack.3.refs_2_), channel_id=1, source_target_pairs={{0,4},{1,3},{2,6},{3,1},{4,0},{5,7},{6,2},{7,5},{8,12},{9,11},{10,... | collective-permute-start | bytes 196616 | tf_op jit(solution)/shard_map/ppermute | solution.py:53
  21.1 5.6 %collective-permute-start.7 = (bf16[128,1024]{1,0:T(8,128)(2,1)S(1)}, bf16[128,1024]{1,0:T(8,128)(2,1)S(1)}, u32[]{:S(2)}, u32[]{:S(2)}) collective-permute-start(bf16[128,1024]{1,0:T(8,128)(2,1)S(1)} %collective-permute-done.6.refs_0_), channel_id=1, source_target_pairs={{0,1},{1,0},{2,3},{3,2},{4,5},{5,4},{6,7},{7,6},{8,9},{9,8},{10,11... | collective-permute-start | bytes 786440 | tf_op jit(solution)/shard_map/ppermute | solution.py:48
  21.1 8.2 %collective-permute-start.9 = (bf16[32,1024]{1,0:T(8,128)(2,1)S(1)}, bf16[32,1024]{1,0:T(8,128)(2,1)S(1)}, u32[]{:S(2)}, u32[]{:S(2)}) collective-permute-start(bf16[32,1024]{1,0:T(8,128)(2,1)S(1)} %pack.3.refs_2_), channel_id=1, source_target_pairs={{0,1},{1,0},{2,3},{3,2},{4,5},{5,4},{6,7},{7,6},{8,9},{9,8},{10,11... | collective-permute-start | bytes 196616 | tf_op jit(solution)/shard_map/ppermute | solution.py:48
  22.6 10.0 %collective-permute-start.12 = (bf16[4,48,256]{2,1,0:T(8,128)(2,1)S(1)}, bf16[4,48,256]{2,1,0:T(8,128)(2,1)S(1)}, u32[]{:S(2)}, u32[]{:S(2)}) collective-permute-start(bf16[4,48,256]{2,1,0:T(8,128)(2,1)S(1)} %get-tuple-element.21), channel_id=1, source_target_pairs={{0,8},{1,9},{2,10},{3,11},{4,12},{5,13},{6,14},{7,15},{8,0},{9,1},... | collective-permute-start | bytes 294920 | tf_op jit(solution)/shard_map/ppermute | solution.py:48
  23.8 5.5 %copy-start.2 = (bf16[128,128]{1,0:T(8,128)(2,1)S(1)}, bf16[128,128]{1,0:T(8,128)(2,1)}, u32[]{:S(2)}) copy-start(bf16[128,128]{1,0:T(8,128)(2,1)} %get-tuple-element.23.bias_ref) | copy-start | bytes 98308
  23.8 5.5 %collective-permute-start.11 = (bf16[32,1024]{1,0:T(8,128)(2,1)S(1)}, bf16[32,1024]{1,0:T(8,128)(2,1)S(1)}, u32[]{:S(2)}, u32[]{:S(2)}) collective-permute-start(bf16[32,1024]{1,0:T(8,128)(2,1)S(1)} %collective-permute-done.10.refs_4_), channel_id=1, source_target_pairs={{0,1},{1,0},{2,3},{3,2},{4,5},{5,4},{6,7},{7,6},{8,9},{9,8},{10,11... | collective-permute-start | bytes 196616 | tf_op jit(solution)/shard_map/ppermute | solution.py:48
  27.4 5.2 %collective-permute-start.13 = (bf16[4,16,256]{2,1,0:T(8,128)(2,1)S(1)}, bf16[4,16,256]{2,1,0:T(8,128)(2,1)S(1)}, u32[]{:S(2)}, u32[]{:S(2)}) collective-permute-start(bf16[4,16,256]{2,1,0:T(8,128)(2,1)S(1)} %get-tuple-element.29), channel_id=1, source_target_pairs={{0,8},{1,9},{2,10},{3,11},{4,12},{5,13},{6,14},{7,15},{8,0},{9,1},... | collective-permute-start | bytes 98312 | tf_op jit(solution)/shard_map/ppermute | solution.py:48

commit v5 on v4

--- a/solution.py
+++ b/solution.py
@@ -471,9 +471,6 @@
         held = held + [(path + (step,), swap_by_core(value, orders, step)) for path, value in held]
     pair = pack([own_page, partner_page])
     pair_hop = swap_by_core(pair, orders, 0)
-    page_held = [((), pack([pair, pair_hop]))]
-    for step in range(1, steps):
-        page_held = page_held + [(path + (step,), swap_by_core(value, orders, step)) for path, value in page_held]
 
     arrivals, pages = [], {}
     for path, value in held[1:]:
@@ -492,6 +489,9 @@
         spans.append(hops)
         if len(pieces) == 1:
             mass, first_sent = after(mass, theirs), theirs
+    page_held = [((), pack([pair, after(pair_hop, first_sent)]))]
+    for step in range(1, steps):
+        page_held = page_held + [(path + (step,), swap_by_core(value, orders, step)) for path, value in page_held]
     for n in range(0, len(arrivals) - 1, 2):
         mass = attend_more(orders, queries, shift, mass, sum(arrivals[n : min(n + 2, len(arrivals) - 1)], []))
     for path, value in page_held:

time: 33.7 us -> 33.7 us (level)
  starting transfers between devices: 14.8 us -> 13.3 us
  waiting for transfers between devices: 2.7 us -> 4.2 us
    ppermute x5, waiting for transfers between devices: 2.68 us -> 3.99 us  [swap_by_core(): return lax.ppermute(value, 'seq', route)]
    ppermute x9, starting transfers between devices: 7.25 us -> 6.46 us  [swap(): return lax.ppermute(value, 'seq', route)]
    ppermute x5, starting transfers between devices: 7.54 us -> 6.81 us  [swap_by_core(): return lax.ppermute(value, 'seq', route)]
  transfers between devices with their start and end apart: 14 -> 14, of which waited for: 1 -> 3; matrix products, arithmetic and copies ran while one was open for 0% -> 0% of each run, Pallas kernels for 34% -> 34%
where the time goes in v5:
time: 33.7 us; the launch traced here: 33.4 us
  starting transfers between devices  13.3 us (39%)
  Pallas kernels  12.2 us (36%)
  waiting for transfers between devices  4.2 us (12%)
  local copies, waits for them, and re-layouts  2.9 us (9%)
  between operations  0.76 us (2%)
    ppermute x5, starting transfers between devices, swap_by_core(): return lax.ppermute(value, 'seq', route)  6.81 us
    ppermute x9, starting transfers between devices, swap(): return lax.ppermute(value, 'seq', route)  6.46 us
    ppermute x5, waiting for transfers between devices, swap_by_core(): return lax.ppermute(value, 'seq', route)  3.99 us
    pallas_call x1, Pallas kernels, attend_last(): pl.pallas_call(functools.partial(last_kernel, orders, tuple((kind for kin...  3.34 us
    unnamed x10, local copies, waits for them, and re-layouts  2.9 us
    pallas_call x1, Pallas kernels, attend_more(): pl.pallas_call(functools.partial(more_kernel, orders, tuple((kind for kin...  2.8 us
    pallas_call x1, Pallas kernels, open_up(): pl.pallas_call(functools.partial(open_kernel, devices, orders, places), o...  2.13 us
    pallas_call x2, Pallas kernels, pick_for_owners(): pl.pallas_call(functools.partial(owner_kernel, devices, orders, rows, tup...  1.78 us
  transfers between devices with their start and end apart: 14, of which 3 were waited for; matrix products, arithmetic and copies ran while one was open for 0% of the time, Pallas kernels for 34%

profile of v5, /device:TPU:0, one launch (start us, length us, event | category | flops | bytes accessed | tf_op | source)
XLA Modules:
  0.0 33.4 jit_solution(9693758983663059408)
XLA Ops:
  0.6 0.0 copy-start.4
  0.6 0.5 %collective-permute-start = (bf16[128,1024]{1,0:T(8,128)(2,1)}, bf16[128,1024]{1,0:T(8,128)(2,1)S(1)}, u32[]{:S(2)}, u32[]{:S(2)}) collective-permute-start(bf16[128,1024]{1,0:T(8,128)(2,1)} %refs_6_.1), channel_id=1, source_target_pairs={{0,1},{1,0},{2,3},{3,2},{4,5},{5,4},{6,7},{7,6},{8,9},{9,8},{10,11... | collective-permute-start | bytes 786440 | tf_op jit(solution)/shard_map/ppermute | solution.py:48
  1.2 2.7 %collective-permute-start.4 = (bf16[128,1024]{1,0:T(8,128)(2,1)}, bf16[128,1024]{1,0:T(8,128)(2,1)S(1)}, u32[]{:S(2)}, u32[]{:S(2)}) collective-permute-start(bf16[128,1024]{1,0:T(8,128)(2,1)} %refs_6_.1), channel_id=1, source_target_pairs={{0,4},{1,3},{2,6},{3,1},{4,0},{5,7},{6,2},{7,5},{8,12},{9,11},{10,... | collective-permute-start | bytes 786440 | tf_op jit(solution)/shard_map/ppermute | solution.py:53
  3.8 1.5 %collective-permute-start.1 = (bf16[128,1024]{1,0:T(8,128)(2,1)}, bf16[128,1024]{1,0:T(8,128)(2,1)S(1)}, u32[]{:S(2)}, u32[]{:S(2)}) collective-permute-start(bf16[128,1024]{1,0:T(8,128)(2,1)} %refs_6_.1), channel_id=1, source_target_pairs={{0,2},{1,5},{2,0},{3,7},{4,6},{5,1},{6,4},{7,3},{8,10},{9,13},{10,... | collective-permute-start | bytes 786440 | tf_op jit(solution)/shard_map/ppermute | solution.py:53
  5.3 2.1 %open_up.1 = (bf16[8,1024]{1,0:T(8,128)(2,1)}, bf16[8,1024]{1,0:T(8,128)(2,1)}, bf16[128,128]{1,0:T(8,128)(2,1)}) custom-call(s32[2,16]{1,0:T(2,128)} %table_hbm.1, s32[2]{0:T(128)} %hit_hbm.1, bf16[32,8,1024]{2,1,0:T(8,128)(2,1)} %store_ref.1), custom_call_target="tpu_custom_call" | custom-call | tf_op jit(solution)/shard_map/open_up/pallas_call | solution.py:112
  7.4 0.0 collective-permute-done.mate_ref.refs_1_.refs_7_
  7.4 2.7 %collective-permute-start.2 = (bf16[8,1024]{1,0:T(8,128)(2,1)}, bf16[8,1024]{1,0:T(8,128)(2,1)S(1)}, u32[]{:S(2)}, u32[]{:S(2)}) collective-permute-start(bf16[8,1024]{1,0:T(8,128)(2,1)} %get-tuple-element.20), channel_id=1, source_target_pairs={{0,8},{1,9},{2,10},{3,11},{4,12},{5,13},{6,14},{7,15},{8,0},{9,1},... | collective-permute-start | bytes 49160 | tf_op jit(solution)/shard_map/ppermute | solution.py:48
  10.1 0.0 copy-start
  10.1 1.2 %copy-done = bf16[128,4096]{1,0:T(8,128)(2,1)S(1)} copy-done((bf16[128,4096]{1,0:T(8,128)(2,1)S(1)}, bf16[128,4096]{1,0:T(8,128)(2,1)}, u32[]{:S(2)}) %copy-start) | copy-done | bytes 1048600
  11.3 0.0 copy-start.1
  11.3 0.9 %copy-done.1 = bf16[128,1024]{1,0:T(8,128)(2,1)S(1)} copy-done((bf16[128,1024]{1,0:T(8,128)(2,1)S(1)}, bf16[128,1024]{1,0:T(8,128)(2,1)}, u32[]{:S(2)}) %copy-start.1) | copy-done | bytes 262168
  12.3 1.5 %attend_first.1 = (f32[4096,256]{1,0:T(8,128)S(1)}, bf16[4096,128]{1,0:T(8,128)(2,1)S(1)}) custom-call(bf16[128,4096]{1,0:T(8,128)(2,1)S(1)} %copy-done, bf16[128,1024]{1,0:T(8,128)(2,1)S(1)} %copy-done.1, bf16[128,1024]{1,0:T(8,128)(2,1)S(1)} %collective-permute-done.mate_ref.refs_1_.refs_7_), custom_call_target="tpu_custom_call" | custom-call | flops 1073741824 | bytes 2097152 | tf_op jit(solution)/shard_map/attend_first/pallas_call | solution.py:199
  13.7 0.0 collective-permute-done.4.refs_4_.refs_2_.refs_10_
  13.7 0.1 collective-permute-start.5
  13.8 0.0 collective-permute-done.1.refs_2_.refs_0_.refs_8_
  13.8 0.0 collective-permute-done.2.refs_1_
  13.8 0.5 %collective-permute-start.3 = (bf16[128,1024]{1,0:T(8,128)(2,1)S(1)}, bf16[128,1024]{1,0:T(8,128)(2,1)S(1)}, u32[]{:S(2)}, u32[]{:S(2)}) collective-permute-start(bf16[128,1024]{1,0:T(8,128)(2,1)S(1)} %collective-permute-done.1.refs_2_.refs_0_.refs_8_), channel_id=1, source_target_pairs={{0,1},{1,0},{2,3},{3,2},{4,5},{5,4},{6,7},{7,6},{8,9},{9,8},{10,11... | collective-permute-start | bytes 786440 | tf_op jit(solution)/shard_map/ppermute | solution.py:48
  14.3 0.4 %collective-permute-start.6 = (bf16[128,1024]{1,0:T(8,128)(2,1)S(1)}, bf16[128,1024]{1,0:T(8,128)(2,1)S(1)}, u32[]{:S(2)}, u32[]{:S(2)}) collective-permute-start(bf16[128,1024]{1,0:T(8,128)(2,1)S(1)} %collective-permute-done.1.refs_2_.refs_0_.refs_8_), channel_id=1, source_target_pairs={{0,4},{1,3},{2,6},{3,1},{4,0},{5,7},{6,2},{7,5},{8,12},{9,11},{10,... | collective-permute-start | bytes 786440 | tf_op jit(solution)/shard_map/ppermute | solution.py:53
  14.8 0.0 copy-start.3
  14.8 0.7 %copy-done.3 = bf16[8,1024]{1,0:T(8,128)(2,1)S(1)} copy-done((bf16[8,1024]{1,0:T(8,128)(2,1)S(1)}, bf16[8,1024]{1,0:T(8,128)(2,1)}, u32[]{:S(2)}) %copy-start.3) | copy-done | bytes 16408
  15.5 1.1 %collective-permute-start.8 = (bf16[16,1024]{1,0:T(8,128)(2,1)S(1)}, bf16[16,1024]{1,0:T(8,128)(2,1)S(1)}, u32[]{:S(2)}, u32[]{:S(2)}) collective-permute-start(bf16[16,1024]{1,0:T(8,128)(2,1)S(1)} %pack.2.refs_0_), channel_id=1, source_target_pairs={{0,2},{1,5},{2,0},{3,7},{4,6},{5,1},{6,4},{7,3},{8,10},{9,13},{10,... | collective-permute-start | bytes 98312 | tf_op jit(solution)/shard_map/ppermute | solution.py:53
  16.6 0.0 collective-permute-done.5.refs_5_.refs_3_.refs_11_
  16.6 0.0 collective-permute-done.3.refs_3_.refs_1_.refs_9_
  16.6 0.0 copy-done.4
  16.6 1.0 %pick_for_owners.2 = (bf16[4,48,256]{2,1,0:T(8,128)(2,1)S(1)}, bf16[4,48,256]{2,1,0:T(8,128)(2,1)S(1)}) custom-call(s32[2,4]{1,0:T(2,128)S(1)} %copy-done.4, bf16[128,1024]{1,0:T(8,128)(2,1)S(1)} %copy-done.1, bf16[128,1024]{1,0:T(8,128)(2,1)S(1)} %collective-permute-done.mate_ref.refs_1_.refs_7_, ...), custom_call_target="tpu_custom_call" | custom-call | tf_op jit(solution)/shard_map/pick_for_owners/pallas_call | solution.py:410
  17.6 2.3 %collective-permute-done.8.refs_1_ = bf16[16,1024]{1,0:T(8,128)(2,1)S(1)} collective-permute-done((bf16[16,1024]{1,0:T(8,128)(2,1)S(1)}, bf16[16,1024]{1,0:T(8,128)(2,1)S(1)}, u32[]{:S(2)}, u32[]{:S(2)}) %collective-permute-start.8) | collective-permute-done | bytes 32800 | tf_op jit(solution)/shard_map/ppermute | solution.py:53
  19.9 1.2 %collective-permute-start.10 = (bf16[32,1024]{1,0:T(8,128)(2,1)S(1)}, bf16[32,1024]{1,0:T(8,128)(2,1)S(1)}, u32[]{:S(2)}, u32[]{:S(2)}) collective-permute-start(bf16[32,1024]{1,0:T(8,128)(2,1)S(1)} %pack.3.refs_2_), channel_id=1, source_target_pairs={{0,4},{1,3},{2,6},{3,1},{4,0},{5,7},{6,2},{7,5},{8,12},{9,11},{10,... | collective-permute-start | bytes 196616 | tf_op jit(solution)/shard_map/ppermute | solution.py:53
  21.1 0.0 collective-permute-done.6.refs_0_
  21.1 0.0 collective-permute-start.7
  21.1 0.5 %collective-permute-start.9 = (bf16[32,1024]{1,0:T(8,128)(2,1)S(1)}, bf16[32,1024]{1,0:T(8,128)(2,1)S(1)}, u32[]{:S(2)}, u32[]{:S(2)}) collective-permute-start(bf16[32,1024]{1,0:T(8,128)(2,1)S(1)} %pack.3.refs_2_), channel_id=1, source_target_pairs={{0,1},{1,0},{2,3},{3,2},{4,5},{5,4},{6,7},{7,6},{8,9},{9,8},{10,11... | collective-permute-start | bytes 196616 | tf_op jit(solution)/shard_map/ppermute | solution.py:48
  21.6 0.9 %collective-permute-start.12 = (bf16[4,48,256]{2,1,0:T(8,128)(2,1)S(1)}, bf16[4,48,256]{2,1,0:T(8,128)(2,1)S(1)}, u32[]{:S(2)}, u32[]{:S(2)}) collective-permute-start(bf16[4,48,256]{2,1,0:T(8,128)(2,1)S(1)} %get-tuple-element.22), channel_id=1, source_target_pairs={{0,8},{1,9},{2,10},{3,11},{4,12},{5,13},{6,14},{7,15},{8,0},{9,1},... | collective-permute-start | bytes 294920 | tf_op jit(solution)/shard_map/ppermute | solution.py:48
  22.5 0.0 copy-start.2
  22.5 1.7 %collective-permute-done.10.refs_4_ = bf16[32,1024]{1,0:T(8,128)(2,1)S(1)} collective-permute-done((bf16[32,1024]{1,0:T(8,128)(2,1)S(1)}, bf16[32,1024]{1,0:T(8,128)(2,1)S(1)}, u32[]{:S(2)}, u32[]{:S(2)}) %collective-permute-start.10) | collective-permute-done | bytes 65568 | tf_op jit(solution)/shard_map/ppermute | solution.py:53
  24.2 0.0 collective-permute-start.11
  24.2 2.8 %attend_more.1.mass_ref = f32[4096,256]{1,0:T(8,128)S(1)} custom-call(bf16[128,4096]{1,0:T(8,128)(2,1)S(1)} %copy-done, bf16[4096,128]{1,0:T(8,128)(2,1)S(1)} %get-tuple-element.17.shift_ref, f32[4096,256]{1,0:T(8,128)S(1)} %get-tuple-element.23.mass_ref, ...), custom_call_target="tpu_custom_call", output_to_operand_aliasing={{}: (2, {})} | custom-call | flops 2147483648 | bytes 2097152 | tf_op jit(solution)/shard_map/attend_more/pallas_call | solution.py:244
  27.0 0.0 collective-permute-done.7.refs_1_
  27.0 0.8 %pick_for_owners.3 = (bf16[4,16,256]{2,1,0:T(8,128)(2,1)S(1)}, bf16[4,16,256]{2,1,0:T(8,128)(2,1)S(1)}) custom-call(s32[2,4]{1,0:T(2,128)S(1)} %copy-done.4, bf16[128,1024]{1,0:T(8,128)(2,1)S(1)} %collective-permute-done.6.refs_0_, bf16[128,1024]{1,0:T(8,128)(2,1)S(1)} %collective-permute-done.7.refs_1_), custom_call_target="tpu_custom_call" | custom-call | tf_op jit(solution)/shard_map/pick_for_owners/pallas_call | solution.py:410
  27.8 1.3 %collective-permute-start.13 = (bf16[4,16,256]{2,1,0:T(8,128)(2,1)S(1)}, bf16[4,16,256]{2,1,0:T(8,128)(2,1)S(1)}, u32[]{:S(2)}, u32[]{:S(2)}) collective-permute-start(bf16[4,16,256]{2,1,0:T(8,128)(2,1)S(1)} %get-tuple-element.31), channel_id=1, source_target_pairs={{0,8},{1,9},{2,10},{3,11},{4,12},{5,13},{6,14},{7,15},{8,0},{9,1},... | collective-permute-start | bytes 98312 | tf_op jit(solution)/shard_map/ppermute | solution.py:48
  29.1 0.0 collective-permute-done.9.refs_3_
  29.1 0.0 collective-permute-done.11.refs_5_
  29.1 0.0 copy-done.2
  29.1 3.3 %attend_last.1 = bf16[128,4096]{1,0:T(8,128)(2,1)} custom-call(bf16[128,4096]{1,0:T(8,128)(2,1)S(1)} %copy-done, bf16[4096,128]{1,0:T(8,128)(2,1)S(1)} %get-tuple-element.17.shift_ref, f32[4096,256]{1,0:T(8,128)S(1)} %attend_more.1.mass_ref, bf16[128,128]{1,0:T(8,128)(2,1)S(1)} %copy-done.2, bf16[128,1024]{1,0:T(8,128)(2,1)S(1)} %collective-permute-done.6.refs_0_, ...), custom_call_target="tpu_custom_call" | custom-call | flops 1610612736 | bytes 2097152 | tf_op jit(solution)/shard_map/attend_last/pallas_call | solution.py:346
  32.4 0.0 collective-permute-done.12.refs_1_
  32.4 0.2 collective-permute-done.13.refs_3_
  32.6 0.7 %place.1 = bf16[1,4,128,256]{3,2,1,0:T(8,128)(2,1)} custom-call(bf16[4,48,256]{2,1,0:T(8,128)(2,1)S(1)} %get-tuple-element.29.refs_0_, bf16[4,48,256]{2,1,0:T(8,128)(2,1)S(1)} %collective-permute-done.12.refs_1_, bf16[4,16,256]{2,1,0:T(8,128)(2,1)S(1)} %get-tuple-element.30.refs_2_, bf16[4,16,256]{2,1,0:T(8,128)(2,1)S(1)} %collective-permute-done.13.refs_3_), custom_call_target="tpu_custom_call" | custom-call | tf_op jit(solution)/shard_map/place/pallas_call | solution.py:442
  (2 shorter events, 0.0 us)
Async XLA Ops:
  0.6 15.9 %copy-start.4 = (s32[2,4]{1,0:T(2,128)S(1)}, s32[2,4]{1,0:T(2,128)}, u32[]{:S(2)}) copy-start(s32[2,4]{1,0:T(2,128)} %offset_ref.3) | copy-start | bytes 100
  0.6 6.8 %collective-permute-start = (bf16[128,1024]{1,0:T(8,128)(2,1)}, bf16[128,1024]{1,0:T(8,128)(2,1)S(1)}, u32[]{:S(2)}, u32[]{:S(2)}) collective-permute-start(bf16[128,1024]{1,0:T(8,128)(2,1)} %refs_6_.1), channel_id=1, source_target_pairs={{0,1},{1,0},{2,3},{3,2},{4,5},{5,4},{6,7},{7,6},{8,9},{9,8},{10,11... | collective-permute-start | bytes 786440 | tf_op jit(solution)/shard_map/ppermute | solution.py:48
  1.2 12.6 %collective-permute-start.4 = (bf16[128,1024]{1,0:T(8,128)(2,1)}, bf16[128,1024]{1,0:T(8,128)(2,1)S(1)}, u32[]{:S(2)}, u32[]{:S(2)}) collective-permute-start(bf16[128,1024]{1,0:T(8,128)(2,1)} %refs_6_.1), channel_id=1, source_target_pairs={{0,4},{1,3},{2,6},{3,1},{4,0},{5,7},{6,2},{7,5},{8,12},{9,11},{10,... | collective-permute-start | bytes 786440 | tf_op jit(solution)/shard_map/ppermute | solution.py:53
  3.8 10.0 %collective-permute-start.1 = (bf16[128,1024]{1,0:T(8,128)(2,1)}, bf16[128,1024]{1,0:T(8,128)(2,1)S(1)}, u32[]{:S(2)}, u32[]{:S(2)}) collective-permute-start(bf16[128,1024]{1,0:T(8,128)(2,1)} %refs_6_.1), channel_id=1, source_target_pairs={{0,2},{1,5},{2,0},{3,7},{4,6},{5,1},{6,4},{7,3},{8,10},{9,13},{10,... | collective-permute-start | bytes 786440 | tf_op jit(solution)/shard_map/ppermute | solution.py:53
  7.4 6.4 %collective-permute-start.2 = (bf16[8,1024]{1,0:T(8,128)(2,1)}, bf16[8,1024]{1,0:T(8,128)(2,1)S(1)}, u32[]{:S(2)}, u32[]{:S(2)}) collective-permute-start(bf16[8,1024]{1,0:T(8,128)(2,1)} %get-tuple-element.20), channel_id=1, source_target_pairs={{0,8},{1,9},{2,10},{3,11},{4,12},{5,13},{6,14},{7,15},{8,0},{9,1},... | collective-permute-start | bytes 49160 | tf_op jit(solution)/shard_map/ppermute | solution.py:48
  10.1 1.2 %copy-start = (bf16[128,4096]{1,0:T(8,128)(2,1)S(1)}, bf16[128,4096]{1,0:T(8,128)(2,1)}, u32[]{:S(2)}) copy-start(bf16[128,4096]{1,0:T(8,128)(2,1)} %q_ref.5) | copy-start | bytes 3145732
  11.3 0.9 %copy-start.1 = (bf16[128,1024]{1,0:T(8,128)(2,1)S(1)}, bf16[128,1024]{1,0:T(8,128)(2,1)}, u32[]{:S(2)}) copy-start(bf16[128,1024]{1,0:T(8,128)(2,1)} %refs_6_.1) | copy-start | bytes 786436
  13.7 2.8 %collective-permute-start.5 = (bf16[128,1024]{1,0:T(8,128)(2,1)S(1)}, bf16[128,1024]{1,0:T(8,128)(2,1)S(1)}, u32[]{:S(2)}, u32[]{:S(2)}) collective-permute-start(bf16[128,1024]{1,0:T(8,128)(2,1)S(1)} %collective-permute-done.4.refs_4_.refs_2_.refs_10_), channel_id=1, source_target_pairs={{0,1},{1,0},{2,3},{3,2},{4,5},{5,4},{6,7},{7,6},{8,9},{9,8},{10,11... | collective-permute-start | bytes 786440 | tf_op jit(solution)/shard_map/ppermute | solution.py:48
  13.8 2.7 %collective-permute-start.3 = (bf16[128,1024]{1,0:T(8,128)(2,1)S(1)}, bf16[128,1024]{1,0:T(8,128)(2,1)S(1)}, u32[]{:S(2)}, u32[]{:S(2)}) collective-permute-start(bf16[128,1024]{1,0:T(8,128)(2,1)S(1)} %collective-permute-done.1.refs_2_.refs_0_.refs_8_), channel_id=1, source_target_pairs={{0,1},{1,0},{2,3},{3,2},{4,5},{5,4},{6,7},{7,6},{8,9},{9,8},{10,11... | collective-permute-start | bytes 786440 | tf_op jit(solution)/shard_map/ppermute | solution.py:48
  14.3 6.7 %collective-permute-start.6 = (bf16[128,1024]{1,0:T(8,128)(2,1)S(1)}, bf16[128,1024]{1,0:T(8,128)(2,1)S(1)}, u32[]{:S(2)}, u32[]{:S(2)}) collective-permute-start(bf16[128,1024]{1,0:T(8,128)(2,1)S(1)} %collective-permute-done.1.refs_2_.refs_0_.refs_8_), channel_id=1, source_target_pairs={{0,4},{1,3},{2,6},{3,1},{4,0},{5,7},{6,2},{7,5},{8,12},{9,11},{10,... | collective-permute-start | bytes 786440 | tf_op jit(solution)/shard_map/ppermute | solution.py:53
  14.8 0.7 %copy-start.3 = (bf16[8,1024]{1,0:T(8,128)(2,1)S(1)}, bf16[8,1024]{1,0:T(8,128)(2,1)}, u32[]{:S(2)}) copy-start(bf16[8,1024]{1,0:T(8,128)(2,1)} %get-tuple-element.26.refs_0_) | copy-start | bytes 49156
  15.5 4.4 %collective-permute-start.8 = (bf16[16,1024]{1,0:T(8,128)(2,1)S(1)}, bf16[16,1024]{1,0:T(8,128)(2,1)S(1)}, u32[]{:S(2)}, u32[]{:S(2)}) collective-permute-start(bf16[16,1024]{1,0:T(8,128)(2,1)S(1)} %pack.2.refs_0_), channel_id=1, source_target_pairs={{0,2},{1,5},{2,0},{3,7},{4,6},{5,1},{6,4},{7,3},{8,10},{9,13},{10,... | collective-permute-start | bytes 98312 | tf_op jit(solution)/shard_map/ppermute | solution.py:53
  19.9 4.3 %collective-permute-start.10 = (bf16[32,1024]{1,0:T(8,128)(2,1)S(1)}, bf16[32,1024]{1,0:T(8,128)(2,1)S(1)}, u32[]{:S(2)}, u32[]{:S(2)}) collective-permute-start(bf16[32,1024]{1,0:T(8,128)(2,1)S(1)} %pack.3.refs_2_), channel_id=1, source_target_pairs={{0,4},{1,3},{2,6},{3,1},{4,0},{5,7},{6,2},{7,5},{8,12},{9,11},{10,... | collective-permute-start | bytes 196616 | tf_op jit(solution)/shard_map/ppermute | solution.py:53
  21.1 5.9 %collective-permute-start.7 = (bf16[128,1024]{1,0:T(8,128)(2,1)S(1)}, bf16[128,1024]{1,0:T(8,128)(2,1)S(1)}, u32[]{:S(2)}, u32[]{:S(2)}) collective-permute-start(bf16[128,1024]{1,0:T(8,128)(2,1)S(1)} %collective-permute-done.6.refs_0_), channel_id=1, source_target_pairs={{0,1},{1,0},{2,3},{3,2},{4,5},{5,4},{6,7},{7,6},{8,9},{9,8},{10,11... | collective-permute-start | bytes 786440 | tf_op jit(solution)/shard_map/ppermute | solution.py:48
  21.1 8.0 %collective-permute-start.9 = (bf16[32,1024]{1,0:T(8,128)(2,1)S(1)}, bf16[32,1024]{1,0:T(8,128)(2,1)S(1)}, u32[]{:S(2)}, u32[]{:S(2)}) collective-permute-start(bf16[32,1024]{1,0:T(8,128)(2,1)S(1)} %pack.3.refs_2_), channel_id=1, source_target_pairs={{0,1},{1,0},{2,3},{3,2},{4,5},{5,4},{6,7},{7,6},{8,9},{9,8},{10,11... | collective-permute-start | bytes 196616 | tf_op jit(solution)/shard_map/ppermute | solution.py:48
  21.6 10.9 %collective-permute-start.12 = (bf16[4,48,256]{2,1,0:T(8,128)(2,1)S(1)}, bf16[4,48,256]{2,1,0:T(8,128)(2,1)S(1)}, u32[]{:S(2)}, u32[]{:S(2)}) collective-permute-start(bf16[4,48,256]{2,1,0:T(8,128)(2,1)S(1)} %get-tuple-element.22), channel_id=1, source_target_pairs={{0,8},{1,9},{2,10},{3,11},{4,12},{5,13},{6,14},{7,15},{8,0},{9,1},... | collective-permute-start | bytes 294920 | tf_op jit(solution)/shard_map/ppermute | solution.py:48
  22.5 6.6 %copy-start.2 = (bf16[128,128]{1,0:T(8,128)(2,1)S(1)}, bf16[128,128]{1,0:T(8,128)(2,1)}, u32[]{:S(2)}) copy-start(bf16[128,128]{1,0:T(8,128)(2,1)} %get-tuple-element.24.bias_ref) | copy-start | bytes 98308
  24.2 4.9 %collective-permute-start.11 = (bf16[32,1024]{1,0:T(8,128)(2,1)S(1)}, bf16[32,1024]{1,0:T(8,128)(2,1)S(1)}, u32[]{:S(2)}, u32[]{:S(2)}) collective-permute-start(bf16[32,1024]{1,0:T(8,128)(2,1)S(1)} %collective-permute-done.10.refs_4_), channel_id=1, source_target_pairs={{0,1},{1,0},{2,3},{3,2},{4,5},{5,4},{6,7},{7,6},{8,9},{9,8},{10,11... | collective-permute-start | bytes 196616 | tf_op jit(solution)/shard_map/ppermute | solution.py:48
  27.8 4.9 %collective-permute-start.13 = (bf16[4,16,256]{2,1,0:T(8,128)(2,1)S(1)}, bf16[4,16,256]{2,1,0:T(8,128)(2,1)S(1)}, u32[]{:S(2)}, u32[]{:S(2)}) collective-permute-start(bf16[4,16,256]{2,1,0:T(8,128)(2,1)S(1)} %get-tuple-element.31), channel_id=1, source_target_pairs={{0,8},{1,9},{2,10},{3,11},{4,12},{5,13},{6,14},{7,15},{8,0},{9,1},... | collective-permute-start | bytes 98312 | tf_op jit(solution)/shard_map/ppermute | solution.py:48
